TPU v7x, 256 devices: a whole 4x4x8 slice. The times are simulated.
256 devices in a mesh: tile: 64 (over y, z_hi, x, core), batch: 4 (over z_lo).
Axes of the slice: x: 4, y: 4, z: 8 (z_hi: 2, z_lo: 4; z = z_hi * 4 + z_lo), core: 2. Of those that a mesh axis runs over, the one named last changes fastest.
Arguments:
- object_tiles: float32 [64, 2, 384, 384], P('tile'), may hold values from -5 to 5
- probe: bfloat16 [8, 2, 256, 256], replicated, may hold values from -4 to 4
- offsets: int32 [64, 4, 2], P('tile', 'batch'), may hold values from 0 to 383, as said below
- amplitude: float32 [64, 4, 256, 256], P('tile', 'batch'), may hold values from 0.3 to 3
Outputs:
- object_grad: float32 [64, 2, 384, 384], P('tile')
- probe_grad: float32 [8, 2, 256, 256], replicated
Inputs may be any that keep to these rules, and one draw needn't show every extreme that they name: `offsets`: offsets are such that every patch lies inside the region: in tiles of the last tile row the row offset is at most 128, in tiles of the last tile column the column offset likewise.
All inputs are finite; a program needn't handle non-finite values.
Results may differ from a plain program's by a relative error of at most 0.0003.
Values sent between devices are 32-bit elements; how exact they have to be, the bound alone decides.
No kernel may reach another device: no remote copies, remote signals or barrier semaphores. Data moves between devices by JAX's collectives and lax.ppermute only.
A program may use at most 64 MiB of HBM per device.

v0:
```python
import math

import jax
import jax.numpy as jnp
from jax import lax
from jax.sharding import PartitionSpec as P

TILE_COLS = 4


def passed_along(block, axis, distance):
    devices = range(lax.axis_size(axis))
    route = [(i - distance, i) for i in devices if i - distance in devices]
    return lax.ppermute(block, axis, route)


def dft_blocks(pattern):
    counter = jnp.arange(pattern, dtype=jnp.int32)
    phase_index = counter[:, None] * counter[None, :] % pattern
    angles = phase_index.astype(jnp.float32) * (2.0 * math.pi / pattern)
    cosine = jnp.cos(angles) / math.sqrt(pattern)
    sine_table = jnp.sin(angles) / math.sqrt(pattern)
    first_table = jnp.stack(
        [jnp.stack([cosine, sine_table], axis=1), jnp.stack([-sine_table, cosine], axis=1)], axis=0
    )
    second_table = jnp.stack(
        [jnp.stack([cosine, -sine_table], axis=1), jnp.stack([sine_table, cosine], axis=1)], axis=0
    )
    return (first_table, second_table)


def transform(wave, left_table, right_table):
    half_done = jnp.einsum("ajbk,mbkc->majc", left_table, wave, precision=lax.Precision.HIGHEST)
    return jnp.einsum("mbjk,bkac->majc", half_done, right_table, precision=lax.Precision.HIGHEST)


def return_margins(grad_ext, tile_side, pattern):
    lower_part = passed_along(grad_ext[:, tile_side:, :], "tile", TILE_COLS)
    upper_part = grad_ext[:, :tile_side, :].at[:, :pattern, :].add(lower_part)
    right_part = passed_along(upper_part[:, :, tile_side:], "tile", 1)
    return upper_part[:, :, :tile_side].at[:, :, :pattern].add(right_part)


def shards(object_tiles, probe, offsets, amplitude):
    own_tile = object_tiles[0]
    pattern = probe.shape[-1]
    tile_side = own_tile.shape[-1]
    right_strip = passed_along(own_tile[:, :, :pattern], "tile", -1)
    widened = jnp.concatenate([own_tile, right_strip], axis=2)
    lower_strip = passed_along(widened[:, :pattern, :], "tile", -TILE_COLS)
    extended = jnp.concatenate([widened, lower_strip], axis=1)
    first_table, second_table = dft_blocks(pattern)
    probe_wide = probe.astype(jnp.float32)
    probe_re = probe_wide[:, 0]
    probe_im = probe_wide[:, 1]
    grad_ext = jnp.zeros_like(extended)
    zero_index = jnp.int32(0)
    row_at = offsets[0, 0, 0]
    col_at = offsets[0, 0, 1]
    object_patch = lax.dynamic_slice(extended, (zero_index, row_at, col_at), (2, pattern, pattern))
    exit_wave = jnp.stack(
        [
            probe_re * object_patch[0] - probe_im * object_patch[1],
            probe_re * object_patch[1] + probe_im * object_patch[0],
        ],
        axis=1,
    )
    far_field = transform(exit_wave, first_table, second_table)
    intensity = jnp.sum(far_field * far_field, axis=(0, 1))
    factor = 1.0 - amplitude[0, 0] / jnp.sqrt(intensity + 0.01)
    back_wave = transform(far_field * factor, second_table, first_table)
    back_re = back_wave[:, 0]
    back_im = back_wave[:, 1]
    object_term = jnp.stack(
        [
            jnp.sum(probe_re * back_re + probe_im * back_im, axis=0),
            jnp.sum(probe_re * back_im - probe_im * back_re, axis=0),
        ]
    )
    grad_ext = lax.dynamic_update_slice(grad_ext, object_term, (zero_index, row_at, col_at))
    grad_probe = jnp.stack(
        [
            object_patch[0] * back_re + object_patch[1] * back_im,
            object_patch[0] * back_im - object_patch[1] * back_re,
        ],
        axis=1,
    )
    object_grad = lax.psum(return_margins(grad_ext, tile_side, pattern), "batch")
    positions = lax.axis_size("tile") * lax.axis_size("batch") * offsets.shape[1]
    summed = lax.psum(grad_probe, ("tile", "batch"))
    return (object_grad[None], summed / math.sqrt(positions))


def solution(mesh):
    placed = (
        P("tile", None, None, None),
        P(),
        P("tile", "batch", None),
        P("tile", "batch", None, None),
    )
    return jax.shard_map(
        shards,
        mesh=mesh,
        in_specs=placed,
        out_specs=(P("tile", None, None, None), P()),
        check_vma=False,
    )
```

profile of v0, /device:TPU:1, one launch (start us, length us, event | category | flops | bytes accessed | tf_op | source)
XLA Modules:
  0.0 531.8 jit_solution(1394719599924922058)
XLA Ops:
  7.2 0.0 all-reduce.5.cloned.1.call-start
  7.2 1.3 slice.115
  8.5 5.1 collective-permute-start
  13.7 9.0 %collective-permute-done = f32[2,384,256]{2,1,0:T(8,128)S(1)} collective-permute-done((f32[2,384,256]{2,1,0:T(8,128)S(1)}, f32[2,384,256]{2,1,0:T(8,128)S(1)}, u32[]{:S(2)}, u32[]{:S(2)}) %collective-permute-start) | collective-permute-done | bytes 786464 | tf_op jit(solution)/shard_map/ppermute | solution.py:14
  22.7 0.9 copy-done.4
  23.6 1.2 pad_maximum_fusion.1
  24.7 1.3 collective-permute-start.1
  26.0 0.6 fusion.36
  29.1 2.9 copy.13
  32.0 2.5 convert_element_type.35
  34.5 1.1 copy.17
  36.8 1.0 fusion.34
  37.8 1.1 sine_multiply_fusion
  38.9 0.2 fusion.23
  39.1 18.6 %collective-permute-done.1 = f32[2,256,640]{2,1,0:T(8,128)} collective-permute-done((f32[2,256,640]{2,1,0:T(8,128)}, f32[2,256,640]{2,1,0:T(8,128)}, u32[]{:S(2)}, u32[]{:S(2)}) %collective-permute-start.1) | collective-permute-done | bytes 1310752 | tf_op jit(solution)/shard_map/ppermute | solution.py:14
  57.6 1.6 fusion.25
  59.3 0.1 copy.15
  59.5 0.1 copy.16
  59.6 2.8 multiply_subtract_fusion.1
  62.4 6.9 %fusion.8 = f32[8,256,2,256,1]{1,3,4,2,0:T(8,128)S(1)} fusion(f32[1,256,2,256]{1,3,2,0:T(8,128)S(1)} %get-tuple-element.39, f32[1,256,2,256]{1,3,2,0:T(8,128)S(1)} %get-tuple-element.44, f32[8,1,256,256]{2,3,0,1:T(8,128)S(1)} %get-tuple-element.35, f32[8,1,256,256]{2,3,0,1:T(8,128)S(1)} %get-tuple-element.34), kind=kOutput, calls=%fused_computation.12 | convolution fusion | flops 6443761664 | bytes 9437184 | tf_op jit(solution)/shard_map/ajbk,mbkc->majc/dot_general | solution.py:33
  69.3 7.6 %fusion.4 = (f32[256,256]{0,1:T(8,128)S(1)}, f32[2,256,8,256,1]{3,1,4,2,0:T(8,128)S(1)}) fusion(f32[8,256,2,256,1]{1,3,4,2,0:T(8,128)S(1)} %fusion.8, f32[1,256,2,256]{1,3,0,2:T(8,128)S(1)} %get-tuple-element.45, f32[1,256,2,256]{1,3,0,2:T(8,128)S(1)} %get-tuple-element.38), kind=kOutput, calls=%fused_computation.8 | convolution fusion | flops 6444744704 | bytes 9699328 | tf_op jit(solution)/shard_map/mbjk,bkac->majc/dot_general | solution.py:34
  76.9 17.1 %fusion.6 = f32[8,256,2,256,1]{1,3,4,2,0:T(8,128)S(1)} fusion(f32[2,256,8,256,1]{3,1,4,2,0:T(8,128)S(1)} %get-tuple-element.49, f32[256,256]{0,1:T(8,128)S(1)} %fusion.30, f32[1,256,2,256]{1,3,0,2:T(8,128)S(1)} %get-tuple-element.45, f32[1,256,2,256]{1,3,0,2:T(8,128)S(1)} %get-tuple-element.38), kind=kOutput, calls=%fused_computation.10 | convolution fusion | flops 6443761664 | bytes 9699328 | tf_op jit(solution)/shard_map/ajbk,mbkc->majc/dot_general | solution.py:33
  94.1 0.0 copy-start
  94.1 7.2 %fusion.10 = f32[8,2,256,256]{2,3,0,1:T(8,128)S(1)} fusion(f32[8,256,2,256,1]{1,3,4,2,0:T(8,128)S(1)} %fusion.6, f32[1,256,2,256]{1,3,2,0:T(8,128)S(1)} %get-tuple-element.39, f32[1,256,2,256]{1,3,2,0:T(8,128)S(1)} %get-tuple-element.44), kind=kOutput, calls=%fused_computation.17 | convolution fusion | flops 6442713088 | bytes 9437184 | tf_op jit(solution)/shard_map/mbjk,bkac->majc/dot_general | solution.py:34
  101.3 3.1 multiply_add_fusion
  104.4 1.0 copy.19
  105.4 0.2 broadcast_in_dim.4
  105.6 7.4 %dynamic_update_slice.3 = f32[2,640,640]{2,1,0:T(8,128)S(1)} dynamic-update-slice(f32[2,640,640]{2,1,0:T(8,128)S(1)} %broadcast_in_dim.4, f32[2,256,256]{2,1,0:T(8,128)} %copy.19, s32[]{:T(128)} %constant.76.clone.1, s32[]{:T(128)S(6)} %select_n.45, s32[]{:T(128)S(6)} %select_n.46) | dynamic-update-slice | bytes 1048580 | tf_op jit(solution)/shard_map/dynamic_update_slice | solution.py:80
  113.0 1.2 slice.123
  114.2 12.7 %collective-permute-start.2 = (f32[2,256,640]{2,1,0:T(8,128)}, f32[2,256,640]{2,1,0:T(8,128)}, u32[]{:S(2)}, u32[]{:S(2)}) collective-permute-start(f32[2,256,640]{2,1,0:T(8,128)} %slice.123), channel_id=1, source_target_pairs={{0,16},{4,20},{8,24},{12,28},{16,32},{20,36},{24,40},{28,44},{32,4... | collective-permute-start | bytes 3932168 | tf_op jit(solution)/shard_map/ppermute | solution.py:14
  126.9 4.0 pad_maximum_fusion
  130.9 0.0 all-reduce.5.cloned.1.call-update
  131.0 0.0 all-reduce.3.cloned.1.call-start
  131.0 0.1 slice.121
  131.1 22.9 %collective-permute-done.2 = f32[2,256,640]{2,1,0:T(8,128)} collective-permute-done((f32[2,256,640]{2,1,0:T(8,128)}, f32[2,256,640]{2,1,0:T(8,128)}, u32[]{:S(2)}, u32[]{:S(2)}) %collective-permute-start.2) | collective-permute-done | bytes 1310752 | tf_op jit(solution)/shard_map/ppermute | solution.py:14
  154.1 1.4 fusion.13
  155.5 0.1 slice.126
  155.6 1.9 collective-permute-start.3
  157.5 0.1 slice_bitcast_fusion
  157.6 8.8 %collective-permute-done.3 = f32[2,384,256]{2,1,0:T(8,128)S(1)} collective-permute-done((f32[2,384,256]{2,1,0:T(8,128)S(1)}, f32[2,384,256]{2,1,0:T(8,128)S(1)}, u32[]{:S(2)}, u32[]{:S(2)}) %collective-permute-start.3) | collective-permute-done | bytes 786464 | tf_op jit(solution)/shard_map/ppermute | solution.py:14
  166.4 0.1 fusion.19
  166.6 1.0 copy-done.3
  167.6 0.0 all-reduce.3.cloned.1.call-update
  167.6 283.2 %all-reduce.5.cloned.1.call-done = f32[8,2,256,256]{2,3,0,1:T(8,128)} async-done(((f32[8,2,256,256]{2,3,0,1:T(8,128)}), f32[8,2,256,256]{2,3,0,1:T(8,128)}) %all-reduce.5.cloned.1.call-update) | async-done | bytes 4194320 | tf_op jit(solution)/shard_map/psum | solution.py:90
  450.8 4.5 broadcast_multiply_fusion
  455.3 5.3 %copy.20 = f32[8,2,256,256]{3,2,1,0:T(8,128)} copy(f32[8,2,256,256]{2,3,0,1:T(8,128)} %broadcast_multiply_fusion) | data formatting | bytes 8388608
  460.6 61.9 %all-reduce.3.cloned.1.call-done = f32[1,2,384,384]{3,2,1,0:T(8,128)} async-done(((f32[1,2,384,384]{3,2,1,0:T(8,128)}), f32[1,2,384,384]{3,2,1,0:T(8,128)}) %all-reduce.3.cloned.1.call-update) | async-done | bytes 1179664 | tf_op jit(solution)/shard_map/psum | solution.py:88
  522.5 2.4 copy.45
  (12 shorter events, 0.1 us)
Async XLA Ops:
  7.2 16.4 %copy-start.1 = (f32[1,2,384,384]{3,2,1,0:T(8,128)S(1)}, f32[1,2,384,384]{3,2,1,0:T(8,128)}, u32[]{:S(2)}) copy-start(f32[1,2,384,384]{3,2,1,0:T(8,128)} %param.8) | copy-start | bytes 3538948
  7.2 443.6 %all-reduce.5.cloned.1.call-start = ((), (), s32[]{:S(2)}) async-start(), calls=%async_computation.1 | async-start | bytes 8388608 | tf_op jit(solution)/shard_map/psum | solution.py:90
  7.2 18.8 %copy-start.5 = (s32[1,1,2]{2,1,0:T(1,128)S(1)}, s32[1,1,2]{2,1,0:T(1,128)}, u32[]{:S(2)}) copy-start(s32[1,1,2]{2,1,0:T(1,128)} %param.10) | copy-start | bytes 28
  8.5 14.2 %collective-permute-start = (f32[2,384,256]{2,1,0:T(8,128)S(1)}, f32[2,384,256]{2,1,0:T(8,128)S(1)}, u32[]{:S(2)}, u32[]{:S(2)}) collective-permute-start(f32[2,384,256]{2,1,0:T(8,128)S(1)} %slice.115), channel_id=1, source_target_pairs={{4,0},{8,4},{12,8},{16,12},{20,16},{24,20},{28,24},{32,28},{36,32}... | collective-permute-start | bytes 2359304 | tf_op jit(solution)/shard_map/ppermute | solution.py:14
  22.7 0.9 copy-start.4
  24.7 32.9 %collective-permute-start.1 = (f32[2,256,640]{2,1,0:T(8,128)}, f32[2,256,640]{2,1,0:T(8,128)}, u32[]{:S(2)}, u32[]{:S(2)}) collective-permute-start(f32[2,256,640]{2,1,0:T(8,128)} %pad_maximum_fusion.1), channel_id=1, source_target_pairs={{16,0},{20,4},{24,8},{28,12},{32,16},{36,20},{40,24},{44,28},{48,3... | collective-permute-start | bytes 3932168 | tf_op jit(solution)/shard_map/ppermute | solution.py:14
  94.1 7.2 %copy-start = (f32[8,2,256,256]{2,3,0,1:T(8,128)S(1)}, f32[8,2,256,256]{2,3,0,1:T(8,128)}, u32[]{:S(2)}) copy-start(f32[8,2,256,256]{2,3,0,1:T(8,128)} %convert_element_type.35) | copy-start | bytes 12582916
  113.0 13.9 %copy-start.2 = (f32[8,1,256,256]{2,3,0,1:T(8,128)S(1)}, f32[8,1,256,256]{2,3,0,1:T(8,128)}, u32[]{:S(2)}) copy-start(f32[8,1,256,256]{2,3,0,1:T(8,128)} %get-tuple-element.32) | copy-start | bytes 6291460
  114.2 39.9 %collective-permute-start.2 = (f32[2,256,640]{2,1,0:T(8,128)}, f32[2,256,640]{2,1,0:T(8,128)}, u32[]{:S(2)}, u32[]{:S(2)}) collective-permute-start(f32[2,256,640]{2,1,0:T(8,128)} %slice.123), channel_id=1, source_target_pairs={{0,16},{4,20},{8,24},{12,28},{16,32},{20,36},{24,40},{28,44},{32,4... | collective-permute-start | bytes 3932168 | tf_op jit(solution)/shard_map/ppermute | solution.py:14
  131.0 391.5 %all-reduce.3.cloned.1.call-start = ((), (), s32[]{:S(2)}) async-start(), calls=%async_computation | async-start | bytes 2359296 | tf_op jit(solution)/shard_map/psum | solution.py:88
  155.6 10.8 %collective-permute-start.3 = (f32[2,384,256]{2,1,0:T(8,128)S(1)}, f32[2,384,256]{2,1,0:T(8,128)S(1)}, u32[]{:S(2)}, u32[]{:S(2)}) collective-permute-start(f32[2,384,256]{2,1,0:T(8,128)S(1)} %slice.126), channel_id=1, source_target_pairs={{0,4},{4,8},{8,12},{12,16},{16,20},{20,24},{24,28},{28,32},{32,36}... | collective-permute-start | bytes 2359304 | tf_op jit(solution)/shard_map/ppermute | solution.py:14
  166.5 1.0 copy-start.3
Sparse Core Ops, SparseCore 0:
  131.1 319.6 all-reduce.4
  454.2 68.2 all-reduce.2
where the time goes:
time: 537 us; the launch traced here: 532 us
  waiting for transfers between devices  404 us (75%)
  matrix products  38.8 us (7%)
  local copies, waits for them, and re-layouts  25.7 us (5%)
  other arithmetic  23.5 us (4%)
  starting transfers between devices  21.1 us (4%)
  between operations  18.3 us (3%)
    psum x1, waiting for transfers between devices, shards(): summed = lax.psum(grad_probe, ('tile', 'batch'))  283 us
    psum x1, waiting for transfers between devices, shards(): lax.psum(return_margins(grad_ext, tile_side, pattern), 'batch')  61.9 us
    ppermute x4, waiting for transfers between devices, passed_along(): return lax.ppermute(block, axis, route)  59.4 us
    dot_general x2, matrix products, transform(): jnp.einsum('ajbk,mbkc->majc', left_table, wave, precision=lax.Precision.H...  24.1 us
    ppermute x4, starting transfers between devices, passed_along(): return lax.ppermute(block, axis, route)  21.1 us
    dot_general x2, matrix products, transform(): jnp.einsum('mbjk,bkac->majc', half_done, right_table, precision=lax.Preci...  14.7 us
    unnamed x16, local copies, waits for them, and re-layouts  13.5 us
  transfers between devices with their start and end apart: 6, of which 6 were waited for; matrix products, arithmetic and copies ran while one was open for 5% of the time, Pallas kernels for 0%

commit v1 on v0

v1 whole, which is shorter than its diff:
```python
import math

import jax
import jax.numpy as jnp
import ml_dtypes
import numpy as np
from jax import lax
from jax.experimental import pallas as pl
from jax.experimental.pallas import tpu as pltpu
from jax.sharding import Mesh, PartitionSpec as P

GROUPS = 4
ROW_BLOCK = 8
BF16 = jnp.bfloat16
F32 = jnp.float32
VMEM_LIMIT = 48 * 1024 * 1024


def split_table(table):
    high = table.astype(ml_dtypes.bfloat16)
    low = (table - high.astype(np.float64)).astype(ml_dtypes.bfloat16)
    return high, low


def dft_tables(pattern):
    half = pattern // 2
    angles = 2.0 * np.pi / half * (np.outer(np.arange(half), np.arange(half)) % half)
    cosine, sine = np.cos(angles) / math.sqrt(pattern), np.sin(angles) / math.sqrt(pattern)
    table = np.block([[cosine, -sine], [sine, cosine]])
    high, low = split_table(table)
    down = np.concatenate([high, high, low], axis=0)
    across = np.concatenate([high, high, low], axis=1)
    turned = [np.ascontiguousarray(part.T) for part in (high, low)]
    down_t = np.concatenate([turned[0], turned[0], turned[1]], axis=0)
    across_t = np.concatenate([turned[0], turned[0], turned[1]], axis=1)
    twist = 2.0 * np.pi / pattern * np.arange(half)
    lanes = np.stack([np.cos(twist), -np.sin(twist)])[:, None, :].astype(np.float32)
    rows = np.ascontiguousarray(
        np.broadcast_to(np.stack([np.cos(twist), -np.sin(twist)])[:, :, None], (2, half, half))
    ).astype(np.float32)
    return down, across, down_t, across_t, lanes, rows


def parts(x):
    high = x.astype(BF16)
    return high, (x - high.astype(F32)).astype(BF16)


def times(x, table):
    high, low = parts(x)
    return jnp.dot(jnp.concatenate([high, low, high], axis=1), table, preferred_element_type=F32)


def under(table, x):
    high, low = parts(x)
    return jnp.dot(table, jnp.concatenate([high, low, high], axis=0), preferred_element_type=F32)


def forward(re, im, down, across_t, lanes, rows):
    h = re.shape[0] // 2
    wr, wi = lanes
    a, b, c, d = re[:, :h], re[:, h:], im[:, :h], im[:, h:]
    p, q = a - b, c - d
    even = times(jnp.concatenate([a + b, c + d], axis=1), down)
    odd = times(jnp.concatenate([p * wr - q * wi, p * wi + q * wr], axis=1), down)
    re = jnp.concatenate([even[:, :h], odd[:, :h]], axis=1)
    im = jnp.concatenate([even[:, h:], odd[:, h:]], axis=1)
    wr, wi = rows
    a, b, c, d = re[:h], re[h:], im[:h], im[h:]
    p, q = a - b, c - d
    even = under(across_t, jnp.concatenate([a + b, c + d], axis=0))
    odd = under(across_t, jnp.concatenate([p * wr - q * wi, p * wi + q * wr], axis=0))
    return jnp.concatenate([even[:h], odd[:h]], axis=0), jnp.concatenate([even[h:], odd[h:]], axis=0)


def backward(re, im, down_t, across, lanes, rows):
    h = re.shape[0] // 2
    wr, wi = rows
    even = under(across, jnp.concatenate([re[:h], im[:h]], axis=0))
    odd = under(across, jnp.concatenate([re[h:], im[h:]], axis=0))
    p, q = odd[:h], odd[h:]
    p, q = p * wr + q * wi, q * wr - p * wi
    re = jnp.concatenate([even[:h] + p, even[:h] - p], axis=0)
    im = jnp.concatenate([even[h:] + q, even[h:] - q], axis=0)
    wr, wi = lanes
    even = times(jnp.concatenate([re[:, :h], im[:, :h]], axis=1), down_t)
    odd = times(jnp.concatenate([re[:, h:], im[:, h:]], axis=1), down_t)
    p, q = odd[:, :h], odd[:, h:]
    p, q = p * wr + q * wi, q * wr - p * wi
    re = jnp.concatenate([even[:, :h] + p, even[:, :h] - p], axis=1)
    im = jnp.concatenate([even[:, h:] + q, even[:, h:] - q], axis=1)
    return re, im


def twiddles(lanes_ref, rows_ref):
    rows = [jnp.concatenate([rows_ref[i], rows_ref[i]], axis=1) for i in range(2)]
    return (lanes_ref[0], lanes_ref[1]), rows


def gradients(re, im, m, i, patch_ref, probe_ref, term, grad_ref, tables):
    re, im = backward(re, im, *tables)
    grad_ref[i, 0] = patch_ref[0] * re + patch_ref[1] * im
    grad_ref[i, 1] = patch_ref[0] * im - patch_ref[1] * re
    probe_re, probe_im = probe_ref[m, 0].astype(F32), probe_ref[m, 1].astype(F32)
    term[0] += probe_re * re + probe_im * im
    term[1] += probe_re * im - probe_im * re


def first_kernel(
    where_ref, rows0, rows1, rows2, rows3, probe_ref, amplitude_ref, down, across, down_t, across_t, lanes_ref, rows_ref,
    sent_ref, corrected_ref, patch_ref, term_ref, frame, far, total,
):
    pattern = amplitude_ref.shape[0]
    modes = probe_ref.shape[0]
    half = modes // 2
    row_at, core, other_turn = where_ref[0], where_ref[1], where_ref[4]
    turn = where_ref[3]
    block, shift = row_at // ROW_BLOCK, row_at % ROW_BLOCK
    count = frame.shape[1]
    for d, rows in enumerate((rows0, rows1, rows2, rows3)):
        first = ((where_ref[2] ^ d) + GROUPS - block % GROUPS) % GROUPS
        for i in range(count // GROUPS):
            frame[:, first + GROUPS * i] = rows[:, i]
    height = pattern + ROW_BLOCK
    for channel in range(2):
        window = frame[channel, : count - 3].reshape(height, pattern)
        patch_ref[channel] = pltpu.roll(window, (height - shift) % height, 0)[:pattern]
    lanes, rows = twiddles(lanes_ref, rows_ref)
    total[...] = jnp.full_like(total, 0.01)

    def outward(m, carry):
        probe_re, probe_im = probe_ref[m, 0].astype(F32), probe_ref[m, 1].astype(F32)
        re = probe_re * patch_ref[0] - probe_im * patch_ref[1]
        im = probe_re * patch_ref[1] + probe_im * patch_ref[0]
        re, im = forward(re, im, down[...], across_t[...], lanes, rows)
        far[m, 0] = re
        far[m, 1] = im
        total[...] += re * re + im * im
        return carry

    lax.fori_loop(0, modes, outward, 0, unroll=UNROLL)
    total[...] = 1.0 - amplitude_ref[...] * lax.rsqrt(total[...])
    term_ref[...] = jnp.zeros_like(term_ref)
    tables = (down_t[...], across[...], lanes, rows)

    def homeward(i, carry):
        m = (1 - core) * half + (other_turn ^ i)
        kept = core * half + (turn ^ i)
        corrected_ref[i, 0] = far[kept, 0] * total[...]
        corrected_ref[i, 1] = far[kept, 1] * total[...]
        gradients(far[m, 0] * total[...], far[m, 1] * total[...], m, i, patch_ref, probe_ref, term_ref, sent_ref, tables)
        return carry

    lax.fori_loop(0, half, homeward, 0, unroll=UNROLL)


def second_kernel(
    where_ref, corrected_ref, patch_ref, term_ref, probe_ref, across, down_t, lanes_ref, rows_ref,
    kept_ref, rows0, rows1, rows2, rows3, term, frame,
):
    pattern = patch_ref.shape[1]
    half = corrected_ref.shape[0]
    row_at, core, row_class, turn = where_ref[0], where_ref[1], where_ref[2], where_ref[3]
    lanes, rows = twiddles(lanes_ref, rows_ref)
    tables = (down_t[...], across[...], lanes, rows)
    term[...] = term_ref[...]

    def homeward(i, carry):
        gradients(
            corrected_ref[i, 0],
            corrected_ref[i, 1],
            core * half + (turn ^ i),
            i,
            patch_ref,
            probe_ref,
            term,
            kept_ref,
            tables,
        )
        return carry

    lax.fori_loop(0, half, homeward, 0, unroll=UNROLL)
    block = row_at // ROW_BLOCK
    shift = row_at % ROW_BLOCK
    count = frame.shape[1]
    for channel in range(2):
        padded = jnp.concatenate([term[channel], jnp.zeros((ROW_BLOCK, pattern), F32)], axis=0)
        frame[channel, : count - 3] = pltpu.roll(padded, shift, 0).reshape(count - 3, ROW_BLOCK, pattern)
        frame[channel, count - 3 :] = jnp.zeros((3, ROW_BLOCK, pattern), F32)
    for d, out in enumerate((rows0, rows1, rows2, rows3)):
        first = ((row_class ^ d) + GROUPS - block % GROUPS) % GROUPS
        for i in range(count // GROUPS):
            out[:, i] = frame[:, first + GROUPS * i]


def whole(space=pltpu.VMEM):
    return pl.BlockSpec(memory_space=space)


UNROLL = 2


def first_call(where, pieces, probe, amplitude, tables):
    modes, _, pattern, _ = probe.shape
    half = (modes // 2, 2, pattern, pattern)
    shapes = [half, half, (2, pattern, pattern), (2, pattern, pattern)]
    return pl.pallas_call(
        first_kernel,
        out_shape=[jax.ShapeDtypeStruct(s, F32) for s in shapes],
        in_specs=[whole(pltpu.SMEM)] + [whole()] * 12,
        out_specs=[whole()] * 4,
        scratch_shapes=[
            pltpu.VMEM((2, pattern // ROW_BLOCK + GROUPS, ROW_BLOCK, pattern), F32),
            pltpu.VMEM((modes, 2, pattern, pattern), F32),
            pltpu.VMEM((pattern, pattern), F32),
        ],
        compiler_params=pltpu.CompilerParams(vmem_limit_bytes=VMEM_LIMIT),
        name="outward",
    )(where, *pieces, probe, amplitude, *tables)


def second_call(where, corrected, patch, term, probe, tables):
    down, across, down_t, across_t, lanes, rows = tables
    pattern = patch.shape[1]
    blocks = pattern // ROW_BLOCK + GROUPS
    piece = (2, blocks // GROUPS, ROW_BLOCK, pattern)
    shapes = [corrected.shape] + [piece] * GROUPS
    return pl.pallas_call(
        second_kernel,
        out_shape=[jax.ShapeDtypeStruct(s, F32) for s in shapes],
        in_specs=[whole(pltpu.SMEM)] + [whole()] * 8,
        out_specs=[whole()] * 5,
        scratch_shapes=[
            pltpu.VMEM((2, pattern, pattern), F32),
            pltpu.VMEM((2, blocks, ROW_BLOCK, pattern), F32),
        ],
        compiler_params=pltpu.CompilerParams(vmem_limit_bytes=VMEM_LIMIT),
        name="homeward",
    )(where, corrected, patch, term, probe, across, down_t, lanes, rows)


def class_start(spot, row_class):
    block = spot[0] // ROW_BLOCK
    start = (block + (row_class + GROUPS - block % GROUPS) % GROUPS) // GROUPS
    return pl.multiple_of(start * ROW_BLOCK, ROW_BLOCK)


def cut_kernel(
    class_ref, spot0, spot1, spot2, spot3, tile_ref, right_ref, low_ref, corner_ref, rows0, rows1, rows2, rows3, owned
):
    row_class = class_ref[0]
    _, blocks, _, _, side = tile_ref.shape
    inside = blocks * ROW_BLOCK
    _, outside, _ = low_ref.shape
    for i in range(blocks):
        owned[:, ROW_BLOCK * i : ROW_BLOCK * (i + 1), :side] = tile_ref[:, i, row_class]
    owned[:, :inside, side:] = right_ref[...]
    owned[:, inside : inside + outside, :side] = low_ref[...]
    owned[:, inside : inside + outside, side:] = corner_ref[...]
    owned[:, inside + outside :] = jnp.zeros((2, ROW_BLOCK, owned.shape[2]), F32)
    for spot, rows in ((spot0, rows0), (spot1, rows1), (spot2, rows2), (spot3, rows3)):
        _, count, _, width = rows.shape
        col_at = spot[1]
        down = pl.ds(class_start(spot, row_class), count * ROW_BLOCK)
        across = pl.ds(pl.multiple_of(col_at // 128 * 128, 128), width + 128)
        for channel in range(2):
            wide = pltpu.roll(owned[channel, down, across], (width + 128 - col_at % 128) % (width + 128), 1)
            rows[channel] = wide[:, :width].reshape(count, ROW_BLOCK, width)


def cut_call(row_class, spots, tile, right, low, corner):
    _, blocks, _, _, side = tile.shape
    width = right.shape[2]
    piece = (2, (width // ROW_BLOCK + GROUPS) // GROUPS, ROW_BLOCK, width)
    return pl.pallas_call(
        cut_kernel,
        out_shape=[jax.ShapeDtypeStruct(piece, F32)] * GROUPS,
        in_specs=[whole(pltpu.SMEM)] * 5 + [whole()] * 4,
        out_specs=[whole()] * GROUPS,
        scratch_shapes=[pltpu.VMEM((2, (side + width) // GROUPS + ROW_BLOCK, side + width), F32)],
        compiler_params=pltpu.CompilerParams(vmem_limit_bytes=VMEM_LIMIT),
        name="cut",
    )(row_class, *spots, tile, right, low, corner)


def place_kernel(class_ref, spot0, spot1, spot2, spot3, rows0, rows1, rows2, rows3, body_ref, margin_ref, owned):
    row_class = class_ref[0]
    owned[...] = jnp.zeros_like(owned)
    for spot, rows in ((spot0, rows0), (spot1, rows1), (spot2, rows2), (spot3, rows3)):
        _, count, _, width = rows.shape
        col_at = spot[1]
        down = pl.ds(class_start(spot, row_class), count * ROW_BLOCK)
        across = pl.ds(pl.multiple_of(col_at // 128 * 128, 128), width + 128)
        for channel in range(2):
            block_rows = rows[channel].reshape(count * ROW_BLOCK, width)
            wide = jnp.concatenate([block_rows, jnp.zeros((count * ROW_BLOCK, 128), F32)], axis=1)
            owned[channel, down, across] += pltpu.roll(wide, col_at % 128, 1)
    height, side = body_ref.shape[1:]
    body_ref[...] = owned[:, :height, :side]
    margin_ref[...] = owned[:, :height, side:]


def place_call(row_class, spots, pieces, side):
    _, count, _, width = pieces[0].shape
    height = (side + width) // GROUPS
    return pl.pallas_call(
        place_kernel,
        out_shape=[jax.ShapeDtypeStruct((2, height, w), F32) for w in (side, width)],
        in_specs=[whole(pltpu.SMEM)] * 5 + [whole()] * 4,
        out_specs=[whole()] * 2,
        scratch_shapes=[pltpu.VMEM((2, height + ROW_BLOCK, side + width), F32)],
        compiler_params=pltpu.CompilerParams(vmem_limit_bytes=VMEM_LIMIT),
        name="place",
    )(row_class, *spots, *pieces)


def join_kernel(class_ref, rows0, rows1, rows2, rows3, out_ref):
    for d, rows in enumerate((rows0, rows1, rows2, rows3)):
        place = class_ref[0] ^ d
        for i in range(out_ref.shape[1]):
            out_ref[:, i, place] = rows[:, ROW_BLOCK * i : ROW_BLOCK * (i + 1)]


def join_call(row_class, pieces):
    _, height, side = pieces[0].shape
    out = pl.pallas_call(
        join_kernel,
        out_shape=jax.ShapeDtypeStruct((2, height // ROW_BLOCK, GROUPS, ROW_BLOCK, side), F32),
        in_specs=[whole(pltpu.SMEM)] + [whole()] * 4,
        out_specs=whole(),
        compiler_params=pltpu.CompilerParams(vmem_limit_bytes=VMEM_LIMIT),
        name="join",
    )(row_class, *pieces)
    return out.reshape(1, 2, height * GROUPS, side)


def fill_kernel(where_ref, *refs):
    count = (len(refs) - 2) // 2
    pieces, out_ref, sems = refs[: 2 * count], refs[-2], refs[-1]
    core, turns = where_ref[1], (where_ref[3], where_ref[4])
    copies = []
    for n, piece in enumerate(pieces):
        side, d = n // count, n % count
        slot = count * (core ^ side) + (turns[side] ^ d)
        copies.append(pltpu.make_async_copy(piece, out_ref.at[slot], sems.at[n]))
    for copy in copies:
        copy.start()
    for copy in copies:
        copy.wait()


def fill_call(where, pieces, shape):
    pieces = [piece.reshape(shape[1:]) for piece in pieces]
    return pl.pallas_call(
        fill_kernel,
        out_shape=jax.ShapeDtypeStruct(shape, F32),
        in_specs=[whole(pltpu.SMEM)] + [whole()] * len(pieces),
        out_specs=whole(pl.ANY),
        scratch_shapes=[pltpu.SemaphoreType.DMA((len(pieces),))],
        compiler_params=pltpu.CompilerParams(vmem_limit_bytes=VMEM_LIMIT),
        name="fill",
    )(where, *pieces)


TILE_COLS = 4
AXES = ("y", "zh", "x", "core", "zl")
SIZES = (4, 2, 4, 2, 4)
TILE_AXES = AXES[:4]


def mirrored(tile, group):
    z_hi = tile // 8 % 2
    return group if z_hi == 0 else GROUPS - 1 - group


def across_columns(block, step):
    route = [(t, t + step) for t in range(64) if 0 <= t % TILE_COLS + step < TILE_COLS]
    return lax.ppermute(block, TILE_AXES, route)


def across_rows(block, step):
    route = []
    for t in range(64):
        u = t + step * TILE_COLS
        if 0 <= u < 64:
            for k in range(GROUPS):
                route.append((t * GROUPS + mirrored(t, k), u * GROUPS + mirrored(u, k)))
    return lax.ppermute(block, AXES, route)


def among(block, axis, distance):
    n = lax.axis_size(axis)
    return lax.ppermute(block, axis, [(i, i ^ distance) for i in range(n)])


def exchange(block, distance, stage):
    route = []
    for y, zh, x, core, zl in np.ndindex(*SIZES):
        to = (y, zh, x ^ distance, core, zl) if core == stage else (y ^ distance, zh, x, core, zl)
        route.append((int(np.ravel_multi_index((y, zh, x, core, zl), SIZES)), int(np.ravel_multi_index(to, SIZES))))
    return lax.ppermute(block, AXES, route)


def exchanged(pieces, stage):
    return [exchange(pieces[d], d, stage) for d in (1, 2, 3)]


def tied(*groups):
    return lax.optimization_barrier(tuple(groups))


def by_place(pieces, me):
    one, two = me % 2 == 1, me // 2 == 1
    pairs = [(jnp.where(one, b, a), jnp.where(one, a, b)) for a, b in (pieces[:2], pieces[2:])]
    low = [jnp.where(two, q, p) for p, q in zip(*pairs)]
    high = [jnp.where(two, p, q) for p, q in zip(*pairs)]
    return jnp.concatenate(low + high)


def total_of(pieces):
    return (pieces[0] + pieces[1]) + (pieces[2] + pieces[3])


def by_parity(amplitude):
    pattern = amplitude.shape[0]
    order = np.concatenate([np.arange(0, pattern, 2), np.arange(1, pattern, 2)])
    table = jnp.asarray(np.eye(pattern, dtype=np.float32)[order])
    exact = lax.Precision.HIGHEST
    return jnp.dot(jnp.dot(table, amplitude, precision=exact), table.T, precision=exact)


def shards(object_tiles, probe, offsets, amplitude):
    own_tile = object_tiles[0]
    pattern = probe.shape[-1]
    tile_side = own_tile.shape[-1]
    place = offsets[0, 0]
    x, y, core, z_hi, z_lo = (lax.axis_index(axis) for axis in ("x", "y", "core", "zh", "zl"))
    row_class = jnp.where(z_hi == 0, z_lo, GROUPS - 1 - z_lo)
    turn, next_turn = jnp.where(core == 0, x, y), jnp.where(core == 0, y, x)
    where = jnp.stack([place[0], core, row_class, turn, next_turn]).astype(jnp.int32)
    own_class = where[2:3]
    tables = [jnp.asarray(table) for table in dft_tables(pattern)]

    blocks = own_tile.reshape(2, -1, GROUPS, ROW_BLOCK, tile_side)
    class_rows = lax.dynamic_index_in_dim(blocks, row_class, 2, keepdims=False).reshape(2, -1, tile_side)
    low = across_rows(class_rows[:, : pattern // GROUPS], -1)
    right = across_columns(class_rows[:, :, :pattern], -1)
    right, place_later = tied(right, place)
    spots = [place] + [among(place_later, "zl", d) for d in (1, 2, 3)]
    target = by_parity(amplitude[0, 0])
    low, spots, target = tied(low, spots, target)
    corner = across_columns(low[:, :, :pattern], -1)
    rows = list(cut_call(own_class, spots, blocks, right, low, corner))
    rows = rows[:1] + [among(rows[d], "zl", d) for d in (1, 2, 3)]

    sent, corrected, patch, term = first_call(where, rows, probe, target, tables)
    arrived = among(sent, "core", 1)
    kept, *rows = second_call(where, corrected, patch, term, probe, tables)

    pieces = [(kept[d] + arrived[d]).reshape(-1, pattern) for d in range(4)]
    pieces, rows = tied(pieces, rows)
    pieces = pieces[:1] + exchanged(pieces, 0)
    rows = rows[:1] + [among(rows[d], "zl", d) for d in (1, 2, 3)]
    mine = total_of(pieces).reshape(4, -1, pattern)
    body, margin = place_call(own_class, spots, rows, tile_side)
    inside = tile_side // GROUPS

    pieces = [lax.dynamic_index_in_dim(mine, next_turn ^ d, 0, keepdims=False) for d in range(4)]
    pieces, margin = tied(pieces, margin)
    body = body.at[:, :, :pattern].add(across_columns(margin, 1))
    pieces = pieces[:1] + exchanged(pieces, 1)
    mine = total_of(pieces).reshape(8, -1, pattern)

    mine, lower = tied(mine, body[:, inside:])
    from_above = across_rows(lower, 1)
    spread = lax.all_to_all(mine, ("zh", "zl"), 0, 0, tiled=True)
    mine = jnp.sum(spread, axis=0) * (1.0 / math.sqrt(mesh_size()))
    body = body[:, :inside].at[:, : pattern // GROUPS].add(from_above)

    spread, body = tied(jnp.broadcast_to(mine[None], (8,) + mine.shape), body)
    second = among(body, "zl", 2)
    mine = lax.all_to_all(spread, ("zh", "zl"), 0, 0, tiled=True).reshape(-1, pattern)
    mine, body, second = tied(mine, body, second)
    first = among(body, "zl", 1)
    mine = by_place([mine] + [exchange(mine, d, 1) for d in (1, 2, 3)], next_turn)
    mine, body, first = tied(mine, body, first)
    third = among(body, "zl", 3)
    pieces = exchanged([mine] * 4, 0)
    other = [among(mine, "core", 1)]
    pieces, third = tied(pieces, third)
    other = other + [among(piece, "core", 1) for piece in pieces]
    return (join_call(own_class, [body, first, second, third]), fill_call(where, [mine, *pieces, *other], probe.shape))


def mesh_size():
    return math.prod(SIZES)


def solution(mesh):
    fine = Mesh(mesh.devices.reshape(SIZES), AXES)
    placed = (
        P(TILE_AXES, None, None, None),
        P(),
        P(TILE_AXES, "zl", None),
        P(TILE_AXES, "zl", None, None),
    )
    return jax.shard_map(
        shards,
        mesh=fine,
        in_specs=placed,
        out_specs=(P(TILE_AXES, None, None, None), P()),
        check_vma=False,
    )
```

time: 537 us -> 175 us (0.33)
  waiting for transfers between devices: 404 us -> 57.7 us
  starting transfers between devices: 21.1 us -> 65 us
  matrix products: 38.8 us -> 1.74 us
  Pallas kernels: 0 us -> 23.8 us
  local copies, waits for them, and re-layouts: 25.7 us -> 2.74 us
  other arithmetic: 23.5 us -> 3.49 us
  blocking collectives: 0 us -> 18.9 us
  between operations: 18.3 us -> 1.22 us
    psum x2 -> x0, waiting for transfers between devices: 345 us -> none  [the longest x1 283 us: shards(): summed = lax.psum(grad_probe, ('tile', 'batch'))]
    ppermute x4 -> x34, starting transfers between devices: 21.1 us -> 61.3 us  [the longest x12 26.3 us: exchange(): return lax.ppermute(block, AXES, route)]
    dot_general x4 -> x2, matrix products: 38.8 us -> 1.74 us  [the longest x1 1.33 us: by_parity(): jnp.dot(table, amplitude, precision=exact)]
    pallas_call x0 -> x6, Pallas kernels: none -> 23.8 us  [the longest x1 12.2 us: first_call(): pl.pallas_call(first_kernel, out_shape=[jax.ShapeDtypeStruct(s, F32) for...]
    all_to_all x0 -> x1, blocking collectives: none -> 18.9 us  [shards(): lax.all_to_all(spread, ('zh', 'zl'), 0, 0, tiled=True).reshape(-1, pattern)]
    unnamed x16 -> x36, local copies, waits for them, and re-layouts: 13.5 us -> 0.77 us
    ppermute x4 -> x34, waiting for transfers between devices: 59.4 us -> 49.1 us  [the longest x17 31.4 us: among(): return lax.ppermute(block, axis, [(i, i ^ distance) for i in range(n)])]
    all_to_all x0 -> x1, waiting for transfers between devices: none -> 8.55 us  [shards(): spread = lax.all_to_all(mine, ('zh', 'zl'), 0, 0, tiled=True)]
  transfers between devices with their start and end apart: 6 -> 35, of which waited for: 6 -> 20; matrix products, arithmetic and copies ran while one was open for 5% -> 2% of each run, Pallas kernels for 0% -> 4%
where the time goes in v1:
time: 175 us
  starting transfers between devices  65 us (37%)
  waiting for transfers between devices  57.7 us (33%)
  Pallas kernels  23.8 us (14%)
  blocking collectives  18.9 us (11%)
  other arithmetic  3.49 us (2%)
  local copies, waits for them, and re-layouts  2.74 us (2%)
    ppermute x17, waiting for transfers between devices, among(): return lax.ppermute(block, axis, [(i, i ^ distance) for i in range(n)])  31.4 us
    ppermute x12, starting transfers between devices, exchange(): return lax.ppermute(block, AXES, route)  26.3 us
    all_to_all x1, blocking collectives, shards(): lax.all_to_all(spread, ('zh', 'zl'), 0, 0, tiled=True).reshape(-1, pattern)  18.9 us
    ppermute x17, starting transfers between devices, among(): return lax.ppermute(block, axis, [(i, i ^ distance) for i in range(n)])  18.3 us
    ppermute x3, starting transfers between devices, across_columns(): return lax.ppermute(block, TILE_AXES, route)  14.1 us
    pallas_call x1, Pallas kernels, first_call(): pl.pallas_call(first_kernel, out_shape=[jax.ShapeDtypeStruct(s, F32) for...  12.2 us
    ppermute x12, waiting for transfers between devices, exchange(): return lax.ppermute(block, AXES, route)  9.08 us
    ppermute x3, waiting for transfers between devices, across_columns(): return lax.ppermute(block, TILE_AXES, route)  8.55 us
  transfers between devices with their start and end apart: 35, of which 20 were waited for; matrix products, arithmetic and copies ran while one was open for 2% of the time, Pallas kernels for 4%

profile of v1, /device:TPU:1, one launch (start us, length us, event | category | flops | bytes accessed | tf_op | source)
XLA Modules:
  0.0 174.5 jit_solution(16660415226682563101)
XLA Ops:
  0.7 1.1 dynamic-slice_bitcast_fusion
  1.9 1.4 collective-permute-start
  3.3 5.1 %collective-permute-start.1 = (f32[2,96,256]{2,1,0:T(8,128)S(1)}, f32[2,96,256]{2,1,0:T(8,128)S(1)}, u32[]{:S(2)}, u32[]{:S(2)}) collective-permute-start(f32[2,96,256]{2,1,0:T(8,128)S(1)} %slice.112), channel_id=1, source_target_pairs={{4,0},{8,4},{12,8},{20,16},{24,20},{28,24},{36,32},{40,36},{44,40}... | collective-permute-start | bytes 589832 | tf_op jit(solution)/shard_map/ppermute | solution.py:378
  8.5 1.3 fusion
  10.3 0.9 collective-permute-done.1.right_ref
  11.2 5.2 %collective-permute-start.4 = (s32[2]{0:T(128)S(1)}, s32[2]{0:T(128)S(1)}, u32[]{:S(2)}, u32[]{:S(2)}) collective-permute-start(s32[2]{0:T(128)S(1)} %bitcast.51), channel_id=1, source_target_pairs={{0,3},{1,2},{2,1},{3,0},{4,7},{5,6},{6,5},{7,4},{8,11},{9,10},{10,... | collective-permute-start | bytes 32 | tf_op jit(solution)/shard_map/ppermute | solution.py:393
  17.4 2.3 %collective-permute-done.3.spot2 = s32[2]{0:T(128)S(1)} collective-permute-done((s32[2]{0:T(128)S(1)}, s32[2]{0:T(128)S(1)}, u32[]{:S(2)}, u32[]{:S(2)}) %collective-permute-start.3) | collective-permute-done | bytes 40 | tf_op jit(solution)/shard_map/ppermute | solution.py:393
  19.7 1.9 %collective-permute-start.5 = (f32[2,64,256]{2,1,0:T(8,128)S(1)}, f32[2,64,256]{2,1,0:T(8,128)S(1)}, u32[]{:S(2)}, u32[]{:S(2)}) collective-permute-start(f32[2,64,256]{2,1,0:T(8,128)S(1)} %slice.98), channel_id=1, source_target_pairs={{4,0},{8,4},{12,8},{20,16},{24,20},{28,24},{36,32},{40,36},{44,40}... | collective-permute-start | bytes 393224 | tf_op jit(solution)/shard_map/ppermute | solution.py:378
  21.6 4.4 %collective-permute-done.5.corner_ref = f32[2,64,256]{2,1,0:T(8,128)S(1)} collective-permute-done((f32[2,64,256]{2,1,0:T(8,128)S(1)}, f32[2,64,256]{2,1,0:T(8,128)S(1)}, u32[]{:S(2)}, u32[]{:S(2)}) %collective-permute-start.5) | collective-permute-done | bytes 131104 | tf_op jit(solution)/shard_map/ppermute | solution.py:378
  26.0 1.6 cut.1
  27.6 1.5 collective-permute-start.7
  29.1 2.2 %collective-permute-start.8 = (f32[2,9,8,256]{3,2,1,0:T(8,128)}, f32[2,9,8,256]{3,2,1,0:T(8,128)S(1)}, u32[]{:S(2)}, u32[]{:S(2)}) collective-permute-start(f32[2,9,8,256]{3,2,1,0:T(8,128)} %get-tuple-element.86), channel_id=1, source_target_pairs={{0,3},{1,2},{2,1},{3,0},{4,7},{5,6},{6,5},{7,4},{8,11},{9,10},{10,... | collective-permute-start | bytes 442376 | tf_op jit(solution)/shard_map/ppermute | solution.py:393
  31.9 1.4 collective-permute-done.6.rows1
  33.3 6.6 %collective-permute-done.7.rows2 = f32[2,9,8,256]{3,2,1,0:T(8,128)S(1)} collective-permute-done((f32[2,9,8,256]{3,2,1,0:T(8,128)}, f32[2,9,8,256]{3,2,1,0:T(8,128)S(1)}, u32[]{:S(2)}, u32[]{:S(2)}) %collective-permute-start.7) | collective-permute-done | bytes 147488 | tf_op jit(solution)/shard_map/ppermute | solution.py:393
  40.6 12.2 %outward.1 = (f32[4,2,256,256]{3,2,1,0:T(8,128)S(1)}, f32[4,2,256,256]{3,2,1,0:T(8,128)}, f32[2,256,256]{2,1,0:T(8,128)S(1)}, f32[2,256,256]{2,1,0:T(8,128)S(1)}) custom-call(s32[5]{0:T(128)S(1)} %stack.19.where_ref, f32[2,9,8,256]{3,2,1,0:T(8,128)S(1)} %get-tuple-element.83.rows0, f32[2,9,8,256]{3,2,1,0:T(8,128)S(1)} %collective-permute-done.6.rows1, ...), custom_call_target="tpu_custom_call" | custom-call | tf_op jit(solution)/shard_map/outward/pallas_call | solution.py:207
  52.8 5.4 %homeward.1 = (f32[4,2,256,256]{3,2,1,0:T(8,128)S(1)}, f32[2,9,8,256]{3,2,1,0:T(8,128)S(1)}, f32[2,9,8,256]{3,2,1,0:T(8,128)S(1)}, f32[2,9,8,256]{3,2,1,0:T(8,128)S(1)}, f32[2,9,8,256]{3,2,1,0:T(8,128)S(1)}) custom-call(s32[5]{0:T(128)S(1)} %stack.19.where_ref, f32[4,2,256,256]{3,2,1,0:T(8,128)} %get-tuple-element.88.corrected_ref, ...), custom_call_target="tpu_custom_call" | custom-call | tf_op jit(solution)/shard_map/homeward/pallas_call | solution.py:228
  58.3 1.1 slice_add_fusion
  59.4 10.2 %collective-permute-start.10 = (f32[512,256]{1,0:T(8,128)}, f32[512,256]{1,0:T(8,128)}, u32[]{:S(2)}, u32[]{:S(2)}) collective-permute-start(f32[512,256]{1,0:T(8,128)} %bitcast.10), channel_id=1, source_target_pairs={{0,8},{1,9},{2,10},{3,11},{4,68},{5,69},{6,70},{7,71},{8,0},{9,1},... | collective-permute-start | bytes 1572872 | tf_op jit(solution)/shard_map/ppermute | solution.py:401
  69.6 2.9 %collective-permute-start.11 = (f32[512,256]{1,0:T(8,128)S(1)}, f32[512,256]{1,0:T(8,128)}, u32[]{:S(2)}, u32[]{:S(2)}) collective-permute-start(f32[512,256]{1,0:T(8,128)S(1)} %bitcast.60), channel_id=1, source_target_pairs={{0,16},{1,17},{2,18},{3,19},{4,132},{5,133},{6,134},{7,135},{8,24}... | collective-permute-start | bytes 1572872 | tf_op jit(solution)/shard_map/ppermute | solution.py:401
  72.5 2.0 %collective-permute-start.13 = (f32[2,9,8,256]{3,2,1,0:T(8,128)S(1)}, f32[2,9,8,256]{3,2,1,0:T(8,128)S(1)}, u32[]{:S(2)}, u32[]{:S(2)}) collective-permute-start(f32[2,9,8,256]{3,2,1,0:T(8,128)S(1)} %get-tuple-element.102), channel_id=1, source_target_pairs={{0,1},{1,0},{2,3},{3,2},{4,5},{5,4},{6,7},{7,6},{8,9},{9,8},{10,11... | collective-permute-start | bytes 442376 | tf_op jit(solution)/shard_map/ppermute | solution.py:393
  74.5 1.0 collective-permute-start.14
  75.5 4.2 %collective-permute-done.13.rows1 = f32[2,9,8,256]{3,2,1,0:T(8,128)S(1)} collective-permute-done((f32[2,9,8,256]{3,2,1,0:T(8,128)S(1)}, f32[2,9,8,256]{3,2,1,0:T(8,128)S(1)}, u32[]{:S(2)}, u32[]{:S(2)}) %collective-permute-start.13) | collective-permute-done | bytes 147488 | tf_op jit(solution)/shard_map/ppermute | solution.py:393
  80.5 1.5 collective-permute-done.14.rows2
  82.1 3.5 %collective-permute-done.15.rows3 = f32[2,9,8,256]{3,2,1,0:T(8,128)S(1)} collective-permute-done((f32[2,9,8,256]{3,2,1,0:T(8,128)S(1)}, f32[2,9,8,256]{3,2,1,0:T(8,128)S(1)}, u32[]{:S(2)}, u32[]{:S(2)}) %collective-permute-start.15) | collective-permute-done | bytes 147488 | tf_op jit(solution)/shard_map/ppermute | solution.py:393
  85.6 0.9 place.1
  86.5 1.0 collective-permute-done.12
  87.5 1.5 add_add_fusion
  89.0 1.3 collective-permute-start.16
  90.3 2.7 %collective-permute-start.18 = (f32[128,256]{1,0:T(8,128)S(1)}, f32[128,256]{1,0:T(8,128)S(1)}, u32[]{:S(2)}, u32[]{:S(2)}) collective-permute-start(f32[128,256]{1,0:T(8,128)S(1)} %get-tuple-element.109), channel_id=1, source_target_pairs={{0,192},{1,193},{2,194},{3,195},{4,28},{5,29},{6,30},{7,31},{8,200... | collective-permute-start | bytes 393224 | tf_op jit(solution)/shard_map/ppermute | solution.py:401
  93.0 7.0 %collective-permute-start.19 = (f32[2,160,256]{2,1,0:T(8,128)S(1)}, f32[2,160,256]{2,1,0:T(8,128)S(1)}, u32[]{:S(2)}, u32[]{:S(2)}) collective-permute-start(f32[2,160,256]{2,1,0:T(8,128)S(1)} %get-tuple-element.111), channel_id=1, source_target_pairs={{0,4},{4,8},{8,12},{16,20},{20,24},{24,28},{32,36},{36,40},{40,44}... | collective-permute-start | bytes 983048 | tf_op jit(solution)/shard_map/ppermute | solution.py:378
  100.7 3.3 %collective-permute-done.19 = f32[2,160,256]{2,1,0:T(8,128)S(1)} collective-permute-done((f32[2,160,256]{2,1,0:T(8,128)S(1)}, f32[2,160,256]{2,1,0:T(8,128)S(1)}, u32[]{:S(2)}, u32[]{:S(2)}) %collective-permute-start.19) | collective-permute-done | bytes 327712 | tf_op jit(solution)/shard_map/ppermute | solution.py:378
  104.1 1.3 collective-permute-start.20
  105.4 3.7 %all-to-all-start = ((f32[8,16,256]{2,1,0:T(8,128)}), f32[8,16,256]{2,1,0:T(8,128)S(1)}, u32[]{:S(2)}, u32[]{:S(2)}) async-start(f32[8,16,256]{2,1,0:T(8,128)} %bitcast.18), calls=%async_computation | async-start | bytes 262144 | tf_op jit(solution)/shard_map/all_to_all | solution.py:476
  109.2 8.5 %all-to-all-done = f32[8,16,256]{2,1,0:T(8,128)S(1)} async-done(((f32[8,16,256]{2,1,0:T(8,128)}), f32[8,16,256]{2,1,0:T(8,128)S(1)}, u32[]{:S(2)}, u32[]{:S(2)}) %all-to-all-start) | async-done | bytes 131104 | tf_op jit(solution)/shard_map/all_to_all | solution.py:476
  117.9 18.9 %all_to_all.10 = f32[8,16,256]{2,1,0:T(8,128)S(1)} all-to-all(f32[8,16,256]{2,1,0:T(8,128)S(1)} %broadcast_in_dim.2), channel_id=1, replica_groups=mesh['y'=4,'zh'=2,'x'=4,'core'=2,'zl'=4] {'zh','zl'}, dimensions={0} | all-to-all | bytes 262144 | tf_op jit(solution)/shard_map/all_to_all | solution.py:482
  136.8 5.6 %collective-permute-start.23 = (f32[128,256]{1,0:T(8,128)S(1)}, f32[128,256]{1,0:T(8,128)S(1)}, u32[]{:S(2)}, u32[]{:S(2)}) collective-permute-start(f32[128,256]{1,0:T(8,128)S(1)} %bitcast.62), channel_id=1, source_target_pairs={{0,128},{1,129},{2,130},{3,131},{4,20},{5,21},{6,22},{7,23},{8,136... | collective-permute-start | bytes 393224 | tf_op jit(solution)/shard_map/ppermute | solution.py:401
  142.9 3.3 %collective-permute-done.23 = f32[128,256]{1,0:T(8,128)S(1)} collective-permute-done((f32[128,256]{1,0:T(8,128)S(1)}, f32[128,256]{1,0:T(8,128)S(1)}, u32[]{:S(2)}, u32[]{:S(2)}) %collective-permute-start.23) | collective-permute-done | bytes 131104 | tf_op jit(solution)/shard_map/ppermute | solution.py:401
  146.2 1.4 collective-permute-done.22
  147.7 3.7 %collective-permute-done.25.rows1 = f32[2,96,384]{2,1,0:T(8,128)S(1)} collective-permute-done((f32[2,96,384]{2,1,0:T(8,128)S(1)}, f32[2,96,384]{2,1,0:T(8,128)S(1)}, u32[]{:S(2)}, u32[]{:S(2)}) %collective-permute-start.25) | collective-permute-done | bytes 294944 | tf_op jit(solution)/shard_map/ppermute | solution.py:393
  151.4 1.6 collective-permute-start.27
  153.0 1.7 collective-permute-start.26
  154.7 0.9 collective-permute-start.29
  155.6 2.2 %collective-permute-start.30 = (f32[512,256]{1,0:T(8,128)S(1)}, f32[512,256]{1,0:T(8,128)S(1)}, u32[]{:S(2)}, u32[]{:S(2)}) collective-permute-start(f32[512,256]{1,0:T(8,128)S(1)} %pad_maximum_fusion), channel_id=1, source_target_pairs={{0,4},{4,0},{1,5},{5,1},{2,6},{6,2},{3,7},{7,3},{8,12},{12,8},{9,1... | collective-permute-start | bytes 1572872 | tf_op jit(solution)/shard_map/ppermute | solution.py:393
  157.7 6.1 %collective-permute-done.29.rows3 = f32[2,96,384]{2,1,0:T(8,128)S(1)} collective-permute-done((f32[2,96,384]{2,1,0:T(8,128)S(1)}, f32[2,96,384]{2,1,0:T(8,128)S(1)}, u32[]{:S(2)}, u32[]{:S(2)}) %collective-permute-start.29) | collective-permute-done | bytes 294944 | tf_op jit(solution)/shard_map/ppermute | solution.py:393
  163.8 2.7 %collective-permute-done.28 = f32[512,256]{1,0:T(8,128)S(1)} collective-permute-done((f32[512,256]{1,0:T(8,128)S(1)}, f32[512,256]{1,0:T(8,128)S(1)}, u32[]{:S(2)}, u32[]{:S(2)}) %collective-permute-start.28) | collective-permute-done | bytes 524320 | tf_op jit(solution)/shard_map/ppermute | solution.py:401
  167.2 1.5 collective-permute-start.31
  169.2 1.1 join.1
  171.8 2.6 %fill.1 = f32[8,2,256,256]{3,2,1,0:T(8,128)} custom-call(s32[5]{0:T(128)S(1)} %stack.19.where_ref, f32[2,256,256]{2,1,0:T(8,128)S(1)} %bitcast.40, f32[2,256,256]{2,1,0:T(8,128)S(1)} %bitcast.45, f32[2,256,256]{2,1,0:T(8,128)S(1)} %bitcast.44, f32[2,256,256]{2,1,0:T(8,128)S(1)} %bitcast.43, f32[2,256,256]{2,1,0:T(8,128)S(1)} %bitcast.46, ...), custom_call_target="tpu_custom_call" | custom-call | tf_op jit(solution)/shard_map/fill/pallas_call | solution.py:354
  (85 shorter events, 7.9 us)
Async XLA Ops:
  0.6 25.3 %copy-start.1 = (f32[1,2,384,384]{3,2,1,0:T(8,128)S(1)}, f32[1,2,384,384]{3,2,1,0:T(8,128)}, u32[]{:S(2)}) copy-start(f32[1,2,384,384]{3,2,1,0:T(8,128)} %param.15) | copy-start | bytes 3538948
  0.7 10.6 %copy-start.7 = (s32[1,1,2]{2,1,0:T(1,128)S(1)}, s32[1,1,2]{2,1,0:T(1,128)}, u32[]{:S(2)}) copy-start(s32[1,1,2]{2,1,0:T(1,128)} %param.17) | copy-start | bytes 28
  0.7 25.3 %copy-start.8 = (s32[1,1,2]{2,1,0:T(1,128)S(1)}, s32[1,1,2]{2,1,0:T(1,128)}, u32[]{:S(2)}) copy-start(s32[1,1,2]{2,1,0:T(1,128)} %param.17) | copy-start | bytes 28
  1.8 38.1 %copy-start.2 = (bf16[768,256]{1,0:T(8,128)(2,1)S(1)}, bf16[768,256]{1,0:T(8,128)(2,1)}, u32[]{:S(2)}) copy-start(bf16[768,256]{1,0:T(8,128)(2,1)} %constant.134.clone.down_t) | copy-start | bytes 1179652
  1.8 38.1 %copy-start.3 = (bf16[256,768]{1,0:T(8,128)(2,1)S(1)}, bf16[256,768]{1,0:T(8,128)(2,1)}, u32[]{:S(2)}) copy-start(bf16[256,768]{1,0:T(8,128)(2,1)} %constant.133.clone.across) | copy-start | bytes 1179652
  1.8 38.0 %copy-start.4 = (f32[2,128,128]{2,1,0:T(8,128)S(1)}, f32[2,128,128]{2,1,0:T(8,128)}, u32[]{:S(2)}) copy-start(f32[2,128,128]{2,1,0:T(8,128)} %constant.137.clone.rows_ref) | copy-start | bytes 393220
  1.8 38.0 %copy-start.5 = (bf16[256,768]{1,0:T(8,128)(2,1)S(1)}, bf16[256,768]{1,0:T(8,128)(2,1)}, u32[]{:S(2)}) copy-start(bf16[256,768]{1,0:T(8,128)(2,1)} %constant.135.clone.across_t) | copy-start | bytes 1179652
  1.9 38.0 %copy-start.6 = (bf16[768,256]{1,0:T(8,128)(2,1)S(1)}, bf16[768,256]{1,0:T(8,128)(2,1)}, u32[]{:S(2)}) copy-start(bf16[768,256]{1,0:T(8,128)(2,1)} %constant.132.clone.down) | copy-start | bytes 1179652
  1.9 14.8 %collective-permute-start = (f32[2,64,384]{2,1,0:T(8,128)S(1)}, f32[2,64,384]{2,1,0:T(8,128)S(1)}, u32[]{:S(2)}, u32[]{:S(2)}) collective-permute-start(f32[2,64,384]{2,1,0:T(8,128)S(1)} %slice.111), channel_id=1, source_target_pairs={{16,0},{17,1},{18,2},{19,3},{20,4},{21,5},{22,6},{23,7},{24,8},{25... | collective-permute-start | bytes 589832 | tf_op jit(solution)/shard_map/ppermute | solution.py:388
  3.3 7.9 %collective-permute-start.1 = (f32[2,96,256]{2,1,0:T(8,128)S(1)}, f32[2,96,256]{2,1,0:T(8,128)S(1)}, u32[]{:S(2)}, u32[]{:S(2)}) collective-permute-start(f32[2,96,256]{2,1,0:T(8,128)S(1)} %slice.112), channel_id=1, source_target_pairs={{4,0},{8,4},{12,8},{20,16},{24,20},{28,24},{36,32},{40,36},{44,40}... | collective-permute-start | bytes 589832 | tf_op jit(solution)/shard_map/ppermute | solution.py:378
  11.2 6.2 %collective-permute-start.4 = (s32[2]{0:T(128)S(1)}, s32[2]{0:T(128)S(1)}, u32[]{:S(2)}, u32[]{:S(2)}) collective-permute-start(s32[2]{0:T(128)S(1)} %bitcast.51), channel_id=1, source_target_pairs={{0,3},{1,2},{2,1},{3,0},{4,7},{5,6},{6,5},{7,4},{8,11},{9,10},{10,... | collective-permute-start | bytes 32 | tf_op jit(solution)/shard_map/ppermute | solution.py:393
  16.4 3.3 %collective-permute-start.3 = (s32[2]{0:T(128)S(1)}, s32[2]{0:T(128)S(1)}, u32[]{:S(2)}, u32[]{:S(2)}) collective-permute-start(s32[2]{0:T(128)S(1)} %bitcast.52), channel_id=1, source_target_pairs={{0,2},{1,3},{2,0},{3,1},{4,6},{5,7},{6,4},{7,5},{8,10},{9,11},{10,... | collective-permute-start | bytes 32 | tf_op jit(solution)/shard_map/ppermute | solution.py:393
  16.4 3.3 %collective-permute-start.2 = (s32[2]{0:T(128)S(1)}, s32[2]{0:T(128)S(1)}, u32[]{:S(2)}, u32[]{:S(2)}) collective-permute-start(s32[2]{0:T(128)S(1)} %bitcast.53), channel_id=1, source_target_pairs={{0,1},{1,0},{2,3},{3,2},{4,5},{5,4},{6,7},{7,6},{8,9},{9,8},{10,11... | collective-permute-start | bytes 32 | tf_op jit(solution)/shard_map/ppermute | solution.py:393
  17.4 11.7 %copy-start.11 = (s32[2]{0:T(128)}, s32[2]{0:T(128)S(1)}, u32[]{:S(2)}) copy-start(s32[2]{0:T(128)S(1)} %collective-permute-done.4.spot3) | copy-start | bytes 28
  19.7 6.3 %collective-permute-start.5 = (f32[2,64,256]{2,1,0:T(8,128)S(1)}, f32[2,64,256]{2,1,0:T(8,128)S(1)}, u32[]{:S(2)}, u32[]{:S(2)}) collective-permute-start(f32[2,64,256]{2,1,0:T(8,128)S(1)} %slice.98), channel_id=1, source_target_pairs={{4,0},{8,4},{12,8},{20,16},{24,20},{28,24},{36,32},{40,36},{44,40}... | collective-permute-start | bytes 393224 | tf_op jit(solution)/shard_map/ppermute | solution.py:378
  27.6 5.7 %collective-permute-start.6 = (f32[2,9,8,256]{3,2,1,0:T(8,128)}, f32[2,9,8,256]{3,2,1,0:T(8,128)S(1)}, u32[]{:S(2)}, u32[]{:S(2)}) collective-permute-start(f32[2,9,8,256]{3,2,1,0:T(8,128)} %get-tuple-element.84), channel_id=1, source_target_pairs={{0,1},{1,0},{2,3},{3,2},{4,5},{5,4},{6,7},{7,6},{8,9},{9,8},{10,11... | collective-permute-start | bytes 442376 | tf_op jit(solution)/shard_map/ppermute | solution.py:393
  27.6 12.3 %collective-permute-start.7 = (f32[2,9,8,256]{3,2,1,0:T(8,128)}, f32[2,9,8,256]{3,2,1,0:T(8,128)S(1)}, u32[]{:S(2)}, u32[]{:S(2)}) collective-permute-start(f32[2,9,8,256]{3,2,1,0:T(8,128)} %get-tuple-element.85), channel_id=1, source_target_pairs={{0,2},{1,3},{2,0},{3,1},{4,6},{5,7},{6,4},{7,5},{8,10},{9,11},{10,... | collective-permute-start | bytes 442376 | tf_op jit(solution)/shard_map/ppermute | solution.py:393
  29.1 10.8 %collective-permute-start.8 = (f32[2,9,8,256]{3,2,1,0:T(8,128)}, f32[2,9,8,256]{3,2,1,0:T(8,128)S(1)}, u32[]{:S(2)}, u32[]{:S(2)}) collective-permute-start(f32[2,9,8,256]{3,2,1,0:T(8,128)} %get-tuple-element.86), channel_id=1, source_target_pairs={{0,3},{1,2},{2,1},{3,0},{4,7},{5,6},{6,5},{7,4},{8,11},{9,10},{10,... | collective-permute-start | bytes 442376 | tf_op jit(solution)/shard_map/ppermute | solution.py:393
  52.8 5.4 %collective-permute-start.9 = (f32[4,2,256,256]{3,2,1,0:T(8,128)S(1)}, f32[4,2,256,256]{3,2,1,0:T(8,128)S(1)}, u32[]{:S(2)}, u32[]{:S(2)}) collective-permute-start(f32[4,2,256,256]{3,2,1,0:T(8,128)S(1)} %get-tuple-element.92), channel_id=1, source_target_pairs={{0,4},{4,0},{1,5},{5,1},{2,6},{6,2},{3,7},{7,3},{8,12},{12,8},{9,1... | collective-permute-start | bytes 6291464 | tf_op jit(solution)/shard_map/ppermute | solution.py:393
  58.2 27.4 %copy-start.9 = (s32[1,1,2]{2,1,0:T(1,128)S(1)}, s32[1,1,2]{2,1,0:T(1,128)}, u32[]{:S(2)}) copy-start(s32[1,1,2]{2,1,0:T(1,128)} %param.17) | copy-start | bytes 28
  58.2 27.3 %copy-start.12 = (s32[2]{0:T(128)S(1)}, s32[2]{0:T(128)}, u32[]{:S(2)}) copy-start(s32[2]{0:T(128)} %copy-done.11) | copy-start | bytes 28
  58.2 27.3 %copy-start.14 = (s32[2]{0:T(128)S(1)}, s32[2]{0:T(128)}, u32[]{:S(2)}) copy-start(s32[2]{0:T(128)} %copy-done.13) | copy-start | bytes 28
  58.2 27.3 %copy-start.16 = (s32[2]{0:T(128)S(1)}, s32[2]{0:T(128)}, u32[]{:S(2)}) copy-start(s32[2]{0:T(128)} %copy-done.15) | copy-start | bytes 28
  59.4 27.1 %collective-permute-start.10 = (f32[512,256]{1,0:T(8,128)}, f32[512,256]{1,0:T(8,128)}, u32[]{:S(2)}, u32[]{:S(2)}) collective-permute-start(f32[512,256]{1,0:T(8,128)} %bitcast.10), channel_id=1, source_target_pairs={{0,8},{1,9},{2,10},{3,11},{4,68},{5,69},{6,70},{7,71},{8,0},{9,1},... | collective-permute-start | bytes 1572872 | tf_op jit(solution)/shard_map/ppermute | solution.py:401
  69.6 16.9 %collective-permute-start.11 = (f32[512,256]{1,0:T(8,128)S(1)}, f32[512,256]{1,0:T(8,128)}, u32[]{:S(2)}, u32[]{:S(2)}) collective-permute-start(f32[512,256]{1,0:T(8,128)S(1)} %bitcast.60), channel_id=1, source_target_pairs={{0,16},{1,17},{2,18},{3,19},{4,132},{5,133},{6,134},{7,135},{8,24}... | collective-permute-start | bytes 1572872 | tf_op jit(solution)/shard_map/ppermute | solution.py:401
  72.5 15.0 %collective-permute-start.12 = (f32[512,256]{1,0:T(8,128)S(1)}, f32[512,256]{1,0:T(8,128)}, u32[]{:S(2)}, u32[]{:S(2)}) collective-permute-start(f32[512,256]{1,0:T(8,128)S(1)} %bitcast.59), channel_id=1, source_target_pairs={{0,24},{1,25},{2,26},{3,27},{4,196},{5,197},{6,198},{7,199},{8,16}... | collective-permute-start | bytes 1572872 | tf_op jit(solution)/shard_map/ppermute | solution.py:401
  72.5 7.2 %collective-permute-start.13 = (f32[2,9,8,256]{3,2,1,0:T(8,128)S(1)}, f32[2,9,8,256]{3,2,1,0:T(8,128)S(1)}, u32[]{:S(2)}, u32[]{:S(2)}) collective-permute-start(f32[2,9,8,256]{3,2,1,0:T(8,128)S(1)} %get-tuple-element.102), channel_id=1, source_target_pairs={{0,1},{1,0},{2,3},{3,2},{4,5},{5,4},{6,7},{7,6},{8,9},{9,8},{10,11... | collective-permute-start | bytes 442376 | tf_op jit(solution)/shard_map/ppermute | solution.py:393
  74.5 7.6 %collective-permute-start.14 = (f32[2,9,8,256]{3,2,1,0:T(8,128)S(1)}, f32[2,9,8,256]{3,2,1,0:T(8,128)S(1)}, u32[]{:S(2)}, u32[]{:S(2)}) collective-permute-start(f32[2,9,8,256]{3,2,1,0:T(8,128)S(1)} %get-tuple-element.103), channel_id=1, source_target_pairs={{0,2},{1,3},{2,0},{3,1},{4,6},{5,7},{6,4},{7,5},{8,10},{9,11},{10,... | collective-permute-start | bytes 442376 | tf_op jit(solution)/shard_map/ppermute | solution.py:393
  79.7 5.8 %collective-permute-start.15 = (f32[2,9,8,256]{3,2,1,0:T(8,128)S(1)}, f32[2,9,8,256]{3,2,1,0:T(8,128)S(1)}, u32[]{:S(2)}, u32[]{:S(2)}) collective-permute-start(f32[2,9,8,256]{3,2,1,0:T(8,128)S(1)} %get-tuple-element.104), channel_id=1, source_target_pairs={{0,3},{1,2},{2,1},{3,0},{4,7},{5,6},{6,5},{7,4},{8,11},{9,10},{10,... | collective-permute-start | bytes 442376 | tf_op jit(solution)/shard_map/ppermute | solution.py:393
  89.0 11.0 %collective-permute-start.16 = (f32[128,256]{1,0:T(8,128)S(1)}, f32[128,256]{1,0:T(8,128)S(1)}, u32[]{:S(2)}, u32[]{:S(2)}) collective-permute-start(f32[128,256]{1,0:T(8,128)S(1)} %get-tuple-element.107), channel_id=1, source_target_pairs={{0,64},{1,65},{2,66},{3,67},{4,12},{5,13},{6,14},{7,15},{8,72},{9,... | collective-permute-start | bytes 393224 | tf_op jit(solution)/shard_map/ppermute | solution.py:401
  90.3 9.7 %collective-permute-start.17 = (f32[128,256]{1,0:T(8,128)S(1)}, f32[128,256]{1,0:T(8,128)S(1)}, u32[]{:S(2)}, u32[]{:S(2)}) collective-permute-start(f32[128,256]{1,0:T(8,128)S(1)} %get-tuple-element.108), channel_id=1, source_target_pairs={{0,128},{1,129},{2,130},{3,131},{4,20},{5,21},{6,22},{7,23},{8,136... | collective-permute-start | bytes 393224 | tf_op jit(solution)/shard_map/ppermute | solution.py:401
  90.3 9.7 %collective-permute-start.18 = (f32[128,256]{1,0:T(8,128)S(1)}, f32[128,256]{1,0:T(8,128)S(1)}, u32[]{:S(2)}, u32[]{:S(2)}) collective-permute-start(f32[128,256]{1,0:T(8,128)S(1)} %get-tuple-element.109), channel_id=1, source_target_pairs={{0,192},{1,193},{2,194},{3,195},{4,28},{5,29},{6,30},{7,31},{8,200... | collective-permute-start | bytes 393224 | tf_op jit(solution)/shard_map/ppermute | solution.py:401
  93.0 11.0 %collective-permute-start.19 = (f32[2,160,256]{2,1,0:T(8,128)S(1)}, f32[2,160,256]{2,1,0:T(8,128)S(1)}, u32[]{:S(2)}, u32[]{:S(2)}) collective-permute-start(f32[2,160,256]{2,1,0:T(8,128)S(1)} %get-tuple-element.111), channel_id=1, source_target_pairs={{0,4},{4,8},{8,12},{16,20},{20,24},{24,28},{32,36},{36,40},{40,44}... | collective-permute-start | bytes 983048 | tf_op jit(solution)/shard_map/ppermute | solution.py:378
  104.1 5.1 %collective-permute-start.20 = (f32[2,64,384]{2,1,0:T(8,128)S(1)}, f32[2,64,384]{2,1,0:T(8,128)S(1)}, u32[]{:S(2)}, u32[]{:S(2)}) collective-permute-start(f32[2,64,384]{2,1,0:T(8,128)S(1)} %slice.117), channel_id=1, source_target_pairs={{0,16},{1,17},{2,18},{3,19},{4,20},{5,21},{6,22},{7,23},{8,24},{9,... | collective-permute-start | bytes 589832 | tf_op jit(solution)/shard_map/ppermute | solution.py:388
  105.4 12.3 %all-to-all-start = ((f32[8,16,256]{2,1,0:T(8,128)}), f32[8,16,256]{2,1,0:T(8,128)S(1)}, u32[]{:S(2)}, u32[]{:S(2)}) async-start(f32[8,16,256]{2,1,0:T(8,128)} %bitcast.18), calls=%async_computation | async-start | bytes 262144 | tf_op jit(solution)/shard_map/all_to_all | solution.py:476
  117.8 19.0 %collective-permute-start.21 = (f32[2,96,384]{2,1,0:T(8,128)S(1)}, f32[2,96,384]{2,1,0:T(8,128)S(1)}, u32[]{:S(2)}, u32[]{:S(2)}) collective-permute-start(f32[2,96,384]{2,1,0:T(8,128)S(1)} %fusion.2.rows0), channel_id=1, source_target_pairs={{0,2},{1,3},{2,0},{3,1},{4,6},{5,7},{6,4},{7,5},{8,10},{9,11},{10,... | collective-permute-start | bytes 884744 | tf_op jit(solution)/shard_map/ppermute | solution.py:393
  136.8 6.1 %collective-permute-start.24 = (f32[128,256]{1,0:T(8,128)S(1)}, f32[128,256]{1,0:T(8,128)S(1)}, u32[]{:S(2)}, u32[]{:S(2)}) collective-permute-start(f32[128,256]{1,0:T(8,128)S(1)} %bitcast.61), channel_id=1, source_target_pairs={{0,64},{1,65},{2,66},{3,67},{4,12},{5,13},{6,14},{7,15},{8,72},{9,... | collective-permute-start | bytes 393224 | tf_op jit(solution)/shard_map/ppermute | solution.py:401
  136.8 9.4 %collective-permute-start.23 = (f32[128,256]{1,0:T(8,128)S(1)}, f32[128,256]{1,0:T(8,128)S(1)}, u32[]{:S(2)}, u32[]{:S(2)}) collective-permute-start(f32[128,256]{1,0:T(8,128)S(1)} %bitcast.62), channel_id=1, source_target_pairs={{0,128},{1,129},{2,130},{3,131},{4,20},{5,21},{6,22},{7,23},{8,136... | collective-permute-start | bytes 393224 | tf_op jit(solution)/shard_map/ppermute | solution.py:401
  142.5 5.2 %collective-permute-start.22 = (f32[128,256]{1,0:T(8,128)S(1)}, f32[128,256]{1,0:T(8,128)S(1)}, u32[]{:S(2)}, u32[]{:S(2)}) collective-permute-start(f32[128,256]{1,0:T(8,128)S(1)} %bitcast.63), channel_id=1, source_target_pairs={{0,192},{1,193},{2,194},{3,195},{4,28},{5,29},{6,30},{7,31},{8,200... | collective-permute-start | bytes 393224 | tf_op jit(solution)/shard_map/ppermute | solution.py:401
  142.7 8.7 %collective-permute-start.25 = (f32[2,96,384]{2,1,0:T(8,128)S(1)}, f32[2,96,384]{2,1,0:T(8,128)S(1)}, u32[]{:S(2)}, u32[]{:S(2)}) collective-permute-start(f32[2,96,384]{2,1,0:T(8,128)S(1)} %fusion.2.rows0), channel_id=1, source_target_pairs={{0,1},{1,0},{2,3},{3,2},{4,5},{5,4},{6,7},{7,6},{8,9},{9,8},{10,11... | collective-permute-start | bytes 884744 | tf_op jit(solution)/shard_map/ppermute | solution.py:393
  151.4 15.2 %collective-permute-start.28 = (f32[512,256]{1,0:T(8,128)S(1)}, f32[512,256]{1,0:T(8,128)S(1)}, u32[]{:S(2)}, u32[]{:S(2)}) collective-permute-start(f32[512,256]{1,0:T(8,128)S(1)} %pad_maximum_fusion), channel_id=1, source_target_pairs={{0,24},{1,25},{2,26},{3,27},{4,196},{5,197},{6,198},{7,199},{8,16}... | collective-permute-start | bytes 1572872 | tf_op jit(solution)/shard_map/ppermute | solution.py:401
  151.4 15.2 %collective-permute-start.27 = (f32[512,256]{1,0:T(8,128)S(1)}, f32[512,256]{1,0:T(8,128)S(1)}, u32[]{:S(2)}, u32[]{:S(2)}) collective-permute-start(f32[512,256]{1,0:T(8,128)S(1)} %pad_maximum_fusion), channel_id=1, source_target_pairs={{0,16},{1,17},{2,18},{3,19},{4,132},{5,133},{6,134},{7,135},{8,24}... | collective-permute-start | bytes 1572872 | tf_op jit(solution)/shard_map/ppermute | solution.py:401
  153.0 14.2 %collective-permute-start.26 = (f32[512,256]{1,0:T(8,128)S(1)}, f32[512,256]{1,0:T(8,128)S(1)}, u32[]{:S(2)}, u32[]{:S(2)}) collective-permute-start(f32[512,256]{1,0:T(8,128)S(1)} %pad_maximum_fusion), channel_id=1, source_target_pairs={{0,8},{1,9},{2,10},{3,11},{4,68},{5,69},{6,70},{7,71},{8,0},{9,1},... | collective-permute-start | bytes 1572872 | tf_op jit(solution)/shard_map/ppermute | solution.py:401
  154.7 9.2 %collective-permute-start.29 = (f32[2,96,384]{2,1,0:T(8,128)S(1)}, f32[2,96,384]{2,1,0:T(8,128)S(1)}, u32[]{:S(2)}, u32[]{:S(2)}) collective-permute-start(f32[2,96,384]{2,1,0:T(8,128)S(1)} %fusion.2.rows0), channel_id=1, source_target_pairs={{0,3},{1,2},{2,1},{3,0},{4,7},{5,6},{6,5},{7,4},{8,11},{9,10},{10,... | collective-permute-start | bytes 884744 | tf_op jit(solution)/shard_map/ppermute | solution.py:393
  155.6 14.8 %collective-permute-start.30 = (f32[512,256]{1,0:T(8,128)S(1)}, f32[512,256]{1,0:T(8,128)S(1)}, u32[]{:S(2)}, u32[]{:S(2)}) collective-permute-start(f32[512,256]{1,0:T(8,128)S(1)} %pad_maximum_fusion), channel_id=1, source_target_pairs={{0,4},{4,0},{1,5},{5,1},{2,6},{6,2},{3,7},{7,3},{8,12},{12,8},{9,1... | collective-permute-start | bytes 1572872 | tf_op jit(solution)/shard_map/ppermute | solution.py:393
  167.2 3.1 %collective-permute-start.31 = (f32[512,256]{1,0:T(8,128)S(1)}, f32[512,256]{1,0:T(8,128)S(1)}, u32[]{:S(2)}, u32[]{:S(2)}) collective-permute-start(f32[512,256]{1,0:T(8,128)S(1)} %collective-permute-done.26), channel_id=1, source_target_pairs={{0,4},{4,0},{1,5},{5,1},{2,6},{6,2},{3,7},{7,3},{8,12},{12,8},{9,1... | collective-permute-start | bytes 1572872 | tf_op jit(solution)/shard_map/ppermute | solution.py:393
  168.7 2.3 %collective-permute-start.32 = (f32[512,256]{1,0:T(8,128)S(1)}, f32[512,256]{1,0:T(8,128)S(1)}, u32[]{:S(2)}, u32[]{:S(2)}) collective-permute-start(f32[512,256]{1,0:T(8,128)S(1)} %collective-permute-done.27), channel_id=1, source_target_pairs={{0,4},{4,0},{1,5},{5,1},{2,6},{6,2},{3,7},{7,3},{8,12},{12,8},{9,1... | collective-permute-start | bytes 1572872 | tf_op jit(solution)/shard_map/ppermute | solution.py:393
  168.7 3.0 %collective-permute-start.33 = (f32[512,256]{1,0:T(8,128)S(1)}, f32[512,256]{1,0:T(8,128)S(1)}, u32[]{:S(2)}, u32[]{:S(2)}) collective-permute-start(f32[512,256]{1,0:T(8,128)S(1)} %collective-permute-done.28), channel_id=1, source_target_pairs={{0,4},{4,0},{1,5},{5,1},{2,6},{6,2},{3,7},{7,3},{8,12},{12,8},{9,1... | collective-permute-start | bytes 1572872 | tf_op jit(solution)/shard_map/ppermute | solution.py:393
  (5 other events, 36.5 us)

commit v2 on v1

--- a/solution.py
+++ b/solution.py
@@ -1,3 +1,4 @@
+import functools
 import math
 
 import jax
@@ -197,7 +198,7 @@
     return pl.BlockSpec(memory_space=space)
 
 
-UNROLL = 2
+UNROLL = 4
 
 
 def first_call(where, pieces, probe, amplitude, tables):
@@ -334,32 +335,34 @@
     return out.reshape(1, 2, height * GROUPS, side)
 
 
-def fill_kernel(where_ref, *refs):
-    count = (len(refs) - 2) // 2
-    pieces, out_ref, sems = refs[: 2 * count], refs[-2], refs[-1]
+def fill_kernel(slots, count, where_ref, *refs):
+    pieces, out_ref, sems = refs[:count], refs[-2], refs[-1]
     core, turns = where_ref[1], (where_ref[3], where_ref[4])
+    half = out_ref.shape[0] // 2
     copies = []
-    for n, piece in enumerate(pieces):
-        side, d = n // count, n % count
-        slot = count * (core ^ side) + (turns[side] ^ d)
-        copies.append(pltpu.make_async_copy(piece, out_ref.at[slot], sems.at[n]))
+    for piece, homes in zip(pieces, slots):
+        for i, (side, d, part) in enumerate(homes):
+            target = out_ref.at[half * (core ^ side) + (turns[side] ^ d), part]
+            copies.append(pltpu.make_async_copy(piece.at[i], target, sems.at[len(copies)]))
     for copy in copies:
         copy.start()
     for copy in copies:
         copy.wait()
 
 
-def fill_call(where, pieces, shape):
-    pieces = [piece.reshape(shape[1:]) for piece in pieces]
+def fill_call(where, pieces, slots, shape, base=None):
+    pieces = [piece.reshape(-1, *shape[2:]) for piece in pieces]
+    given = [] if base is None else [base]
     return pl.pallas_call(
-        fill_kernel,
+        functools.partial(fill_kernel, slots, len(pieces)),
         out_shape=jax.ShapeDtypeStruct(shape, F32),
-        in_specs=[whole(pltpu.SMEM)] + [whole()] * len(pieces),
+        in_specs=[whole(pltpu.SMEM)] + [whole()] * len(pieces) + [whole(pl.ANY)] * len(given),
         out_specs=whole(pl.ANY),
-        scratch_shapes=[pltpu.SemaphoreType.DMA((len(pieces),))],
+        scratch_shapes=[pltpu.SemaphoreType.DMA((sum(len(homes) for homes in slots),))],
+        input_output_aliases={1 + len(pieces): 0} if given else {},
         compiler_params=pltpu.CompilerParams(vmem_limit_bytes=VMEM_LIMIT),
         name="fill",
-    )(where, *pieces)
+    )(where, *pieces, *given)
 
 
 TILE_COLS = 4
@@ -378,11 +381,11 @@
     return lax.ppermute(block, TILE_AXES, route)
 
 
-def across_rows(block, step):
+def across_rows(block, step, columns=0):
     route = []
     for t in range(64):
-        u = t + step * TILE_COLS
-        if 0 <= u < 64:
+        u = t + step * TILE_COLS + columns
+        if 0 <= u < 64 and 0 <= t % TILE_COLS + columns < TILE_COLS:
             for k in range(GROUPS):
                 route.append((t * GROUPS + mirrored(t, k), u * GROUPS + mirrored(u, k)))
     return lax.ppermute(block, AXES, route)
@@ -401,8 +404,22 @@
     return lax.ppermute(block, AXES, route)
 
 
+def opposite(block):
+    route = []
+    for y, zh, x, core, zl in np.ndindex(*SIZES):
+        to = (y, 1 - zh, x, core, GROUPS - 1 - zl)
+        route.append((int(np.ravel_multi_index((y, zh, x, core, zl), SIZES)), int(np.ravel_multi_index(to, SIZES))))
+    return lax.ppermute(block, AXES, route)
+
+
 def exchanged(pieces, stage):
     return [exchange(pieces[d], d, stage) for d in (1, 2, 3)]
+
+
+def swapped(blocks):
+    ranks = np.arange(math.prod(SIZES)).reshape(SIZES)
+    groups = [ranks[y, zh, x, core, :: 1 - 2 * zh].tolist() for y, zh, x, core in np.ndindex(*SIZES[:4])]
+    return lax.all_to_all(blocks, AXES, 0, 0, axis_index_groups=groups, tiled=True)
 
 
 def tied(*groups):
@@ -443,13 +460,13 @@
 
     blocks = own_tile.reshape(2, -1, GROUPS, ROW_BLOCK, tile_side)
     class_rows = lax.dynamic_index_in_dim(blocks, row_class, 2, keepdims=False).reshape(2, -1, tile_side)
-    low = across_rows(class_rows[:, : pattern // GROUPS], -1)
+    outside = pattern // GROUPS
+    low = across_rows(class_rows[:, :outside], -1)
+    corner = across_rows(class_rows[:, :outside, :pattern], -1, -1)
     right = across_columns(class_rows[:, :, :pattern], -1)
     right, place_later = tied(right, place)
     spots = [place] + [among(place_later, "zl", d) for d in (1, 2, 3)]
     target = by_parity(amplitude[0, 0])
-    low, spots, target = tied(low, spots, target)
-    corner = across_columns(low[:, :, :pattern], -1)
     rows = list(cut_call(own_class, spots, blocks, right, low, corner))
     rows = rows[:1] + [among(rows[d], "zl", d) for d in (1, 2, 3)]
 
@@ -471,25 +488,33 @@
     pieces = pieces[:1] + exchanged(pieces, 1)
     mine = total_of(pieces).reshape(8, -1, pattern)
 
+    mine = total_of(pieces).reshape(GROUPS, -1, pattern)
     mine, lower = tied(mine, body[:, inside:])
     from_above = across_rows(lower, 1)
-    spread = lax.all_to_all(mine, ("zh", "zl"), 0, 0, tiled=True)
-    mine = jnp.sum(spread, axis=0) * (1.0 / math.sqrt(mesh_size()))
-    body = body[:, :inside].at[:, : pattern // GROUPS].add(from_above)
-
-    spread, body = tied(jnp.broadcast_to(mine[None], (8,) + mine.shape), body)
-    second = among(body, "zl", 2)
-    mine = lax.all_to_all(spread, ("zh", "zl"), 0, 0, tiled=True).reshape(-1, pattern)
-    mine, body, second = tied(mine, body, second)
-    first = among(body, "zl", 1)
-    mine = by_place([mine] + [exchange(mine, d, 1) for d in (1, 2, 3)], next_turn)
-    mine, body, first = tied(mine, body, first)
-    third = among(body, "zl", 3)
-    pieces = exchanged([mine] * 4, 0)
-    other = [among(mine, "core", 1)]
-    pieces, third = tied(pieces, third)
-    other = other + [among(piece, "core", 1) for piece in pieces]
-    return (join_call(own_class, [body, first, second, third]), fill_call(where, [mine, *pieces, *other], probe.shape))
+    mine = jnp.sum(swapped(mine), axis=0)
+    mine = (mine + opposite(mine)) * (1.0 / math.sqrt(mesh_size()))
+    body = body[:, :inside].at[:, :outside].add(from_above)
+
+    mine, body = tied(mine, body)
+    second = among(body[0], "zl", 2)
+    near = [among(mine, "zl", d) for d in (1, 2, 3)]
+    near, second, body = tied(near, second, body)
+    later = among(body[1], "zl", 2)
+    mine = by_place([mine, *near], row_class)
+    near = [exchange(mine, d, 1) for d in (1, 2, 3)]
+    near, later = tied(near, later)
+    second = jnp.stack([second, later])
+    mine = by_place([mine, *near], next_turn)
+    mine, pair = tied(mine, jnp.stack([body, second]))
+    pair = among(pair, "zl", 1)
+    pieces = [mine] + exchanged([mine] * 4, 0)
+    homes = [[((side, d, 0), (side, d, 1)) for side in range(2)] for d in range(4)]
+    *pieces[2:], pair = tied(*pieces[2:], pair)
+    other = [among(piece, "core", 1) for piece in pieces]
+    done = [pieces[0], other[0], pieces[1], other[1], pieces[2], pieces[3]]
+    grad = fill_call(where, done, homes[0] + homes[1] + homes[2][:1] + homes[3][:1], probe.shape)
+    grad = fill_call(where, other[2:], homes[2][1:] + homes[3][1:], probe.shape, grad)
+    return (join_call(own_class, [body, pair[0], second, pair[1]]), grad)
 
 
 def mesh_size():

time: 175 us -> 168 us (0.960)
  starting transfers between devices: 65 us -> 90.8 us
  blocking collectives: 18.9 us -> 0 us
  waiting for transfers between devices: 57.7 us -> 41.9 us
    all_to_all x1 -> x0, blocking collectives: 18.9 us -> none  [shards(): lax.all_to_all(spread, ('zh', 'zl'), 0, 0, tiled=True).reshape(-1, pattern)]
    ppermute x17 -> x20, starting transfers between devices: 18.3 us -> 36.3 us  [among(): return lax.ppermute(block, axis, [(i, i ^ distance) for i in range(n)])]
    all_to_all x1, waiting for transfers between devices: 8.55 us -> 0.01 us  [swapped(): lax.all_to_all(blocks, AXES, 0, 0, axis_index_groups=groups, tiled=True)]
    ppermute x17 -> x20, waiting for transfers between devices: 31.4 us -> 24.4 us  [among(): return lax.ppermute(block, axis, [(i, i ^ distance) for i in range(n)])]
    ppermute x2 -> x3, starting transfers between devices: 2.73 us -> 8.18 us  [across_rows(): return lax.ppermute(block, AXES, route)]
    ppermute x3 -> x2, waiting for transfers between devices: 8.55 us -> 3.45 us  [across_columns(): return lax.ppermute(block, TILE_AXES, route)]
    ppermute x0 -> x1, starting transfers between devices: none -> 3.8 us  [opposite(): return lax.ppermute(block, AXES, route)]
    ppermute x3 -> x2, starting transfers between devices: 14.1 us -> 10.7 us  [across_columns(): return lax.ppermute(block, TILE_AXES, route)]
  transfers between devices with their start and end apart: 35 -> 39, of which waited for: 20 -> 16; matrix products, arithmetic and copies ran while one was open for 2% -> 3% of each run, Pallas kernels for 4% -> 6%
where the time goes in v2:
time: 168 us; the launch traced here: 167 us
  starting transfers between devices  90.8 us (54%)
  waiting for transfers between devices  41.9 us (25%)
  Pallas kernels  23.7 us (14%)
  local copies, waits for them, and re-layouts  4.06 us (2%)
  other arithmetic  3.62 us (2%)
  matrix products  1.81 us (1%)
    ppermute x20, starting transfers between devices, among(): return lax.ppermute(block, axis, [(i, i ^ distance) for i in range(n)])  36.3 us
    ppermute x12, starting transfers between devices, exchange(): return lax.ppermute(block, AXES, route)  27.8 us
    ppermute x20, waiting for transfers between devices, among(): return lax.ppermute(block, axis, [(i, i ^ distance) for i in range(n)])  24.4 us
    pallas_call x1, Pallas kernels, first_call(): pl.pallas_call(first_kernel, out_shape=[jax.ShapeDtypeStruct(s, F32) for...  11.4 us
    ppermute x2, starting transfers between devices, across_columns(): return lax.ppermute(block, TILE_AXES, route)  10.7 us
    ppermute x12, waiting for transfers between devices, exchange(): return lax.ppermute(block, AXES, route)  9.59 us
    ppermute x3, starting transfers between devices, across_rows(): return lax.ppermute(block, AXES, route)  8.18 us
    pallas_call x1, Pallas kernels, second_call(): pl.pallas_call(second_kernel, out_shape=[jax.ShapeDtypeStruct(s, F32) for...  5.21 us
  transfers between devices with their start and end apart: 39, of which 16 were waited for; matrix products, arithmetic and copies ran while one was open for 3% of the time, Pallas kernels for 6%

profile of v2, /device:TPU:1, one launch (start us, length us, event | category | flops | bytes accessed | tf_op | source)
XLA Modules:
  0.0 167.1 jit_solution(15200375113081057484)
XLA Ops:
  2.5 1.4 collective-permute-start.5
  4.6 5.1 %collective-permute-start = (f32[2,96,256]{2,1,0:T(8,128)}, f32[2,96,256]{2,1,0:T(8,128)S(1)}, u32[]{:S(2)}, u32[]{:S(2)}) collective-permute-start(f32[2,96,256]{2,1,0:T(8,128)} %slice.127), channel_id=1, source_target_pairs={{4,0},{8,4},{12,8},{20,16},{24,20},{28,24},{36,32},{40,36},{44,40}... | collective-permute-start | bytes 589832 | tf_op jit(solution)/shard_map/ppermute | solution.py:381
  10.4 1.3 collective-permute-start.4
  12.5 1.4 fusion
  14.0 2.9 %collective-permute-start.3 = (s32[2]{0:T(128)S(1)}, s32[2]{0:T(128)S(1)}, u32[]{:S(2)}, u32[]{:S(2)}) collective-permute-start(s32[2]{0:T(128)S(1)} %bitcast.64), channel_id=1, source_target_pairs={{0,3},{1,2},{2,1},{3,0},{4,7},{5,6},{6,5},{7,4},{8,11},{9,10},{10,... | collective-permute-start | bytes 32 | tf_op jit(solution)/shard_map/ppermute | solution.py:396
  17.6 2.9 %collective-permute-done.4.low_ref = f32[2,64,384]{2,1,0:T(8,128)S(1)} collective-permute-done((f32[2,64,384]{2,1,0:T(8,128)}, f32[2,64,384]{2,1,0:T(8,128)S(1)}, u32[]{:S(2)}, u32[]{:S(2)}) %collective-permute-start.4) | collective-permute-done | bytes 196640 | tf_op jit(solution)/shard_map/ppermute | solution.py:391
  20.5 1.3 cut.1
  21.9 2.9 %collective-permute-start.7 = (f32[2,9,8,256]{3,2,1,0:T(8,128)S(1)}, f32[2,9,8,256]{3,2,1,0:T(8,128)S(1)}, u32[]{:S(2)}, u32[]{:S(2)}) collective-permute-start(f32[2,9,8,256]{3,2,1,0:T(8,128)S(1)} %get-tuple-element.78), channel_id=1, source_target_pairs={{0,2},{1,3},{2,0},{3,1},{4,6},{5,7},{6,4},{7,5},{8,10},{9,11},{10,... | collective-permute-start | bytes 442376 | tf_op jit(solution)/shard_map/ppermute | solution.py:396
  25.9 4.0 %collective-permute-done.6.rows1 = f32[2,9,8,256]{3,2,1,0:T(8,128)S(1)} collective-permute-done((f32[2,9,8,256]{3,2,1,0:T(8,128)S(1)}, f32[2,9,8,256]{3,2,1,0:T(8,128)S(1)}, u32[]{:S(2)}, u32[]{:S(2)}) %collective-permute-start.6) | collective-permute-done | bytes 147488 | tf_op jit(solution)/shard_map/ppermute | solution.py:396
  29.9 4.6 %collective-permute-done.8.rows3 = f32[2,9,8,256]{3,2,1,0:T(8,128)S(1)} collective-permute-done((f32[2,9,8,256]{3,2,1,0:T(8,128)S(1)}, f32[2,9,8,256]{3,2,1,0:T(8,128)S(1)}, u32[]{:S(2)}, u32[]{:S(2)}) %collective-permute-start.8) | collective-permute-done | bytes 147488 | tf_op jit(solution)/shard_map/ppermute | solution.py:396
  34.5 11.4 %outward.1 = (f32[4,2,256,256]{3,2,1,0:T(8,128)S(1)}, f32[4,2,256,256]{3,2,1,0:T(8,128)}, f32[2,256,256]{2,1,0:T(8,128)S(1)}, f32[2,256,256]{2,1,0:T(8,128)S(1)}) custom-call(s32[5]{0:T(128)S(1)} %stack.37.where_ref, f32[2,9,8,256]{3,2,1,0:T(8,128)S(1)} %get-tuple-element.76.rows0, f32[2,9,8,256]{3,2,1,0:T(8,128)S(1)} %collective-permute-done.6.rows1, ...), custom_call_target="tpu_custom_call" | custom-call | tf_op jit(solution)/shard_map/outward/pallas_call | solution.py:208
  45.9 2.2 %collective-permute-start.9 = (f32[4,2,256,256]{3,2,1,0:T(8,128)S(1)}, f32[4,2,256,256]{3,2,1,0:T(8,128)S(1)}, u32[]{:S(2)}, u32[]{:S(2)}) collective-permute-start(f32[4,2,256,256]{3,2,1,0:T(8,128)S(1)} %get-tuple-element.84), channel_id=1, source_target_pairs={{0,4},{4,0},{1,5},{5,1},{2,6},{6,2},{3,7},{7,3},{8,12},{12,8},{9,1... | collective-permute-start | bytes 6291464 | tf_op jit(solution)/shard_map/ppermute | solution.py:396
  48.1 5.2 %homeward.1 = (f32[4,2,256,256]{3,2,1,0:T(8,128)S(1)}, f32[2,9,8,256]{3,2,1,0:T(8,128)S(1)}, f32[2,9,8,256]{3,2,1,0:T(8,128)S(1)}, f32[2,9,8,256]{3,2,1,0:T(8,128)S(1)}, f32[2,9,8,256]{3,2,1,0:T(8,128)S(1)}) custom-call(s32[5]{0:T(128)S(1)} %stack.37.where_ref, f32[4,2,256,256]{3,2,1,0:T(8,128)} %get-tuple-element.80.corrected_ref, ...), custom_call_target="tpu_custom_call" | custom-call | tf_op jit(solution)/shard_map/homeward/pallas_call | solution.py:229
  54.4 8.8 %collective-permute-start.10 = (f32[512,256]{1,0:T(8,128)}, f32[512,256]{1,0:T(8,128)}, u32[]{:S(2)}, u32[]{:S(2)}) collective-permute-start(f32[512,256]{1,0:T(8,128)} %bitcast.10), channel_id=1, source_target_pairs={{0,8},{1,9},{2,10},{3,11},{4,68},{5,69},{6,70},{7,71},{8,0},{9,1},... | collective-permute-start | bytes 1572872 | tf_op jit(solution)/shard_map/ppermute | solution.py:404
  63.2 2.9 %collective-permute-start.11 = (f32[512,256]{1,0:T(8,128)S(1)}, f32[512,256]{1,0:T(8,128)}, u32[]{:S(2)}, u32[]{:S(2)}) collective-permute-start(f32[512,256]{1,0:T(8,128)S(1)} %bitcast.73), channel_id=1, source_target_pairs={{0,16},{1,17},{2,18},{3,19},{4,132},{5,133},{6,134},{7,135},{8,24}... | collective-permute-start | bytes 1572872 | tf_op jit(solution)/shard_map/ppermute | solution.py:404
  66.1 2.3 %collective-permute-start.13 = (f32[2,9,8,256]{3,2,1,0:T(8,128)S(1)}, f32[2,9,8,256]{3,2,1,0:T(8,128)S(1)}, u32[]{:S(2)}, u32[]{:S(2)}) collective-permute-start(f32[2,9,8,256]{3,2,1,0:T(8,128)S(1)} %get-tuple-element.94), channel_id=1, source_target_pairs={{0,1},{1,0},{2,3},{3,2},{4,5},{5,4},{6,7},{7,6},{8,9},{9,8},{10,11... | collective-permute-start | bytes 442376 | tf_op jit(solution)/shard_map/ppermute | solution.py:396
  68.9 3.0 %collective-permute-done.13.rows1 = f32[2,9,8,256]{3,2,1,0:T(8,128)S(1)} collective-permute-done((f32[2,9,8,256]{3,2,1,0:T(8,128)S(1)}, f32[2,9,8,256]{3,2,1,0:T(8,128)S(1)}, u32[]{:S(2)}, u32[]{:S(2)}) %collective-permute-start.13) | collective-permute-done | bytes 147488 | tf_op jit(solution)/shard_map/ppermute | solution.py:396
  72.6 3.3 %collective-permute-done.14.rows2 = f32[2,9,8,256]{3,2,1,0:T(8,128)S(1)} collective-permute-done((f32[2,9,8,256]{3,2,1,0:T(8,128)S(1)}, f32[2,9,8,256]{3,2,1,0:T(8,128)S(1)}, u32[]{:S(2)}, u32[]{:S(2)}) %collective-permute-start.14) | collective-permute-done | bytes 147488 | tf_op jit(solution)/shard_map/ppermute | solution.py:396
  75.9 3.5 %collective-permute-done.15.rows3 = f32[2,9,8,256]{3,2,1,0:T(8,128)S(1)} collective-permute-done((f32[2,9,8,256]{3,2,1,0:T(8,128)S(1)}, f32[2,9,8,256]{3,2,1,0:T(8,128)S(1)}, u32[]{:S(2)}, u32[]{:S(2)}) %collective-permute-start.15) | collective-permute-done | bytes 147488 | tf_op jit(solution)/shard_map/ppermute | solution.py:396
  80.2 1.2 collective-permute-done.12
  81.4 1.5 add_add_fusion
  83.0 2.4 %collective-permute-start.16 = (f32[128,256]{1,0:T(8,128)S(1)}, f32[128,256]{1,0:T(8,128)S(1)}, u32[]{:S(2)}, u32[]{:S(2)}) collective-permute-start(f32[128,256]{1,0:T(8,128)S(1)} %get-tuple-element.99), channel_id=1, source_target_pairs={{0,64},{1,65},{2,66},{3,67},{4,12},{5,13},{6,14},{7,15},{8,72},{9,... | collective-permute-start | bytes 393224 | tf_op jit(solution)/shard_map/ppermute | solution.py:404
  85.4 2.3 %collective-permute-start.17 = (f32[128,256]{1,0:T(8,128)S(1)}, f32[128,256]{1,0:T(8,128)S(1)}, u32[]{:S(2)}, u32[]{:S(2)}) collective-permute-start(f32[128,256]{1,0:T(8,128)S(1)} %get-tuple-element.100), channel_id=1, source_target_pairs={{0,128},{1,129},{2,130},{3,131},{4,20},{5,21},{6,22},{7,23},{8,136... | collective-permute-start | bytes 393224 | tf_op jit(solution)/shard_map/ppermute | solution.py:404
  87.9 5.5 %collective-permute-start.19 = (f32[2,160,256]{2,1,0:T(8,128)S(1)}, f32[2,160,256]{2,1,0:T(8,128)S(1)}, u32[]{:S(2)}, u32[]{:S(2)}) collective-permute-start(f32[2,160,256]{2,1,0:T(8,128)S(1)} %get-tuple-element.103), channel_id=1, source_target_pairs={{0,4},{4,8},{8,12},{16,20},{20,24},{24,28},{32,36},{36,40},{40,44}... | collective-permute-start | bytes 983048 | tf_op jit(solution)/shard_map/ppermute | solution.py:381
  94.1 3.3 %collective-permute-done.19 = f32[2,160,256]{2,1,0:T(8,128)S(1)} collective-permute-done((f32[2,160,256]{2,1,0:T(8,128)S(1)}, f32[2,160,256]{2,1,0:T(8,128)S(1)}, u32[]{:S(2)}, u32[]{:S(2)}) %collective-permute-start.19) | collective-permute-done | bytes 327712 | tf_op jit(solution)/shard_map/ppermute | solution.py:381
  97.5 4.0 %all-to-all-start = ((f32[4,32,256]{2,1,0:T(8,128)}), f32[4,32,256]{2,1,0:T(8,128)S(1)}, u32[]{:S(2)}, u32[]{:S(2)}) async-start(f32[4,32,256]{2,1,0:T(8,128)} %bitcast.18), calls=%async_computation | async-start | bytes 262144 | tf_op jit(solution)/shard_map/all_to_all | solution.py:422
  101.5 5.5 %collective-permute-start.21 = (f32[2,64,384]{2,1,0:T(8,128)S(1)}, f32[2,64,384]{2,1,0:T(8,128)S(1)}, u32[]{:S(2)}, u32[]{:S(2)}) collective-permute-start(f32[2,64,384]{2,1,0:T(8,128)S(1)} %slice.134), channel_id=1, source_target_pairs={{0,16},{1,17},{2,18},{3,19},{4,20},{5,21},{6,22},{7,23},{8,24},{9,... | collective-permute-start | bytes 589832 | tf_op jit(solution)/shard_map/ppermute | solution.py:391
  107.0 3.8 %collective-permute-start.20 = (f32[32,256]{1,0:T(8,128)S(1)}, f32[32,256]{1,0:T(8,128)S(1)}, u32[]{:S(2)}, u32[]{:S(2)}) collective-permute-start(f32[32,256]{1,0:T(8,128)S(1)} %reduce_sum.9), channel_id=1, source_target_pairs={{0,35},{1,34},{2,33},{3,32},{4,39},{5,38},{6,37},{7,36},{8,43},{9,... | collective-permute-start | bytes 98312 | tf_op jit(solution)/shard_map/ppermute | solution.py:412
  110.9 1.6 collective-permute-done.20
  112.5 3.0 %collective-permute-start.25 = (f32[96,384]{1,0:T(8,128)S(1)}, f32[96,384]{1,0:T(8,128)S(1)}, u32[]{:S(2)}, u32[]{:S(2)}) collective-permute-start(f32[96,384]{1,0:T(8,128)S(1)} %slice_bitcast_fusion.3), channel_id=1, source_target_pairs={{0,2},{1,3},{2,0},{3,1},{4,6},{5,7},{6,4},{7,5},{8,10},{9,11},{10,... | collective-permute-start | bytes 442376 | tf_op jit(solution)/shard_map/ppermute | solution.py:396
  115.6 1.3 collective-permute-start.24
  117.4 1.7 %collective-permute-start.22 = (f32[32,256]{1,0:T(8,128)S(1)}, f32[32,256]{1,0:T(8,128)S(1)}, u32[]{:S(2)}, u32[]{:S(2)}) collective-permute-start(f32[32,256]{1,0:T(8,128)S(1)} %add_multiply_fusion), channel_id=1, source_target_pairs={{0,1},{1,0},{2,3},{3,2},{4,5},{5,4},{6,7},{7,6},{8,9},{9,8},{10,11... | collective-permute-start | bytes 98312 | tf_op jit(solution)/shard_map/ppermute | solution.py:396
  119.1 1.4 collective-permute-done.24
  120.5 4.7 %collective-permute-done.23 = f32[32,256]{1,0:T(8,128)S(1)} collective-permute-done((f32[32,256]{1,0:T(8,128)S(1)}, f32[32,256]{1,0:T(8,128)S(1)}, u32[]{:S(2)}, u32[]{:S(2)}) %collective-permute-start.23) | collective-permute-done | bytes 32800 | tf_op jit(solution)/shard_map/ppermute | solution.py:396
  125.2 1.8 %collective-permute-start.29 = (f32[96,384]{1,0:T(8,128)S(1)}, f32[96,384]{1,0:T(8,128)S(1)}, u32[]{:S(2)}, u32[]{:S(2)}) collective-permute-start(f32[96,384]{1,0:T(8,128)S(1)} %slice_bitcast_fusion.2), channel_id=1, source_target_pairs={{0,2},{1,3},{2,0},{3,1},{4,6},{5,7},{6,4},{7,5},{8,10},{9,11},{10,... | collective-permute-start | bytes 442376 | tf_op jit(solution)/shard_map/ppermute | solution.py:396
  127.3 5.2 %collective-permute-start.27 = (f32[128,256]{1,0:T(8,128)S(1)}, f32[128,256]{1,0:T(8,128)S(1)}, u32[]{:S(2)}, u32[]{:S(2)}) collective-permute-start(f32[128,256]{1,0:T(8,128)S(1)} %pad_maximum_fusion.3), channel_id=1, source_target_pairs={{0,128},{1,129},{2,130},{3,131},{4,20},{5,21},{6,22},{7,23},{8,136... | collective-permute-start | bytes 393224 | tf_op jit(solution)/shard_map/ppermute | solution.py:404
  132.5 2.4 %collective-permute-done.27 = f32[128,256]{1,0:T(8,128)S(1)} collective-permute-done((f32[128,256]{1,0:T(8,128)S(1)}, f32[128,256]{1,0:T(8,128)S(1)}, u32[]{:S(2)}, u32[]{:S(2)}) %collective-permute-start.27) | collective-permute-done | bytes 131104 | tf_op jit(solution)/shard_map/ppermute | solution.py:404
  134.9 1.5 collective-permute-done.26
  136.6 1.3 collective-permute-start.32
  137.9 3.9 %collective-permute-start.36 = (f32[512,256]{1,0:T(8,128)S(1)}, f32[512,256]{1,0:T(8,128)S(1)}, u32[]{:S(2)}, u32[]{:S(2)}) collective-permute-start(f32[512,256]{1,0:T(8,128)S(1)} %pad_maximum_fusion.1), channel_id=1, source_target_pairs={{0,8},{1,9},{2,10},{3,11},{4,68},{5,69},{6,70},{7,71},{8,0},{9,1},... | collective-permute-start | bytes 1572872 | tf_op jit(solution)/shard_map/ppermute | solution.py:404
  141.8 1.4 collective-permute-start.31
  143.6 4.5 %collective-permute-start.35 = (f32[512,256]{1,0:T(8,128)S(1)}, f32[512,256]{1,0:T(8,128)S(1)}, u32[]{:S(2)}, u32[]{:S(2)}) collective-permute-start(f32[512,256]{1,0:T(8,128)S(1)} %pad_maximum_fusion.1), channel_id=1, source_target_pairs={{0,4},{4,0},{1,5},{5,1},{2,6},{6,2},{3,7},{7,3},{8,12},{12,8},{9,1... | collective-permute-start | bytes 1572872 | tf_op jit(solution)/shard_map/ppermute | solution.py:396
  148.7 4.3 %collective-permute-start.37 = (f32[512,256]{1,0:T(8,128)S(1)}, f32[512,256]{1,0:T(8,128)S(1)}, u32[]{:S(2)}, u32[]{:S(2)}) collective-permute-start(f32[512,256]{1,0:T(8,128)S(1)} %collective-permute-done.36), channel_id=1, source_target_pairs={{0,4},{4,0},{1,5},{5,1},{2,6},{6,2},{3,7},{7,3},{8,12},{12,8},{9,1... | collective-permute-start | bytes 1572872 | tf_op jit(solution)/shard_map/ppermute | solution.py:396
  153.0 4.0 %collective-permute-done.31 = f32[512,256]{1,0:T(8,128)S(1)} collective-permute-done((f32[512,256]{1,0:T(8,128)S(1)}, f32[512,256]{1,0:T(8,128)S(1)}, u32[]{:S(2)}, u32[]{:S(2)}) %collective-permute-start.31) | collective-permute-done | bytes 524320 | tf_op jit(solution)/shard_map/ppermute | solution.py:404
  157.0 4.9 %collective-permute-start.33 = (f32[512,256]{1,0:T(8,128)S(1)}, f32[512,256]{1,0:T(8,128)S(1)}, u32[]{:S(2)}, u32[]{:S(2)}) collective-permute-start(f32[512,256]{1,0:T(8,128)S(1)} %collective-permute-done.30), channel_id=1, source_target_pairs={{0,4},{4,0},{1,5},{5,1},{2,6},{6,2},{3,7},{7,3},{8,12},{12,8},{9,1... | collective-permute-start | bytes 1572872 | tf_op jit(solution)/shard_map/ppermute | solution.py:396
  162.0 1.1 join.1
  163.1 2.3 %fill.2.refs_2_ = f32[8,2,256,256]{3,2,1,0:T(8,128)} custom-call(s32[5]{0:T(128)S(1)} %stack.37.where_ref, f32[2,256,256]{2,1,0:T(8,128)S(1)} %bitcast.53, f32[2,256,256]{2,1,0:T(8,128)S(1)} %bitcast.61, f32[2,256,256]{2,1,0:T(8,128)S(1)} %bitcast.59, f32[2,256,256]{2,1,0:T(8,128)S(1)} %bitcast.62, f32[2,256,256]{2,1,0:T(8,128)S(1)} %bitcast.60, ...), custom_call_target="tpu_custom_call" | custom-call | tf_op jit(solution)/shard_map/fill/pallas_call | solution.py:356
  165.4 1.5 fill.3
  (92 shorter events, 12.3 us)
Async XLA Ops:
  0.6 19.9 %copy-start.1 = (f32[1,2,384,384]{3,2,1,0:T(8,128)S(1)}, f32[1,2,384,384]{3,2,1,0:T(8,128)}, u32[]{:S(2)}) copy-start(f32[1,2,384,384]{3,2,1,0:T(8,128)} %param.15) | copy-start | bytes 3538948
  2.4 32.0 %copy-start.2 = (bf16[768,256]{1,0:T(8,128)(2,1)S(1)}, bf16[768,256]{1,0:T(8,128)(2,1)}, u32[]{:S(2)}) copy-start(bf16[768,256]{1,0:T(8,128)(2,1)} %constant.145.clone.down_t) | copy-start | bytes 1179652
  2.4 32.0 %copy-start.3 = (bf16[256,768]{1,0:T(8,128)(2,1)S(1)}, bf16[256,768]{1,0:T(8,128)(2,1)}, u32[]{:S(2)}) copy-start(bf16[256,768]{1,0:T(8,128)(2,1)} %constant.144.clone.across) | copy-start | bytes 1179652
  2.4 32.0 %copy-start.4 = (f32[2,128,128]{2,1,0:T(8,128)S(1)}, f32[2,128,128]{2,1,0:T(8,128)}, u32[]{:S(2)}) copy-start(f32[2,128,128]{2,1,0:T(8,128)} %constant.148.clone.rows_ref) | copy-start | bytes 393220
  2.4 32.0 %copy-start.5 = (bf16[256,768]{1,0:T(8,128)(2,1)S(1)}, bf16[256,768]{1,0:T(8,128)(2,1)}, u32[]{:S(2)}) copy-start(bf16[256,768]{1,0:T(8,128)(2,1)} %constant.146.clone.across_t) | copy-start | bytes 1179652
  2.4 32.0 %copy-start.6 = (bf16[768,256]{1,0:T(8,128)(2,1)S(1)}, bf16[768,256]{1,0:T(8,128)(2,1)}, u32[]{:S(2)}) copy-start(bf16[768,256]{1,0:T(8,128)(2,1)} %constant.143.clone.down) | copy-start | bytes 1179652
  2.4 32.0 %copy-start.8 = (f32[2,1,128]{2,1,0:T(1,128)S(1)}, f32[2,1,128]{2,1,0:T(1,128)}, u32[]{:S(2)}) copy-start(f32[2,1,128]{2,1,0:T(1,128)} %constant.147.clone.lanes_ref) | copy-start | bytes 3076
  2.5 15.1 %collective-permute-start.5 = (f32[2,64,256]{2,1,0:T(8,128)}, f32[2,64,256]{2,1,0:T(8,128)}, u32[]{:S(2)}, u32[]{:S(2)}) collective-permute-start(f32[2,64,256]{2,1,0:T(8,128)} %slice.129), channel_id=1, source_target_pairs={{20,0},{21,1},{22,2},{23,3},{24,4},{25,5},{26,6},{27,7},{28,8},{29... | collective-permute-start | bytes 393224 | tf_op jit(solution)/shard_map/ppermute | solution.py:391
  4.6 9.5 %collective-permute-start = (f32[2,96,256]{2,1,0:T(8,128)}, f32[2,96,256]{2,1,0:T(8,128)S(1)}, u32[]{:S(2)}, u32[]{:S(2)}) collective-permute-start(f32[2,96,256]{2,1,0:T(8,128)} %slice.127), channel_id=1, source_target_pairs={{4,0},{8,4},{12,8},{20,16},{24,20},{28,24},{36,32},{40,36},{44,40}... | collective-permute-start | bytes 589832 | tf_op jit(solution)/shard_map/ppermute | solution.py:381
  10.4 10.1 %collective-permute-start.4 = (f32[2,64,384]{2,1,0:T(8,128)}, f32[2,64,384]{2,1,0:T(8,128)S(1)}, u32[]{:S(2)}, u32[]{:S(2)}) collective-permute-start(f32[2,64,384]{2,1,0:T(8,128)} %slice.128), channel_id=1, source_target_pairs={{16,0},{17,1},{18,2},{19,3},{20,4},{21,5},{22,6},{23,7},{24,8},{25... | collective-permute-start | bytes 589832 | tf_op jit(solution)/shard_map/ppermute | solution.py:391
  14.0 6.4 %collective-permute-start.3 = (s32[2]{0:T(128)S(1)}, s32[2]{0:T(128)S(1)}, u32[]{:S(2)}, u32[]{:S(2)}) collective-permute-start(s32[2]{0:T(128)S(1)} %bitcast.64), channel_id=1, source_target_pairs={{0,3},{1,2},{2,1},{3,0},{4,7},{5,6},{6,5},{7,4},{8,11},{9,10},{10,... | collective-permute-start | bytes 32 | tf_op jit(solution)/shard_map/ppermute | solution.py:396
  17.0 3.5 %collective-permute-start.2 = (s32[2]{0:T(128)S(1)}, s32[2]{0:T(128)S(1)}, u32[]{:S(2)}, u32[]{:S(2)}) collective-permute-start(s32[2]{0:T(128)S(1)} %bitcast.65), channel_id=1, source_target_pairs={{0,2},{1,3},{2,0},{3,1},{4,6},{5,7},{6,4},{7,5},{8,10},{9,11},{10,... | collective-permute-start | bytes 32 | tf_op jit(solution)/shard_map/ppermute | solution.py:396
  17.0 3.5 %collective-permute-start.1 = (s32[2]{0:T(128)S(1)}, s32[2]{0:T(128)S(1)}, u32[]{:S(2)}, u32[]{:S(2)}) collective-permute-start(s32[2]{0:T(128)S(1)} %bitcast.66), channel_id=1, source_target_pairs={{0,1},{1,0},{2,3},{3,2},{4,5},{5,4},{6,7},{7,6},{8,9},{9,8},{10,11... | collective-permute-start | bytes 32 | tf_op jit(solution)/shard_map/ppermute | solution.py:396
  21.8 8.0 %collective-permute-start.6 = (f32[2,9,8,256]{3,2,1,0:T(8,128)S(1)}, f32[2,9,8,256]{3,2,1,0:T(8,128)S(1)}, u32[]{:S(2)}, u32[]{:S(2)}) collective-permute-start(f32[2,9,8,256]{3,2,1,0:T(8,128)S(1)} %get-tuple-element.77), channel_id=1, source_target_pairs={{0,1},{1,0},{2,3},{3,2},{4,5},{5,4},{6,7},{7,6},{8,9},{9,8},{10,11... | collective-permute-start | bytes 442376 | tf_op jit(solution)/shard_map/ppermute | solution.py:396
  21.9 7.9 %collective-permute-start.7 = (f32[2,9,8,256]{3,2,1,0:T(8,128)S(1)}, f32[2,9,8,256]{3,2,1,0:T(8,128)S(1)}, u32[]{:S(2)}, u32[]{:S(2)}) collective-permute-start(f32[2,9,8,256]{3,2,1,0:T(8,128)S(1)} %get-tuple-element.78), channel_id=1, source_target_pairs={{0,2},{1,3},{2,0},{3,1},{4,6},{5,7},{6,4},{7,5},{8,10},{9,11},{10,... | collective-permute-start | bytes 442376 | tf_op jit(solution)/shard_map/ppermute | solution.py:396
  24.8 9.6 %collective-permute-start.8 = (f32[2,9,8,256]{3,2,1,0:T(8,128)S(1)}, f32[2,9,8,256]{3,2,1,0:T(8,128)S(1)}, u32[]{:S(2)}, u32[]{:S(2)}) collective-permute-start(f32[2,9,8,256]{3,2,1,0:T(8,128)S(1)} %get-tuple-element.79), channel_id=1, source_target_pairs={{0,3},{1,2},{2,1},{3,0},{4,7},{5,6},{6,5},{7,4},{8,11},{9,10},{10,... | collective-permute-start | bytes 442376 | tf_op jit(solution)/shard_map/ppermute | solution.py:396
  45.9 7.4 %collective-permute-start.9 = (f32[4,2,256,256]{3,2,1,0:T(8,128)S(1)}, f32[4,2,256,256]{3,2,1,0:T(8,128)S(1)}, u32[]{:S(2)}, u32[]{:S(2)}) collective-permute-start(f32[4,2,256,256]{3,2,1,0:T(8,128)S(1)} %get-tuple-element.84), channel_id=1, source_target_pairs={{0,4},{4,0},{1,5},{5,1},{2,6},{6,2},{3,7},{7,3},{8,12},{12,8},{9,1... | collective-permute-start | bytes 6291464 | tf_op jit(solution)/shard_map/ppermute | solution.py:396
  53.3 26.0 %copy-start.10 = (s32[2]{0:T(128)S(1)}, s32[2]{0:T(128)}, u32[]{:S(2)}) copy-start(s32[2]{0:T(128)} %copy-done.9) | copy-start | bytes 28
  53.3 26.0 %copy-start.12 = (s32[2]{0:T(128)S(1)}, s32[2]{0:T(128)}, u32[]{:S(2)}) copy-start(s32[2]{0:T(128)} %copy-done.11) | copy-start | bytes 28
  54.4 25.8 %collective-permute-start.10 = (f32[512,256]{1,0:T(8,128)}, f32[512,256]{1,0:T(8,128)}, u32[]{:S(2)}, u32[]{:S(2)}) collective-permute-start(f32[512,256]{1,0:T(8,128)} %bitcast.10), channel_id=1, source_target_pairs={{0,8},{1,9},{2,10},{3,11},{4,68},{5,69},{6,70},{7,71},{8,0},{9,1},... | collective-permute-start | bytes 1572872 | tf_op jit(solution)/shard_map/ppermute | solution.py:404
  63.2 17.0 %collective-permute-start.11 = (f32[512,256]{1,0:T(8,128)S(1)}, f32[512,256]{1,0:T(8,128)}, u32[]{:S(2)}, u32[]{:S(2)}) collective-permute-start(f32[512,256]{1,0:T(8,128)S(1)} %bitcast.73), channel_id=1, source_target_pairs={{0,16},{1,17},{2,18},{3,19},{4,132},{5,133},{6,134},{7,135},{8,24}... | collective-permute-start | bytes 1572872 | tf_op jit(solution)/shard_map/ppermute | solution.py:404
  66.1 15.3 %collective-permute-start.12 = (f32[512,256]{1,0:T(8,128)S(1)}, f32[512,256]{1,0:T(8,128)}, u32[]{:S(2)}, u32[]{:S(2)}) collective-permute-start(f32[512,256]{1,0:T(8,128)S(1)} %bitcast.72), channel_id=1, source_target_pairs={{0,24},{1,25},{2,26},{3,27},{4,196},{5,197},{6,198},{7,199},{8,16}... | collective-permute-start | bytes 1572872 | tf_op jit(solution)/shard_map/ppermute | solution.py:404
  66.1 5.8 %collective-permute-start.13 = (f32[2,9,8,256]{3,2,1,0:T(8,128)S(1)}, f32[2,9,8,256]{3,2,1,0:T(8,128)S(1)}, u32[]{:S(2)}, u32[]{:S(2)}) collective-permute-start(f32[2,9,8,256]{3,2,1,0:T(8,128)S(1)} %get-tuple-element.94), channel_id=1, source_target_pairs={{0,1},{1,0},{2,3},{3,2},{4,5},{5,4},{6,7},{7,6},{8,9},{9,8},{10,11... | collective-permute-start | bytes 442376 | tf_op jit(solution)/shard_map/ppermute | solution.py:396
  68.5 7.4 %collective-permute-start.14 = (f32[2,9,8,256]{3,2,1,0:T(8,128)S(1)}, f32[2,9,8,256]{3,2,1,0:T(8,128)S(1)}, u32[]{:S(2)}, u32[]{:S(2)}) collective-permute-start(f32[2,9,8,256]{3,2,1,0:T(8,128)S(1)} %get-tuple-element.95), channel_id=1, source_target_pairs={{0,2},{1,3},{2,0},{3,1},{4,6},{5,7},{6,4},{7,5},{8,10},{9,11},{10,... | collective-permute-start | bytes 442376 | tf_op jit(solution)/shard_map/ppermute | solution.py:396
  71.9 7.4 %collective-permute-start.15 = (f32[2,9,8,256]{3,2,1,0:T(8,128)S(1)}, f32[2,9,8,256]{3,2,1,0:T(8,128)S(1)}, u32[]{:S(2)}, u32[]{:S(2)}) collective-permute-start(f32[2,9,8,256]{3,2,1,0:T(8,128)S(1)} %get-tuple-element.96), channel_id=1, source_target_pairs={{0,3},{1,2},{2,1},{3,0},{4,7},{5,6},{6,5},{7,4},{8,11},{9,10},{10,... | collective-permute-start | bytes 442376 | tf_op jit(solution)/shard_map/ppermute | solution.py:396
  83.0 10.4 %collective-permute-start.16 = (f32[128,256]{1,0:T(8,128)S(1)}, f32[128,256]{1,0:T(8,128)S(1)}, u32[]{:S(2)}, u32[]{:S(2)}) collective-permute-start(f32[128,256]{1,0:T(8,128)S(1)} %get-tuple-element.99), channel_id=1, source_target_pairs={{0,64},{1,65},{2,66},{3,67},{4,12},{5,13},{6,14},{7,15},{8,72},{9,... | collective-permute-start | bytes 393224 | tf_op jit(solution)/shard_map/ppermute | solution.py:404
  85.4 8.0 %collective-permute-start.17 = (f32[128,256]{1,0:T(8,128)S(1)}, f32[128,256]{1,0:T(8,128)S(1)}, u32[]{:S(2)}, u32[]{:S(2)}) collective-permute-start(f32[128,256]{1,0:T(8,128)S(1)} %get-tuple-element.100), channel_id=1, source_target_pairs={{0,128},{1,129},{2,130},{3,131},{4,20},{5,21},{6,22},{7,23},{8,136... | collective-permute-start | bytes 393224 | tf_op jit(solution)/shard_map/ppermute | solution.py:404
  87.6 5.8 %collective-permute-start.18 = (f32[128,256]{1,0:T(8,128)S(1)}, f32[128,256]{1,0:T(8,128)S(1)}, u32[]{:S(2)}, u32[]{:S(2)}) collective-permute-start(f32[128,256]{1,0:T(8,128)S(1)} %get-tuple-element.101), channel_id=1, source_target_pairs={{0,192},{1,193},{2,194},{3,195},{4,28},{5,29},{6,30},{7,31},{8,200... | collective-permute-start | bytes 393224 | tf_op jit(solution)/shard_map/ppermute | solution.py:404
  87.9 9.5 %collective-permute-start.19 = (f32[2,160,256]{2,1,0:T(8,128)S(1)}, f32[2,160,256]{2,1,0:T(8,128)S(1)}, u32[]{:S(2)}, u32[]{:S(2)}) collective-permute-start(f32[2,160,256]{2,1,0:T(8,128)S(1)} %get-tuple-element.103), channel_id=1, source_target_pairs={{0,4},{4,8},{8,12},{16,20},{20,24},{24,28},{32,36},{36,40},{40,44}... | collective-permute-start | bytes 983048 | tf_op jit(solution)/shard_map/ppermute | solution.py:381
  97.5 9.5 %all-to-all-start = ((f32[4,32,256]{2,1,0:T(8,128)}), f32[4,32,256]{2,1,0:T(8,128)S(1)}, u32[]{:S(2)}, u32[]{:S(2)}) async-start(f32[4,32,256]{2,1,0:T(8,128)} %bitcast.18), calls=%async_computation | async-start | bytes 262144 | tf_op jit(solution)/shard_map/all_to_all | solution.py:422
  101.5 9.3 %collective-permute-start.21 = (f32[2,64,384]{2,1,0:T(8,128)S(1)}, f32[2,64,384]{2,1,0:T(8,128)S(1)}, u32[]{:S(2)}, u32[]{:S(2)}) collective-permute-start(f32[2,64,384]{2,1,0:T(8,128)S(1)} %slice.134), channel_id=1, source_target_pairs={{0,16},{1,17},{2,18},{3,19},{4,20},{5,21},{6,22},{7,23},{8,24},{9,... | collective-permute-start | bytes 589832 | tf_op jit(solution)/shard_map/ppermute | solution.py:391
  107.0 5.4 %collective-permute-start.20 = (f32[32,256]{1,0:T(8,128)S(1)}, f32[32,256]{1,0:T(8,128)S(1)}, u32[]{:S(2)}, u32[]{:S(2)}) collective-permute-start(f32[32,256]{1,0:T(8,128)S(1)} %reduce_sum.9), channel_id=1, source_target_pairs={{0,35},{1,34},{2,33},{3,32},{4,39},{5,38},{6,37},{7,36},{8,43},{9,... | collective-permute-start | bytes 98312 | tf_op jit(solution)/shard_map/ppermute | solution.py:412
  112.5 12.6 %collective-permute-start.25 = (f32[96,384]{1,0:T(8,128)S(1)}, f32[96,384]{1,0:T(8,128)S(1)}, u32[]{:S(2)}, u32[]{:S(2)}) collective-permute-start(f32[96,384]{1,0:T(8,128)S(1)} %slice_bitcast_fusion.3), channel_id=1, source_target_pairs={{0,2},{1,3},{2,0},{3,1},{4,6},{5,7},{6,4},{7,5},{8,10},{9,11},{10,... | collective-permute-start | bytes 442376 | tf_op jit(solution)/shard_map/ppermute | solution.py:396
  115.6 4.9 %collective-permute-start.24 = (f32[32,256]{1,0:T(8,128)S(1)}, f32[32,256]{1,0:T(8,128)S(1)}, u32[]{:S(2)}, u32[]{:S(2)}) collective-permute-start(f32[32,256]{1,0:T(8,128)S(1)} %add_multiply_fusion), channel_id=1, source_target_pairs={{0,3},{1,2},{2,1},{3,0},{4,7},{5,6},{6,5},{7,4},{8,11},{9,10},{10,... | collective-permute-start | bytes 98312 | tf_op jit(solution)/shard_map/ppermute | solution.py:396
  116.9 8.3 %collective-permute-start.23 = (f32[32,256]{1,0:T(8,128)S(1)}, f32[32,256]{1,0:T(8,128)S(1)}, u32[]{:S(2)}, u32[]{:S(2)}) collective-permute-start(f32[32,256]{1,0:T(8,128)S(1)} %add_multiply_fusion), channel_id=1, source_target_pairs={{0,2},{1,3},{2,0},{3,1},{4,6},{5,7},{6,4},{7,5},{8,10},{9,11},{10,... | collective-permute-start | bytes 98312 | tf_op jit(solution)/shard_map/ppermute | solution.py:396
  117.4 7.8 %collective-permute-start.22 = (f32[32,256]{1,0:T(8,128)S(1)}, f32[32,256]{1,0:T(8,128)S(1)}, u32[]{:S(2)}, u32[]{:S(2)}) collective-permute-start(f32[32,256]{1,0:T(8,128)S(1)} %add_multiply_fusion), channel_id=1, source_target_pairs={{0,1},{1,0},{2,3},{3,2},{4,5},{5,4},{6,7},{7,6},{8,9},{9,8},{10,11... | collective-permute-start | bytes 98312 | tf_op jit(solution)/shard_map/ppermute | solution.py:396
  125.2 11.2 %collective-permute-start.29 = (f32[96,384]{1,0:T(8,128)S(1)}, f32[96,384]{1,0:T(8,128)S(1)}, u32[]{:S(2)}, u32[]{:S(2)}) collective-permute-start(f32[96,384]{1,0:T(8,128)S(1)} %slice_bitcast_fusion.2), channel_id=1, source_target_pairs={{0,2},{1,3},{2,0},{3,1},{4,6},{5,7},{6,4},{7,5},{8,10},{9,11},{10,... | collective-permute-start | bytes 442376 | tf_op jit(solution)/shard_map/ppermute | solution.py:396
  127.0 5.5 %collective-permute-start.28 = (f32[128,256]{1,0:T(8,128)S(1)}, f32[128,256]{1,0:T(8,128)S(1)}, u32[]{:S(2)}, u32[]{:S(2)}) collective-permute-start(f32[128,256]{1,0:T(8,128)S(1)} %pad_maximum_fusion.3), channel_id=1, source_target_pairs={{0,192},{1,193},{2,194},{3,195},{4,28},{5,29},{6,30},{7,31},{8,200... | collective-permute-start | bytes 393224 | tf_op jit(solution)/shard_map/ppermute | solution.py:404
  127.3 7.6 %collective-permute-start.27 = (f32[128,256]{1,0:T(8,128)S(1)}, f32[128,256]{1,0:T(8,128)S(1)}, u32[]{:S(2)}, u32[]{:S(2)}) collective-permute-start(f32[128,256]{1,0:T(8,128)S(1)} %pad_maximum_fusion.3), channel_id=1, source_target_pairs={{0,128},{1,129},{2,130},{3,131},{4,20},{5,21},{6,22},{7,23},{8,136... | collective-permute-start | bytes 393224 | tf_op jit(solution)/shard_map/ppermute | solution.py:404
  132.5 3.8 %collective-permute-start.26 = (f32[128,256]{1,0:T(8,128)S(1)}, f32[128,256]{1,0:T(8,128)S(1)}, u32[]{:S(2)}, u32[]{:S(2)}) collective-permute-start(f32[128,256]{1,0:T(8,128)S(1)} %pad_maximum_fusion.3), channel_id=1, source_target_pairs={{0,64},{1,65},{2,66},{3,67},{4,12},{5,13},{6,14},{7,15},{8,72},{9,... | collective-permute-start | bytes 393224 | tf_op jit(solution)/shard_map/ppermute | solution.py:404
  136.6 20.4 %collective-permute-start.32 = (f32[2,2,96,384]{3,2,1,0:T(8,128)S(1)}, f32[2,2,96,384]{3,2,1,0:T(8,128)S(1)}, u32[]{:S(2)}, u32[]{:S(2)}) collective-permute-start(f32[2,2,96,384]{3,2,1,0:T(8,128)S(1)} %pad_maximum_fusion), channel_id=1, source_target_pairs={{0,1},{1,0},{2,3},{3,2},{4,5},{5,4},{6,7},{7,6},{8,9},{9,8},{10,11... | collective-permute-start | bytes 1769480 | tf_op jit(solution)/shard_map/ppermute | solution.py:396
  137.9 10.8 %collective-permute-start.36 = (f32[512,256]{1,0:T(8,128)S(1)}, f32[512,256]{1,0:T(8,128)S(1)}, u32[]{:S(2)}, u32[]{:S(2)}) collective-permute-start(f32[512,256]{1,0:T(8,128)S(1)} %pad_maximum_fusion.1), channel_id=1, source_target_pairs={{0,8},{1,9},{2,10},{3,11},{4,68},{5,69},{6,70},{7,71},{8,0},{9,1},... | collective-permute-start | bytes 1572872 | tf_op jit(solution)/shard_map/ppermute | solution.py:404
  141.8 15.2 %collective-permute-start.31 = (f32[512,256]{1,0:T(8,128)S(1)}, f32[512,256]{1,0:T(8,128)S(1)}, u32[]{:S(2)}, u32[]{:S(2)}) collective-permute-start(f32[512,256]{1,0:T(8,128)S(1)} %pad_maximum_fusion.1), channel_id=1, source_target_pairs={{0,24},{1,25},{2,26},{3,27},{4,196},{5,197},{6,198},{7,199},{8,16}... | collective-permute-start | bytes 1572872 | tf_op jit(solution)/shard_map/ppermute | solution.py:404
  143.2 13.8 %collective-permute-start.30 = (f32[512,256]{1,0:T(8,128)S(1)}, f32[512,256]{1,0:T(8,128)S(1)}, u32[]{:S(2)}, u32[]{:S(2)}) collective-permute-start(f32[512,256]{1,0:T(8,128)S(1)} %pad_maximum_fusion.1), channel_id=1, source_target_pairs={{0,16},{1,17},{2,18},{3,19},{4,132},{5,133},{6,134},{7,135},{8,24}... | collective-permute-start | bytes 1572872 | tf_op jit(solution)/shard_map/ppermute | solution.py:404
  143.6 19.5 %collective-permute-start.35 = (f32[512,256]{1,0:T(8,128)S(1)}, f32[512,256]{1,0:T(8,128)S(1)}, u32[]{:S(2)}, u32[]{:S(2)}) collective-permute-start(f32[512,256]{1,0:T(8,128)S(1)} %pad_maximum_fusion.1), channel_id=1, source_target_pairs={{0,4},{4,0},{1,5},{5,1},{2,6},{6,2},{3,7},{7,3},{8,12},{12,8},{9,1... | collective-permute-start | bytes 1572872 | tf_op jit(solution)/shard_map/ppermute | solution.py:396
  148.7 14.4 %collective-permute-start.37 = (f32[512,256]{1,0:T(8,128)S(1)}, f32[512,256]{1,0:T(8,128)S(1)}, u32[]{:S(2)}, u32[]{:S(2)}) collective-permute-start(f32[512,256]{1,0:T(8,128)S(1)} %collective-permute-done.36), channel_id=1, source_target_pairs={{0,4},{4,0},{1,5},{5,1},{2,6},{6,2},{3,7},{7,3},{8,12},{12,8},{9,1... | collective-permute-start | bytes 1572872 | tf_op jit(solution)/shard_map/ppermute | solution.py:396
  157.0 8.4 %collective-permute-start.33 = (f32[512,256]{1,0:T(8,128)S(1)}, f32[512,256]{1,0:T(8,128)S(1)}, u32[]{:S(2)}, u32[]{:S(2)}) collective-permute-start(f32[512,256]{1,0:T(8,128)S(1)} %collective-permute-done.30), channel_id=1, source_target_pairs={{0,4},{4,0},{1,5},{5,1},{2,6},{6,2},{3,7},{7,3},{8,12},{12,8},{9,1... | collective-permute-start | bytes 1572872 | tf_op jit(solution)/shard_map/ppermute | solution.py:396
  161.8 3.6 %collective-permute-start.34 = (f32[512,256]{1,0:T(8,128)S(1)}, f32[512,256]{1,0:T(8,128)S(1)}, u32[]{:S(2)}, u32[]{:S(2)}) collective-permute-start(f32[512,256]{1,0:T(8,128)S(1)} %collective-permute-done.31), channel_id=1, source_target_pairs={{0,4},{4,0},{1,5},{5,1},{2,6},{6,2},{3,7},{7,3},{8,12},{12,8},{9,1... | collective-permute-start | bytes 1572872 | tf_op jit(solution)/shard_map/ppermute | solution.py:396
  (5 other events, 53.4 us)

commit v3 on v2

--- a/solution.py
+++ b/solution.py
@@ -139,7 +139,7 @@
         total[...] += re * re + im * im
         return carry
 
-    lax.fori_loop(0, modes, outward, 0, unroll=UNROLL)
+    lax.fori_loop(0, modes, outward, 0, unroll=2 * UNROLL)
     total[...] = 1.0 - amplitude_ref[...] * lax.rsqrt(total[...])
     term_ref[...] = jnp.zeros_like(term_ref)
     tables = (down_t[...], across[...], lanes, rows)
@@ -464,9 +464,8 @@
     low = across_rows(class_rows[:, :outside], -1)
     corner = across_rows(class_rows[:, :outside, :pattern], -1, -1)
     right = across_columns(class_rows[:, :, :pattern], -1)
-    right, place_later = tied(right, place)
+    target, place_later = tied(by_parity(amplitude[0, 0]), place)
     spots = [place] + [among(place_later, "zl", d) for d in (1, 2, 3)]
-    target = by_parity(amplitude[0, 0])
     rows = list(cut_call(own_class, spots, blocks, right, low, corner))
     rows = rows[:1] + [among(rows[d], "zl", d) for d in (1, 2, 3)]
 

time: 168 us -> 165 us (0.982)
    ppermute x12, waiting for transfers between devices: 9.59 us -> 12.9 us  [exchange(): return lax.ppermute(block, AXES, route)]
    ppermute x3, waiting for transfers between devices: 2.89 us -> 0.58 us  [across_rows(): return lax.ppermute(block, AXES, route)]
  transfers between devices with their start and end apart: 39 -> 39, of which waited for: 16 -> 21; matrix products, arithmetic and copies ran while one was open for 3% -> 2% of each run, Pallas kernels for 6% -> 6%
where the time goes in v3:
time: 165 us
  starting transfers between devices  89.7 us (54%)
  waiting for transfers between devices  42.3 us (26%)
  Pallas kernels  23.3 us (14%)
  other arithmetic  3.63 us (2%)
  local copies, waits for them, and re-layouts  2.79 us (2%)
  matrix products  1.74 us (1%)
    ppermute x20, starting transfers between devices, among(): return lax.ppermute(block, axis, [(i, i ^ distance) for i in range(n)])  36.2 us
    ppermute x12, starting transfers between devices, exchange(): return lax.ppermute(block, AXES, route)  27.4 us
    ppermute x20, waiting for transfers between devices, among(): return lax.ppermute(block, axis, [(i, i ^ distance) for i in range(n)])  25.8 us
    ppermute x12, waiting for transfers between devices, exchange(): return lax.ppermute(block, AXES, route)  12.9 us
    pallas_call x1, Pallas kernels, first_call(): pl.pallas_call(first_kernel, out_shape=[jax.ShapeDtypeStruct(s, F32) for...  10.8 us
    ppermute x2, starting transfers between devices, across_columns(): return lax.ppermute(block, TILE_AXES, route)  9.65 us
    ppermute x3, starting transfers between devices, across_rows(): return lax.ppermute(block, AXES, route)  8.93 us
    pallas_call x1, Pallas kernels, second_call(): pl.pallas_call(second_kernel, out_shape=[jax.ShapeDtypeStruct(s, F32) for...  5.14 us
  transfers between devices with their start and end apart: 39, of which 21 were waited for; matrix products, arithmetic and copies ran while one was open for 2% of the time, Pallas kernels for 6%

profile of v3, /device:TPU:1, one launch (start us, length us, event | category | flops | bytes accessed | tf_op | source)
XLA Modules:
  0.0 164.9 jit_solution(5850879920697888125)
XLA Ops:
  1.9 1.4 collective-permute-start.5
  3.3 5.1 %collective-permute-start.3 = (f32[2,96,256]{2,1,0:T(8,128)S(1)}, f32[2,96,256]{2,1,0:T(8,128)S(1)}, u32[]{:S(2)}, u32[]{:S(2)}) collective-permute-start(f32[2,96,256]{2,1,0:T(8,128)S(1)} %slice.127), channel_id=1, source_target_pairs={{4,0},{8,4},{12,8},{20,16},{24,20},{28,24},{36,32},{40,36},{44,40}... | collective-permute-start | bytes 589832 | tf_op jit(solution)/shard_map/ppermute | solution.py:381
  8.5 1.3 collective-permute-start.4
  9.8 1.3 fusion
  11.6 2.7 %collective-permute-start.2 = (s32[2]{0:T(128)S(1)}, s32[2]{0:T(128)S(1)}, u32[]{:S(2)}, u32[]{:S(2)}) collective-permute-start(s32[2]{0:T(128)S(1)} %bitcast.64), channel_id=1, source_target_pairs={{0,3},{1,2},{2,1},{3,0},{4,7},{5,6},{6,5},{7,4},{8,11},{9,10},{10,... | collective-permute-start | bytes 32 | tf_op jit(solution)/shard_map/ppermute | solution.py:396
  14.3 1.9 %collective-permute-done.2.spot3 = s32[2]{0:T(128)S(1)} collective-permute-done((s32[2]{0:T(128)S(1)}, s32[2]{0:T(128)S(1)}, u32[]{:S(2)}, u32[]{:S(2)}) %collective-permute-start.2) | collective-permute-done | bytes 40 | tf_op jit(solution)/shard_map/ppermute | solution.py:396
  16.2 1.7 %collective-permute-done.1.spot2 = s32[2]{0:T(128)S(1)} collective-permute-done((s32[2]{0:T(128)S(1)}, s32[2]{0:T(128)S(1)}, u32[]{:S(2)}, u32[]{:S(2)}) %collective-permute-start.1) | collective-permute-done | bytes 40 | tf_op jit(solution)/shard_map/ppermute | solution.py:396
  18.6 1.6 cut.1
  20.3 2.8 %collective-permute-start.7 = (f32[2,9,8,256]{3,2,1,0:T(8,128)}, f32[2,9,8,256]{3,2,1,0:T(8,128)S(1)}, u32[]{:S(2)}, u32[]{:S(2)}) collective-permute-start(f32[2,9,8,256]{3,2,1,0:T(8,128)} %get-tuple-element.77), channel_id=1, source_target_pairs={{0,2},{1,3},{2,0},{3,1},{4,6},{5,7},{6,4},{7,5},{8,10},{9,11},{10,... | collective-permute-start | bytes 442376 | tf_op jit(solution)/shard_map/ppermute | solution.py:396
  26.1 5.9 %collective-permute-done.8.rows3 = f32[2,9,8,256]{3,2,1,0:T(8,128)S(1)} collective-permute-done((f32[2,9,8,256]{3,2,1,0:T(8,128)}, f32[2,9,8,256]{3,2,1,0:T(8,128)S(1)}, u32[]{:S(2)}, u32[]{:S(2)}) %collective-permute-start.8) | collective-permute-done | bytes 147488 | tf_op jit(solution)/shard_map/ppermute | solution.py:396
  32.7 10.8 %outward.1 = (f32[4,2,256,256]{3,2,1,0:T(8,128)S(1)}, f32[4,2,256,256]{3,2,1,0:T(8,128)}, f32[2,256,256]{2,1,0:T(8,128)S(1)}, f32[2,256,256]{2,1,0:T(8,128)S(1)}) custom-call(s32[5]{0:T(128)S(1)} %stack.37.where_ref, f32[2,9,8,256]{3,2,1,0:T(8,128)S(1)} %get-tuple-element.75.rows0, f32[2,9,8,256]{3,2,1,0:T(8,128)S(1)} %collective-permute-done.6.rows1, ...), custom_call_target="tpu_custom_call" | custom-call | tf_op jit(solution)/shard_map/outward/pallas_call | solution.py:208
  43.5 4.0 %collective-permute-start.9 = (f32[4,2,256,256]{3,2,1,0:T(8,128)S(1)}, f32[4,2,256,256]{3,2,1,0:T(8,128)S(1)}, u32[]{:S(2)}, u32[]{:S(2)}) collective-permute-start(f32[4,2,256,256]{3,2,1,0:T(8,128)S(1)} %get-tuple-element.84), channel_id=1, source_target_pairs={{0,4},{4,0},{1,5},{5,1},{2,6},{6,2},{3,7},{7,3},{8,12},{12,8},{9,1... | collective-permute-start | bytes 6291464 | tf_op jit(solution)/shard_map/ppermute | solution.py:396
  47.6 5.1 %homeward.1 = (f32[4,2,256,256]{3,2,1,0:T(8,128)S(1)}, f32[2,9,8,256]{3,2,1,0:T(8,128)S(1)}, f32[2,9,8,256]{3,2,1,0:T(8,128)S(1)}, f32[2,9,8,256]{3,2,1,0:T(8,128)S(1)}, f32[2,9,8,256]{3,2,1,0:T(8,128)S(1)}) custom-call(s32[5]{0:T(128)S(1)} %stack.37.where_ref, f32[4,2,256,256]{3,2,1,0:T(8,128)} %get-tuple-element.80.corrected_ref, ...), custom_call_target="tpu_custom_call" | custom-call | tf_op jit(solution)/shard_map/homeward/pallas_call | solution.py:229
  53.9 8.0 %collective-permute-start.10 = (f32[512,256]{1,0:T(8,128)}, f32[512,256]{1,0:T(8,128)}, u32[]{:S(2)}, u32[]{:S(2)}) collective-permute-start(f32[512,256]{1,0:T(8,128)} %bitcast.10), channel_id=1, source_target_pairs={{0,8},{1,9},{2,10},{3,11},{4,68},{5,69},{6,70},{7,71},{8,0},{9,1},... | collective-permute-start | bytes 1572872 | tf_op jit(solution)/shard_map/ppermute | solution.py:404
  61.9 2.9 %collective-permute-start.11 = (f32[512,256]{1,0:T(8,128)S(1)}, f32[512,256]{1,0:T(8,128)}, u32[]{:S(2)}, u32[]{:S(2)}) collective-permute-start(f32[512,256]{1,0:T(8,128)S(1)} %bitcast.73), channel_id=1, source_target_pairs={{0,16},{1,17},{2,18},{3,19},{4,132},{5,133},{6,134},{7,135},{8,24}... | collective-permute-start | bytes 1572872 | tf_op jit(solution)/shard_map/ppermute | solution.py:404
  64.8 1.9 %collective-permute-start.13 = (f32[2,9,8,256]{3,2,1,0:T(8,128)S(1)}, f32[2,9,8,256]{3,2,1,0:T(8,128)S(1)}, u32[]{:S(2)}, u32[]{:S(2)}) collective-permute-start(f32[2,9,8,256]{3,2,1,0:T(8,128)S(1)} %get-tuple-element.94), channel_id=1, source_target_pairs={{0,1},{1,0},{2,3},{3,2},{4,5},{5,4},{6,7},{7,6},{8,9},{9,8},{10,11... | collective-permute-start | bytes 442376 | tf_op jit(solution)/shard_map/ppermute | solution.py:396
  67.3 1.9 %collective-permute-done.13.rows1 = f32[2,9,8,256]{3,2,1,0:T(8,128)S(1)} collective-permute-done((f32[2,9,8,256]{3,2,1,0:T(8,128)S(1)}, f32[2,9,8,256]{3,2,1,0:T(8,128)S(1)}, u32[]{:S(2)}, u32[]{:S(2)}) %collective-permute-start.13) | collective-permute-done | bytes 147488 | tf_op jit(solution)/shard_map/ppermute | solution.py:396
  69.2 1.8 %collective-permute-start.15 = (f32[2,9,8,256]{3,2,1,0:T(8,128)S(1)}, f32[2,9,8,256]{3,2,1,0:T(8,128)S(1)}, u32[]{:S(2)}, u32[]{:S(2)}) collective-permute-start(f32[2,9,8,256]{3,2,1,0:T(8,128)S(1)} %get-tuple-element.96), channel_id=1, source_target_pairs={{0,3},{1,2},{2,1},{3,0},{4,7},{5,6},{6,5},{7,4},{8,11},{9,10},{10,... | collective-permute-start | bytes 442376 | tf_op jit(solution)/shard_map/ppermute | solution.py:396
  71.0 2.7 %collective-permute-done.14.rows2 = f32[2,9,8,256]{3,2,1,0:T(8,128)S(1)} collective-permute-done((f32[2,9,8,256]{3,2,1,0:T(8,128)S(1)}, f32[2,9,8,256]{3,2,1,0:T(8,128)S(1)}, u32[]{:S(2)}, u32[]{:S(2)}) %collective-permute-start.14) | collective-permute-done | bytes 147488 | tf_op jit(solution)/shard_map/ppermute | solution.py:396
  73.7 3.4 %collective-permute-done.15.rows3 = f32[2,9,8,256]{3,2,1,0:T(8,128)S(1)} collective-permute-done((f32[2,9,8,256]{3,2,1,0:T(8,128)S(1)}, f32[2,9,8,256]{3,2,1,0:T(8,128)S(1)}, u32[]{:S(2)}, u32[]{:S(2)}) %collective-permute-start.15) | collective-permute-done | bytes 147488 | tf_op jit(solution)/shard_map/ppermute | solution.py:396
  78.0 2.0 %collective-permute-done.12 = f32[512,256]{1,0:T(8,128)} collective-permute-done((f32[512,256]{1,0:T(8,128)S(1)}, f32[512,256]{1,0:T(8,128)}, u32[]{:S(2)}, u32[]{:S(2)}) %collective-permute-start.12) | collective-permute-done | bytes 524320 | tf_op jit(solution)/shard_map/ppermute | solution.py:404
  80.1 1.5 add_add_fusion
  82.5 3.8 %collective-permute-start.17 = (f32[128,256]{1,0:T(8,128)S(1)}, f32[128,256]{1,0:T(8,128)S(1)}, u32[]{:S(2)}, u32[]{:S(2)}) collective-permute-start(f32[128,256]{1,0:T(8,128)S(1)} %get-tuple-element.100), channel_id=1, source_target_pairs={{0,128},{1,129},{2,130},{3,131},{4,20},{5,21},{6,22},{7,23},{8,136... | collective-permute-start | bytes 393224 | tf_op jit(solution)/shard_map/ppermute | solution.py:404
  86.4 4.5 %collective-permute-start.19 = (f32[2,160,256]{2,1,0:T(8,128)S(1)}, f32[2,160,256]{2,1,0:T(8,128)S(1)}, u32[]{:S(2)}, u32[]{:S(2)}) collective-permute-start(f32[2,160,256]{2,1,0:T(8,128)S(1)} %get-tuple-element.103), channel_id=1, source_target_pairs={{0,4},{4,8},{8,12},{16,20},{20,24},{24,28},{32,36},{36,40},{40,44}... | collective-permute-start | bytes 983048 | tf_op jit(solution)/shard_map/ppermute | solution.py:381
  92.5 2.4 %collective-permute-done.19 = f32[2,160,256]{2,1,0:T(8,128)S(1)} collective-permute-done((f32[2,160,256]{2,1,0:T(8,128)S(1)}, f32[2,160,256]{2,1,0:T(8,128)S(1)}, u32[]{:S(2)}, u32[]{:S(2)}) %collective-permute-start.19) | collective-permute-done | bytes 327712 | tf_op jit(solution)/shard_map/ppermute | solution.py:381
  95.0 4.5 %all-to-all-start = ((f32[4,32,256]{2,1,0:T(8,128)}), f32[4,32,256]{2,1,0:T(8,128)S(1)}, u32[]{:S(2)}, u32[]{:S(2)}) async-start(f32[4,32,256]{2,1,0:T(8,128)} %bitcast.18), calls=%async_computation | async-start | bytes 262144 | tf_op jit(solution)/shard_map/all_to_all | solution.py:422
  99.4 6.2 %collective-permute-start.21 = (f32[2,64,384]{2,1,0:T(8,128)S(1)}, f32[2,64,384]{2,1,0:T(8,128)S(1)}, u32[]{:S(2)}, u32[]{:S(2)}) collective-permute-start(f32[2,64,384]{2,1,0:T(8,128)S(1)} %slice.134), channel_id=1, source_target_pairs={{0,16},{1,17},{2,18},{3,19},{4,20},{5,21},{6,22},{7,23},{8,24},{9,... | collective-permute-start | bytes 589832 | tf_op jit(solution)/shard_map/ppermute | solution.py:391
  105.7 3.1 %collective-permute-start.20 = (f32[32,256]{1,0:T(8,128)S(1)}, f32[32,256]{1,0:T(8,128)S(1)}, u32[]{:S(2)}, u32[]{:S(2)}) collective-permute-start(f32[32,256]{1,0:T(8,128)S(1)} %reduce_sum.9), channel_id=1, source_target_pairs={{0,35},{1,34},{2,33},{3,32},{4,39},{5,38},{6,37},{7,36},{8,43},{9,... | collective-permute-start | bytes 98312 | tf_op jit(solution)/shard_map/ppermute | solution.py:412
  110.2 4.0 %collective-permute-start.25 = (f32[96,384]{1,0:T(8,128)S(1)}, f32[96,384]{1,0:T(8,128)S(1)}, u32[]{:S(2)}, u32[]{:S(2)}) collective-permute-start(f32[96,384]{1,0:T(8,128)S(1)} %slice_bitcast_fusion.3), channel_id=1, source_target_pairs={{0,2},{1,3},{2,0},{3,1},{4,6},{5,7},{6,4},{7,5},{8,10},{9,11},{10,... | collective-permute-start | bytes 442376 | tf_op jit(solution)/shard_map/ppermute | solution.py:396
  114.1 1.5 collective-permute-start.24
  115.7 2.0 %collective-permute-start.22 = (f32[32,256]{1,0:T(8,128)S(1)}, f32[32,256]{1,0:T(8,128)S(1)}, u32[]{:S(2)}, u32[]{:S(2)}) collective-permute-start(f32[32,256]{1,0:T(8,128)S(1)} %add_multiply_fusion), channel_id=1, source_target_pairs={{0,1},{1,0},{2,3},{3,2},{4,5},{5,4},{6,7},{7,6},{8,9},{9,8},{10,11... | collective-permute-start | bytes 98312 | tf_op jit(solution)/shard_map/ppermute | solution.py:396
  117.7 1.8 %collective-permute-done.24 = f32[32,256]{1,0:T(8,128)S(1)} collective-permute-done((f32[32,256]{1,0:T(8,128)S(1)}, f32[32,256]{1,0:T(8,128)S(1)}, u32[]{:S(2)}, u32[]{:S(2)}) %collective-permute-start.24) | collective-permute-done | bytes 32800 | tf_op jit(solution)/shard_map/ppermute | solution.py:396
  119.5 4.3 %collective-permute-done.23 = f32[32,256]{1,0:T(8,128)S(1)} collective-permute-done((f32[32,256]{1,0:T(8,128)S(1)}, f32[32,256]{1,0:T(8,128)S(1)}, u32[]{:S(2)}, u32[]{:S(2)}) %collective-permute-start.23) | collective-permute-done | bytes 32800 | tf_op jit(solution)/shard_map/ppermute | solution.py:396
  123.8 1.6 collective-permute-start.29
  125.6 5.2 %collective-permute-start.27 = (f32[128,256]{1,0:T(8,128)S(1)}, f32[128,256]{1,0:T(8,128)S(1)}, u32[]{:S(2)}, u32[]{:S(2)}) collective-permute-start(f32[128,256]{1,0:T(8,128)S(1)} %pad_maximum_fusion.3), channel_id=1, source_target_pairs={{0,128},{1,129},{2,130},{3,131},{4,20},{5,21},{6,22},{7,23},{8,136... | collective-permute-start | bytes 393224 | tf_op jit(solution)/shard_map/ppermute | solution.py:404
  130.8 2.4 %collective-permute-done.27 = f32[128,256]{1,0:T(8,128)S(1)} collective-permute-done((f32[128,256]{1,0:T(8,128)S(1)}, f32[128,256]{1,0:T(8,128)S(1)}, u32[]{:S(2)}, u32[]{:S(2)}) %collective-permute-start.27) | collective-permute-done | bytes 131104 | tf_op jit(solution)/shard_map/ppermute | solution.py:404
  133.1 1.8 %collective-permute-done.26 = f32[128,256]{1,0:T(8,128)S(1)} collective-permute-done((f32[128,256]{1,0:T(8,128)S(1)}, f32[128,256]{1,0:T(8,128)S(1)}, u32[]{:S(2)}, u32[]{:S(2)}) %collective-permute-start.26) | collective-permute-done | bytes 131104 | tf_op jit(solution)/shard_map/ppermute | solution.py:404
  135.1 1.3 collective-permute-start.32
  136.4 3.7 %collective-permute-start.36 = (f32[512,256]{1,0:T(8,128)S(1)}, f32[512,256]{1,0:T(8,128)S(1)}, u32[]{:S(2)}, u32[]{:S(2)}) collective-permute-start(f32[512,256]{1,0:T(8,128)S(1)} %pad_maximum_fusion.1), channel_id=1, source_target_pairs={{0,8},{1,9},{2,10},{3,11},{4,68},{5,69},{6,70},{7,71},{8,0},{9,1},... | collective-permute-start | bytes 1572872 | tf_op jit(solution)/shard_map/ppermute | solution.py:404
  140.1 1.7 %collective-permute-start.31 = (f32[512,256]{1,0:T(8,128)S(1)}, f32[512,256]{1,0:T(8,128)S(1)}, u32[]{:S(2)}, u32[]{:S(2)}) collective-permute-start(f32[512,256]{1,0:T(8,128)S(1)} %pad_maximum_fusion.1), channel_id=1, source_target_pairs={{0,24},{1,25},{2,26},{3,27},{4,196},{5,197},{6,198},{7,199},{8,16}... | collective-permute-start | bytes 1572872 | tf_op jit(solution)/shard_map/ppermute | solution.py:404
  142.8 2.8 %collective-permute-start.35 = (f32[512,256]{1,0:T(8,128)S(1)}, f32[512,256]{1,0:T(8,128)S(1)}, u32[]{:S(2)}, u32[]{:S(2)}) collective-permute-start(f32[512,256]{1,0:T(8,128)S(1)} %pad_maximum_fusion.1), channel_id=1, source_target_pairs={{0,4},{4,0},{1,5},{5,1},{2,6},{6,2},{3,7},{7,3},{8,12},{12,8},{9,1... | collective-permute-start | bytes 1572872 | tf_op jit(solution)/shard_map/ppermute | solution.py:396
  145.7 1.3 collective-permute-done.36
  146.9 3.8 %collective-permute-start.37 = (f32[512,256]{1,0:T(8,128)S(1)}, f32[512,256]{1,0:T(8,128)S(1)}, u32[]{:S(2)}, u32[]{:S(2)}) collective-permute-start(f32[512,256]{1,0:T(8,128)S(1)} %collective-permute-done.36), channel_id=1, source_target_pairs={{0,4},{4,0},{1,5},{5,1},{2,6},{6,2},{3,7},{7,3},{8,12},{12,8},{9,1... | collective-permute-start | bytes 1572872 | tf_op jit(solution)/shard_map/ppermute | solution.py:396
  150.7 2.7 %collective-permute-done.31 = f32[512,256]{1,0:T(8,128)S(1)} collective-permute-done((f32[512,256]{1,0:T(8,128)S(1)}, f32[512,256]{1,0:T(8,128)S(1)}, u32[]{:S(2)}, u32[]{:S(2)}) %collective-permute-start.31) | collective-permute-done | bytes 524320 | tf_op jit(solution)/shard_map/ppermute | solution.py:404
  153.5 1.8 %collective-permute-done.30 = f32[512,256]{1,0:T(8,128)S(1)} collective-permute-done((f32[512,256]{1,0:T(8,128)S(1)}, f32[512,256]{1,0:T(8,128)S(1)}, u32[]{:S(2)}, u32[]{:S(2)}) %collective-permute-start.30) | collective-permute-done | bytes 524320 | tf_op jit(solution)/shard_map/ppermute | solution.py:404
  155.3 4.3 %collective-permute-start.33 = (f32[512,256]{1,0:T(8,128)S(1)}, f32[512,256]{1,0:T(8,128)S(1)}, u32[]{:S(2)}, u32[]{:S(2)}) collective-permute-start(f32[512,256]{1,0:T(8,128)S(1)} %collective-permute-done.30), channel_id=1, source_target_pairs={{0,4},{4,0},{1,5},{5,1},{2,6},{6,2},{3,7},{7,3},{8,12},{12,8},{9,1... | collective-permute-start | bytes 1572872 | tf_op jit(solution)/shard_map/ppermute | solution.py:396
  160.8 2.3 %fill.2.refs_2_ = f32[8,2,256,256]{3,2,1,0:T(8,128)} custom-call(s32[5]{0:T(128)S(1)} %stack.37.where_ref, f32[2,256,256]{2,1,0:T(8,128)S(1)} %bitcast.53, f32[2,256,256]{2,1,0:T(8,128)S(1)} %bitcast.61, f32[2,256,256]{2,1,0:T(8,128)S(1)} %bitcast.59, f32[2,256,256]{2,1,0:T(8,128)S(1)} %bitcast.62, f32[2,256,256]{2,1,0:T(8,128)S(1)} %bitcast.60, ...), custom_call_target="tpu_custom_call" | custom-call | tf_op jit(solution)/shard_map/fill/pallas_call | solution.py:356
  163.2 1.5 fill.3
  (100 shorter events, 15.5 us)
Async XLA Ops:
  1.8 30.2 %copy-start.2 = (bf16[768,256]{1,0:T(8,128)(2,1)S(1)}, bf16[768,256]{1,0:T(8,128)(2,1)}, u32[]{:S(2)}) copy-start(bf16[768,256]{1,0:T(8,128)(2,1)} %constant.145.clone.down_t) | copy-start | bytes 1179652
  1.8 30.2 %copy-start.3 = (bf16[256,768]{1,0:T(8,128)(2,1)S(1)}, bf16[256,768]{1,0:T(8,128)(2,1)}, u32[]{:S(2)}) copy-start(bf16[256,768]{1,0:T(8,128)(2,1)} %constant.144.clone.across) | copy-start | bytes 1179652
  1.9 30.2 %copy-start.4 = (f32[2,128,128]{2,1,0:T(8,128)S(1)}, f32[2,128,128]{2,1,0:T(8,128)}, u32[]{:S(2)}) copy-start(f32[2,128,128]{2,1,0:T(8,128)} %constant.148.clone.rows_ref) | copy-start | bytes 393220
  1.9 30.2 %copy-start.5 = (bf16[256,768]{1,0:T(8,128)(2,1)S(1)}, bf16[256,768]{1,0:T(8,128)(2,1)}, u32[]{:S(2)}) copy-start(bf16[256,768]{1,0:T(8,128)(2,1)} %constant.146.clone.across_t) | copy-start | bytes 1179652
  1.9 30.2 %copy-start.6 = (bf16[768,256]{1,0:T(8,128)(2,1)S(1)}, bf16[768,256]{1,0:T(8,128)(2,1)}, u32[]{:S(2)}) copy-start(bf16[768,256]{1,0:T(8,128)(2,1)} %constant.143.clone.down) | copy-start | bytes 1179652
  1.9 16.7 %collective-permute-start.5 = (f32[2,64,256]{2,1,0:T(8,128)S(1)}, f32[2,64,256]{2,1,0:T(8,128)S(1)}, u32[]{:S(2)}, u32[]{:S(2)}) collective-permute-start(f32[2,64,256]{2,1,0:T(8,128)S(1)} %slice.129), channel_id=1, source_target_pairs={{20,0},{21,1},{22,2},{23,3},{24,4},{25,5},{26,6},{27,7},{28,8},{29... | collective-permute-start | bytes 393224 | tf_op jit(solution)/shard_map/ppermute | solution.py:391
  3.3 15.2 %collective-permute-start.3 = (f32[2,96,256]{2,1,0:T(8,128)S(1)}, f32[2,96,256]{2,1,0:T(8,128)S(1)}, u32[]{:S(2)}, u32[]{:S(2)}) collective-permute-start(f32[2,96,256]{2,1,0:T(8,128)S(1)} %slice.127), channel_id=1, source_target_pairs={{4,0},{8,4},{12,8},{20,16},{24,20},{28,24},{36,32},{40,36},{44,40}... | collective-permute-start | bytes 589832 | tf_op jit(solution)/shard_map/ppermute | solution.py:381
  8.5 10.1 %collective-permute-start.4 = (f32[2,64,384]{2,1,0:T(8,128)S(1)}, f32[2,64,384]{2,1,0:T(8,128)S(1)}, u32[]{:S(2)}, u32[]{:S(2)}) collective-permute-start(f32[2,64,384]{2,1,0:T(8,128)S(1)} %slice.128), channel_id=1, source_target_pairs={{16,0},{17,1},{18,2},{19,3},{20,4},{21,5},{22,6},{23,7},{24,8},{25... | collective-permute-start | bytes 589832 | tf_op jit(solution)/shard_map/ppermute | solution.py:391
  11.6 4.6 %collective-permute-start.2 = (s32[2]{0:T(128)S(1)}, s32[2]{0:T(128)S(1)}, u32[]{:S(2)}, u32[]{:S(2)}) collective-permute-start(s32[2]{0:T(128)S(1)} %bitcast.64), channel_id=1, source_target_pairs={{0,3},{1,2},{2,1},{3,0},{4,7},{5,6},{6,5},{7,4},{8,11},{9,10},{10,... | collective-permute-start | bytes 32 | tf_op jit(solution)/shard_map/ppermute | solution.py:396
  14.3 3.6 %collective-permute-start.1 = (s32[2]{0:T(128)S(1)}, s32[2]{0:T(128)S(1)}, u32[]{:S(2)}, u32[]{:S(2)}) collective-permute-start(s32[2]{0:T(128)S(1)} %bitcast.65), channel_id=1, source_target_pairs={{0,2},{1,3},{2,0},{3,1},{4,6},{5,7},{6,4},{7,5},{8,10},{9,11},{10,... | collective-permute-start | bytes 32 | tf_op jit(solution)/shard_map/ppermute | solution.py:396
  16.2 2.4 %collective-permute-start = (s32[2]{0:T(128)S(1)}, s32[2]{0:T(128)S(1)}, u32[]{:S(2)}, u32[]{:S(2)}) collective-permute-start(s32[2]{0:T(128)S(1)} %bitcast.66), channel_id=1, source_target_pairs={{0,1},{1,0},{2,3},{3,2},{4,5},{5,4},{6,7},{7,6},{8,9},{9,8},{10,11... | collective-permute-start | bytes 32 | tf_op jit(solution)/shard_map/ppermute | solution.py:396
  20.2 5.6 %collective-permute-start.6 = (f32[2,9,8,256]{3,2,1,0:T(8,128)}, f32[2,9,8,256]{3,2,1,0:T(8,128)S(1)}, u32[]{:S(2)}, u32[]{:S(2)}) collective-permute-start(f32[2,9,8,256]{3,2,1,0:T(8,128)} %get-tuple-element.76), channel_id=1, source_target_pairs={{0,1},{1,0},{2,3},{3,2},{4,5},{5,4},{6,7},{7,6},{8,9},{9,8},{10,11... | collective-permute-start | bytes 442376 | tf_op jit(solution)/shard_map/ppermute | solution.py:396
  20.3 5.9 %collective-permute-start.7 = (f32[2,9,8,256]{3,2,1,0:T(8,128)}, f32[2,9,8,256]{3,2,1,0:T(8,128)S(1)}, u32[]{:S(2)}, u32[]{:S(2)}) collective-permute-start(f32[2,9,8,256]{3,2,1,0:T(8,128)} %get-tuple-element.77), channel_id=1, source_target_pairs={{0,2},{1,3},{2,0},{3,1},{4,6},{5,7},{6,4},{7,5},{8,10},{9,11},{10,... | collective-permute-start | bytes 442376 | tf_op jit(solution)/shard_map/ppermute | solution.py:396
  23.1 8.9 %collective-permute-start.8 = (f32[2,9,8,256]{3,2,1,0:T(8,128)}, f32[2,9,8,256]{3,2,1,0:T(8,128)S(1)}, u32[]{:S(2)}, u32[]{:S(2)}) collective-permute-start(f32[2,9,8,256]{3,2,1,0:T(8,128)} %get-tuple-element.78), channel_id=1, source_target_pairs={{0,3},{1,2},{2,1},{3,0},{4,7},{5,6},{6,5},{7,4},{8,11},{9,10},{10,... | collective-permute-start | bytes 442376 | tf_op jit(solution)/shard_map/ppermute | solution.py:396
  43.5 9.2 %collective-permute-start.9 = (f32[4,2,256,256]{3,2,1,0:T(8,128)S(1)}, f32[4,2,256,256]{3,2,1,0:T(8,128)S(1)}, u32[]{:S(2)}, u32[]{:S(2)}) collective-permute-start(f32[4,2,256,256]{3,2,1,0:T(8,128)S(1)} %get-tuple-element.84), channel_id=1, source_target_pairs={{0,4},{4,0},{1,5},{5,1},{2,6},{6,2},{3,7},{7,3},{8,12},{12,8},{9,1... | collective-permute-start | bytes 6291464 | tf_op jit(solution)/shard_map/ppermute | solution.py:396
  52.7 24.4 %copy-start.9 = (s32[1,1,2]{2,1,0:T(1,128)S(1)}, s32[1,1,2]{2,1,0:T(1,128)}, u32[]{:S(2)}) copy-start(s32[1,1,2]{2,1,0:T(1,128)} %param.17) | copy-start | bytes 28
  52.7 24.4 %copy-start.12 = (s32[2]{0:T(128)S(1)}, s32[2]{0:T(128)}, u32[]{:S(2)}) copy-start(s32[2]{0:T(128)} %copy-done.11) | copy-start | bytes 28
  52.8 24.4 %copy-start.14 = (s32[2]{0:T(128)S(1)}, s32[2]{0:T(128)}, u32[]{:S(2)}) copy-start(s32[2]{0:T(128)} %copy-done.13) | copy-start | bytes 28
  52.8 24.4 %copy-start.16 = (s32[2]{0:T(128)S(1)}, s32[2]{0:T(128)}, u32[]{:S(2)}) copy-start(s32[2]{0:T(128)} %copy-done.15) | copy-start | bytes 28
  53.9 24.1 %collective-permute-start.10 = (f32[512,256]{1,0:T(8,128)}, f32[512,256]{1,0:T(8,128)}, u32[]{:S(2)}, u32[]{:S(2)}) collective-permute-start(f32[512,256]{1,0:T(8,128)} %bitcast.10), channel_id=1, source_target_pairs={{0,8},{1,9},{2,10},{3,11},{4,68},{5,69},{6,70},{7,71},{8,0},{9,1},... | collective-permute-start | bytes 1572872 | tf_op jit(solution)/shard_map/ppermute | solution.py:404
  61.9 16.1 %collective-permute-start.11 = (f32[512,256]{1,0:T(8,128)S(1)}, f32[512,256]{1,0:T(8,128)}, u32[]{:S(2)}, u32[]{:S(2)}) collective-permute-start(f32[512,256]{1,0:T(8,128)S(1)} %bitcast.73), channel_id=1, source_target_pairs={{0,16},{1,17},{2,18},{3,19},{4,132},{5,133},{6,134},{7,135},{8,24}... | collective-permute-start | bytes 1572872 | tf_op jit(solution)/shard_map/ppermute | solution.py:404
  64.8 15.3 %collective-permute-start.12 = (f32[512,256]{1,0:T(8,128)S(1)}, f32[512,256]{1,0:T(8,128)}, u32[]{:S(2)}, u32[]{:S(2)}) collective-permute-start(f32[512,256]{1,0:T(8,128)S(1)} %bitcast.72), channel_id=1, source_target_pairs={{0,24},{1,25},{2,26},{3,27},{4,196},{5,197},{6,198},{7,199},{8,16}... | collective-permute-start | bytes 1572872 | tf_op jit(solution)/shard_map/ppermute | solution.py:404
  64.8 4.4 %collective-permute-start.13 = (f32[2,9,8,256]{3,2,1,0:T(8,128)S(1)}, f32[2,9,8,256]{3,2,1,0:T(8,128)S(1)}, u32[]{:S(2)}, u32[]{:S(2)}) collective-permute-start(f32[2,9,8,256]{3,2,1,0:T(8,128)S(1)} %get-tuple-element.94), channel_id=1, source_target_pairs={{0,1},{1,0},{2,3},{3,2},{4,5},{5,4},{6,7},{7,6},{8,9},{9,8},{10,11... | collective-permute-start | bytes 442376 | tf_op jit(solution)/shard_map/ppermute | solution.py:396
  66.7 7.1 %collective-permute-start.14 = (f32[2,9,8,256]{3,2,1,0:T(8,128)S(1)}, f32[2,9,8,256]{3,2,1,0:T(8,128)S(1)}, u32[]{:S(2)}, u32[]{:S(2)}) collective-permute-start(f32[2,9,8,256]{3,2,1,0:T(8,128)S(1)} %get-tuple-element.95), channel_id=1, source_target_pairs={{0,2},{1,3},{2,0},{3,1},{4,6},{5,7},{6,4},{7,5},{8,10},{9,11},{10,... | collective-permute-start | bytes 442376 | tf_op jit(solution)/shard_map/ppermute | solution.py:396
  69.2 7.9 %collective-permute-start.15 = (f32[2,9,8,256]{3,2,1,0:T(8,128)S(1)}, f32[2,9,8,256]{3,2,1,0:T(8,128)S(1)}, u32[]{:S(2)}, u32[]{:S(2)}) collective-permute-start(f32[2,9,8,256]{3,2,1,0:T(8,128)S(1)} %get-tuple-element.96), channel_id=1, source_target_pairs={{0,3},{1,2},{2,1},{3,0},{4,7},{5,6},{6,5},{7,4},{8,11},{9,10},{10,... | collective-permute-start | bytes 442376 | tf_op jit(solution)/shard_map/ppermute | solution.py:396
  81.6 9.3 %collective-permute-start.16 = (f32[128,256]{1,0:T(8,128)S(1)}, f32[128,256]{1,0:T(8,128)S(1)}, u32[]{:S(2)}, u32[]{:S(2)}) collective-permute-start(f32[128,256]{1,0:T(8,128)S(1)} %get-tuple-element.99), channel_id=1, source_target_pairs={{0,64},{1,65},{2,66},{3,67},{4,12},{5,13},{6,14},{7,15},{8,72},{9,... | collective-permute-start | bytes 393224 | tf_op jit(solution)/shard_map/ppermute | solution.py:404
  82.5 8.3 %collective-permute-start.17 = (f32[128,256]{1,0:T(8,128)S(1)}, f32[128,256]{1,0:T(8,128)S(1)}, u32[]{:S(2)}, u32[]{:S(2)}) collective-permute-start(f32[128,256]{1,0:T(8,128)S(1)} %get-tuple-element.100), channel_id=1, source_target_pairs={{0,128},{1,129},{2,130},{3,131},{4,20},{5,21},{6,22},{7,23},{8,136... | collective-permute-start | bytes 393224 | tf_op jit(solution)/shard_map/ppermute | solution.py:404
  86.4 5.5 %collective-permute-start.18 = (f32[128,256]{1,0:T(8,128)S(1)}, f32[128,256]{1,0:T(8,128)S(1)}, u32[]{:S(2)}, u32[]{:S(2)}) collective-permute-start(f32[128,256]{1,0:T(8,128)S(1)} %get-tuple-element.101), channel_id=1, source_target_pairs={{0,192},{1,193},{2,194},{3,195},{4,28},{5,29},{6,30},{7,31},{8,200... | collective-permute-start | bytes 393224 | tf_op jit(solution)/shard_map/ppermute | solution.py:404
  86.4 8.5 %collective-permute-start.19 = (f32[2,160,256]{2,1,0:T(8,128)S(1)}, f32[2,160,256]{2,1,0:T(8,128)S(1)}, u32[]{:S(2)}, u32[]{:S(2)}) collective-permute-start(f32[2,160,256]{2,1,0:T(8,128)S(1)} %get-tuple-element.103), channel_id=1, source_target_pairs={{0,4},{4,8},{8,12},{16,20},{20,24},{24,28},{32,36},{36,40},{40,44}... | collective-permute-start | bytes 983048 | tf_op jit(solution)/shard_map/ppermute | solution.py:381
  95.0 10.7 %all-to-all-start = ((f32[4,32,256]{2,1,0:T(8,128)}), f32[4,32,256]{2,1,0:T(8,128)S(1)}, u32[]{:S(2)}, u32[]{:S(2)}) async-start(f32[4,32,256]{2,1,0:T(8,128)} %bitcast.18), calls=%async_computation | async-start | bytes 262144 | tf_op jit(solution)/shard_map/all_to_all | solution.py:422
  99.4 10.0 %collective-permute-start.21 = (f32[2,64,384]{2,1,0:T(8,128)S(1)}, f32[2,64,384]{2,1,0:T(8,128)S(1)}, u32[]{:S(2)}, u32[]{:S(2)}) collective-permute-start(f32[2,64,384]{2,1,0:T(8,128)S(1)} %slice.134), channel_id=1, source_target_pairs={{0,16},{1,17},{2,18},{3,19},{4,20},{5,21},{6,22},{7,23},{8,24},{9,... | collective-permute-start | bytes 589832 | tf_op jit(solution)/shard_map/ppermute | solution.py:391
  105.7 4.4 %collective-permute-start.20 = (f32[32,256]{1,0:T(8,128)S(1)}, f32[32,256]{1,0:T(8,128)S(1)}, u32[]{:S(2)}, u32[]{:S(2)}) collective-permute-start(f32[32,256]{1,0:T(8,128)S(1)} %reduce_sum.9), channel_id=1, source_target_pairs={{0,35},{1,34},{2,33},{3,32},{4,39},{5,38},{6,37},{7,36},{8,43},{9,... | collective-permute-start | bytes 98312 | tf_op jit(solution)/shard_map/ppermute | solution.py:412
  110.2 13.6 %collective-permute-start.25 = (f32[96,384]{1,0:T(8,128)S(1)}, f32[96,384]{1,0:T(8,128)S(1)}, u32[]{:S(2)}, u32[]{:S(2)}) collective-permute-start(f32[96,384]{1,0:T(8,128)S(1)} %slice_bitcast_fusion.3), channel_id=1, source_target_pairs={{0,2},{1,3},{2,0},{3,1},{4,6},{5,7},{6,4},{7,5},{8,10},{9,11},{10,... | collective-permute-start | bytes 442376 | tf_op jit(solution)/shard_map/ppermute | solution.py:396
  114.1 5.3 %collective-permute-start.24 = (f32[32,256]{1,0:T(8,128)S(1)}, f32[32,256]{1,0:T(8,128)S(1)}, u32[]{:S(2)}, u32[]{:S(2)}) collective-permute-start(f32[32,256]{1,0:T(8,128)S(1)} %add_multiply_fusion), channel_id=1, source_target_pairs={{0,3},{1,2},{2,1},{3,0},{4,7},{5,6},{6,5},{7,4},{8,11},{9,10},{10,... | collective-permute-start | bytes 98312 | tf_op jit(solution)/shard_map/ppermute | solution.py:396
  115.6 8.1 %collective-permute-start.23 = (f32[32,256]{1,0:T(8,128)S(1)}, f32[32,256]{1,0:T(8,128)S(1)}, u32[]{:S(2)}, u32[]{:S(2)}) collective-permute-start(f32[32,256]{1,0:T(8,128)S(1)} %add_multiply_fusion), channel_id=1, source_target_pairs={{0,2},{1,3},{2,0},{3,1},{4,6},{5,7},{6,4},{7,5},{8,10},{9,11},{10,... | collective-permute-start | bytes 98312 | tf_op jit(solution)/shard_map/ppermute | solution.py:396
  115.7 8.1 %collective-permute-start.22 = (f32[32,256]{1,0:T(8,128)S(1)}, f32[32,256]{1,0:T(8,128)S(1)}, u32[]{:S(2)}, u32[]{:S(2)}) collective-permute-start(f32[32,256]{1,0:T(8,128)S(1)} %add_multiply_fusion), channel_id=1, source_target_pairs={{0,1},{1,0},{2,3},{3,2},{4,5},{5,4},{6,7},{7,6},{8,9},{9,8},{10,11... | collective-permute-start | bytes 98312 | tf_op jit(solution)/shard_map/ppermute | solution.py:396
  123.8 11.1 %collective-permute-start.29 = (f32[96,384]{1,0:T(8,128)S(1)}, f32[96,384]{1,0:T(8,128)S(1)}, u32[]{:S(2)}, u32[]{:S(2)}) collective-permute-start(f32[96,384]{1,0:T(8,128)S(1)} %slice_bitcast_fusion.2), channel_id=1, source_target_pairs={{0,2},{1,3},{2,0},{3,1},{4,6},{5,7},{6,4},{7,5},{8,10},{9,11},{10,... | collective-permute-start | bytes 442376 | tf_op jit(solution)/shard_map/ppermute | solution.py:396
  125.5 5.3 %collective-permute-start.28 = (f32[128,256]{1,0:T(8,128)S(1)}, f32[128,256]{1,0:T(8,128)S(1)}, u32[]{:S(2)}, u32[]{:S(2)}) collective-permute-start(f32[128,256]{1,0:T(8,128)S(1)} %pad_maximum_fusion.3), channel_id=1, source_target_pairs={{0,192},{1,193},{2,194},{3,195},{4,28},{5,29},{6,30},{7,31},{8,200... | collective-permute-start | bytes 393224 | tf_op jit(solution)/shard_map/ppermute | solution.py:404
  125.6 7.6 %collective-permute-start.27 = (f32[128,256]{1,0:T(8,128)S(1)}, f32[128,256]{1,0:T(8,128)S(1)}, u32[]{:S(2)}, u32[]{:S(2)}) collective-permute-start(f32[128,256]{1,0:T(8,128)S(1)} %pad_maximum_fusion.3), channel_id=1, source_target_pairs={{0,128},{1,129},{2,130},{3,131},{4,20},{5,21},{6,22},{7,23},{8,136... | collective-permute-start | bytes 393224 | tf_op jit(solution)/shard_map/ppermute | solution.py:404
  130.8 4.1 %collective-permute-start.26 = (f32[128,256]{1,0:T(8,128)S(1)}, f32[128,256]{1,0:T(8,128)S(1)}, u32[]{:S(2)}, u32[]{:S(2)}) collective-permute-start(f32[128,256]{1,0:T(8,128)S(1)} %pad_maximum_fusion.3), channel_id=1, source_target_pairs={{0,64},{1,65},{2,66},{3,67},{4,12},{5,13},{6,14},{7,15},{8,72},{9,... | collective-permute-start | bytes 393224 | tf_op jit(solution)/shard_map/ppermute | solution.py:404
  135.1 20.2 %collective-permute-start.32 = (f32[2,2,96,384]{3,2,1,0:T(8,128)S(1)}, f32[2,2,96,384]{3,2,1,0:T(8,128)S(1)}, u32[]{:S(2)}, u32[]{:S(2)}) collective-permute-start(f32[2,2,96,384]{3,2,1,0:T(8,128)S(1)} %pad_maximum_fusion), channel_id=1, source_target_pairs={{0,1},{1,0},{2,3},{3,2},{4,5},{5,4},{6,7},{7,6},{8,9},{9,8},{10,11... | collective-permute-start | bytes 1769480 | tf_op jit(solution)/shard_map/ppermute | solution.py:396
  136.4 10.5 %collective-permute-start.36 = (f32[512,256]{1,0:T(8,128)S(1)}, f32[512,256]{1,0:T(8,128)S(1)}, u32[]{:S(2)}, u32[]{:S(2)}) collective-permute-start(f32[512,256]{1,0:T(8,128)S(1)} %pad_maximum_fusion.1), channel_id=1, source_target_pairs={{0,8},{1,9},{2,10},{3,11},{4,68},{5,69},{6,70},{7,71},{8,0},{9,1},... | collective-permute-start | bytes 1572872 | tf_op jit(solution)/shard_map/ppermute | solution.py:404
  140.1 13.4 %collective-permute-start.31 = (f32[512,256]{1,0:T(8,128)S(1)}, f32[512,256]{1,0:T(8,128)S(1)}, u32[]{:S(2)}, u32[]{:S(2)}) collective-permute-start(f32[512,256]{1,0:T(8,128)S(1)} %pad_maximum_fusion.1), channel_id=1, source_target_pairs={{0,24},{1,25},{2,26},{3,27},{4,196},{5,197},{6,198},{7,199},{8,16}... | collective-permute-start | bytes 1572872 | tf_op jit(solution)/shard_map/ppermute | solution.py:404
  141.7 13.6 %collective-permute-start.30 = (f32[512,256]{1,0:T(8,128)S(1)}, f32[512,256]{1,0:T(8,128)S(1)}, u32[]{:S(2)}, u32[]{:S(2)}) collective-permute-start(f32[512,256]{1,0:T(8,128)S(1)} %pad_maximum_fusion.1), channel_id=1, source_target_pairs={{0,16},{1,17},{2,18},{3,19},{4,132},{5,133},{6,134},{7,135},{8,24}... | collective-permute-start | bytes 1572872 | tf_op jit(solution)/shard_map/ppermute | solution.py:404
  142.8 18.0 %collective-permute-start.35 = (f32[512,256]{1,0:T(8,128)S(1)}, f32[512,256]{1,0:T(8,128)S(1)}, u32[]{:S(2)}, u32[]{:S(2)}) collective-permute-start(f32[512,256]{1,0:T(8,128)S(1)} %pad_maximum_fusion.1), channel_id=1, source_target_pairs={{0,4},{4,0},{1,5},{5,1},{2,6},{6,2},{3,7},{7,3},{8,12},{12,8},{9,1... | collective-permute-start | bytes 1572872 | tf_op jit(solution)/shard_map/ppermute | solution.py:396
  146.9 13.9 %collective-permute-start.37 = (f32[512,256]{1,0:T(8,128)S(1)}, f32[512,256]{1,0:T(8,128)S(1)}, u32[]{:S(2)}, u32[]{:S(2)}) collective-permute-start(f32[512,256]{1,0:T(8,128)S(1)} %collective-permute-done.36), channel_id=1, source_target_pairs={{0,4},{4,0},{1,5},{5,1},{2,6},{6,2},{3,7},{7,3},{8,12},{12,8},{9,1... | collective-permute-start | bytes 1572872 | tf_op jit(solution)/shard_map/ppermute | solution.py:396
  155.3 7.9 %collective-permute-start.33 = (f32[512,256]{1,0:T(8,128)S(1)}, f32[512,256]{1,0:T(8,128)S(1)}, u32[]{:S(2)}, u32[]{:S(2)}) collective-permute-start(f32[512,256]{1,0:T(8,128)S(1)} %collective-permute-done.30), channel_id=1, source_target_pairs={{0,4},{4,0},{1,5},{5,1},{2,6},{6,2},{3,7},{7,3},{8,12},{12,8},{9,1... | collective-permute-start | bytes 1572872 | tf_op jit(solution)/shard_map/ppermute | solution.py:396
  159.6 3.6 %collective-permute-start.34 = (f32[512,256]{1,0:T(8,128)S(1)}, f32[512,256]{1,0:T(8,128)S(1)}, u32[]{:S(2)}, u32[]{:S(2)}) collective-permute-start(f32[512,256]{1,0:T(8,128)S(1)} %collective-permute-done.31), channel_id=1, source_target_pairs={{0,4},{4,0},{1,5},{5,1},{2,6},{6,2},{3,7},{7,3},{8,12},{12,8},{9,1... | collective-permute-start | bytes 1572872 | tf_op jit(solution)/shard_map/ppermute | solution.py:396
  (9 other events, 83.8 us)

commit v4 on v3

--- a/solution.py
+++ b/solution.py
@@ -495,14 +495,11 @@
     body = body[:, :inside].at[:, :outside].add(from_above)
 
     mine, body = tied(mine, body)
-    second = among(body[0], "zl", 2)
+    second = among(body, "zl", 2)
     near = [among(mine, "zl", d) for d in (1, 2, 3)]
-    near, second, body = tied(near, second, body)
-    later = among(body[1], "zl", 2)
     mine = by_place([mine, *near], row_class)
     near = [exchange(mine, d, 1) for d in (1, 2, 3)]
-    near, later = tied(near, later)
-    second = jnp.stack([second, later])
+    near, second = tied(near, second)
     mine = by_place([mine, *near], next_turn)
     mine, pair = tied(mine, jnp.stack([body, second]))
     pair = among(pair, "zl", 1)

time: 165 us -> 163 us (0.988)
  waiting for transfers between devices: 42.3 us -> 39.4 us
    ppermute x12, starting transfers between devices: 27.4 us -> 31.7 us  [exchange(): return lax.ppermute(block, AXES, route)]
    ppermute x20 -> x19, starting transfers between devices: 36.2 us -> 32.6 us  [among(): return lax.ppermute(block, axis, [(i, i ^ distance) for i in range(n)])]
    ppermute x20 -> x19, waiting for transfers between devices: 25.8 us -> 23.9 us  [among(): return lax.ppermute(block, axis, [(i, i ^ distance) for i in range(n)])]
  transfers between devices with their start and end apart: 39 -> 38, of which waited for: 21 -> 21; matrix products, arithmetic and copies ran while one was open for 2% -> 2% of each run, Pallas kernels for 6% -> 6%
where the time goes in v4:
time: 163 us
  starting transfers between devices  90.4 us (55%)
  waiting for transfers between devices  39.4 us (24%)
  Pallas kernels  23.3 us (14%)
  other arithmetic  3.59 us (2%)
  local copies, waits for them, and re-layouts  2.77 us (2%)
  matrix products  1.74 us (1%)
    ppermute x19, starting transfers between devices, among(): return lax.ppermute(block, axis, [(i, i ^ distance) for i in range(n)])  32.6 us
    ppermute x12, starting transfers between devices, exchange(): return lax.ppermute(block, AXES, route)  31.7 us
    ppermute x19, waiting for transfers between devices, among(): return lax.ppermute(block, axis, [(i, i ^ distance) for i in range(n)])  23.9 us
    ppermute x12, waiting for transfers between devices, exchange(): return lax.ppermute(block, AXES, route)  11.9 us
    pallas_call x1, Pallas kernels, first_call(): pl.pallas_call(first_kernel, out_shape=[jax.ShapeDtypeStruct(s, F32) for...  10.8 us
    ppermute x2, starting transfers between devices, across_columns(): return lax.ppermute(block, TILE_AXES, route)  9.62 us
    ppermute x3, starting transfers between devices, across_rows(): return lax.ppermute(block, AXES, route)  8.92 us
    pallas_call x1, Pallas kernels, second_call(): pl.pallas_call(second_kernel, out_shape=[jax.ShapeDtypeStruct(s, F32) for...  5.14 us
  transfers between devices with their start and end apart: 38, of which 21 were waited for; matrix products, arithmetic and copies ran while one was open for 2% of the time, Pallas kernels for 6%

profile of v4, /device:TPU:1, one launch (start us, length us, event | category | flops | bytes accessed | tf_op | source)
XLA Modules:
  0.0 162.5 jit_solution(8707193779259765624)
XLA Ops:
  0.7 1.1 dynamic-slice_bitcast_fusion
  1.9 1.4 collective-permute-start.5
  3.3 5.1 %collective-permute-start.3 = (f32[2,96,256]{2,1,0:T(8,128)S(1)}, f32[2,96,256]{2,1,0:T(8,128)S(1)}, u32[]{:S(2)}, u32[]{:S(2)}) collective-permute-start(f32[2,96,256]{2,1,0:T(8,128)S(1)} %slice.119), channel_id=1, source_target_pairs={{4,0},{8,4},{12,8},{20,16},{24,20},{28,24},{36,32},{40,36},{44,40}... | collective-permute-start | bytes 589832 | tf_op jit(solution)/shard_map/ppermute | solution.py:381
  8.5 1.3 collective-permute-start.4
  9.8 1.3 fusion
  11.6 2.7 %collective-permute-start.2 = (s32[2]{0:T(128)S(1)}, s32[2]{0:T(128)S(1)}, u32[]{:S(2)}, u32[]{:S(2)}) collective-permute-start(s32[2]{0:T(128)S(1)} %bitcast.58), channel_id=1, source_target_pairs={{0,3},{1,2},{2,1},{3,0},{4,7},{5,6},{6,5},{7,4},{8,11},{9,10},{10,... | collective-permute-start | bytes 32 | tf_op jit(solution)/shard_map/ppermute | solution.py:396
  14.3 1.9 %collective-permute-done.2.spot3 = s32[2]{0:T(128)S(1)} collective-permute-done((s32[2]{0:T(128)S(1)}, s32[2]{0:T(128)S(1)}, u32[]{:S(2)}, u32[]{:S(2)}) %collective-permute-start.2) | collective-permute-done | bytes 40 | tf_op jit(solution)/shard_map/ppermute | solution.py:396
  16.2 1.7 %collective-permute-done.1.spot2 = s32[2]{0:T(128)S(1)} collective-permute-done((s32[2]{0:T(128)S(1)}, s32[2]{0:T(128)S(1)}, u32[]{:S(2)}, u32[]{:S(2)}) %collective-permute-start.1) | collective-permute-done | bytes 40 | tf_op jit(solution)/shard_map/ppermute | solution.py:396
  18.6 1.6 cut.1
  20.3 2.8 %collective-permute-start.7 = (f32[2,9,8,256]{3,2,1,0:T(8,128)}, f32[2,9,8,256]{3,2,1,0:T(8,128)S(1)}, u32[]{:S(2)}, u32[]{:S(2)}) collective-permute-start(f32[2,9,8,256]{3,2,1,0:T(8,128)} %get-tuple-element.72), channel_id=1, source_target_pairs={{0,2},{1,3},{2,0},{3,1},{4,6},{5,7},{6,4},{7,5},{8,10},{9,11},{10,... | collective-permute-start | bytes 442376 | tf_op jit(solution)/shard_map/ppermute | solution.py:396
  24.6 1.3 collective-permute-done.6.rows1
  26.1 5.9 %collective-permute-done.8.rows3 = f32[2,9,8,256]{3,2,1,0:T(8,128)S(1)} collective-permute-done((f32[2,9,8,256]{3,2,1,0:T(8,128)}, f32[2,9,8,256]{3,2,1,0:T(8,128)S(1)}, u32[]{:S(2)}, u32[]{:S(2)}) %collective-permute-start.8) | collective-permute-done | bytes 147488 | tf_op jit(solution)/shard_map/ppermute | solution.py:396
  32.7 10.8 %outward.1 = (f32[4,2,256,256]{3,2,1,0:T(8,128)S(1)}, f32[4,2,256,256]{3,2,1,0:T(8,128)}, f32[2,256,256]{2,1,0:T(8,128)S(1)}, f32[2,256,256]{2,1,0:T(8,128)S(1)}) custom-call(s32[5]{0:T(128)S(1)} %stack.28.where_ref, f32[2,9,8,256]{3,2,1,0:T(8,128)S(1)} %get-tuple-element.70.rows0, f32[2,9,8,256]{3,2,1,0:T(8,128)S(1)} %collective-permute-done.6.rows1, ...), custom_call_target="tpu_custom_call" | custom-call | tf_op jit(solution)/shard_map/outward/pallas_call | solution.py:208
  43.5 4.0 %collective-permute-start.9 = (f32[4,2,256,256]{3,2,1,0:T(8,128)S(1)}, f32[4,2,256,256]{3,2,1,0:T(8,128)S(1)}, u32[]{:S(2)}, u32[]{:S(2)}) collective-permute-start(f32[4,2,256,256]{3,2,1,0:T(8,128)S(1)} %get-tuple-element.79), channel_id=1, source_target_pairs={{0,4},{4,0},{1,5},{5,1},{2,6},{6,2},{3,7},{7,3},{8,12},{12,8},{9,1... | collective-permute-start | bytes 6291464 | tf_op jit(solution)/shard_map/ppermute | solution.py:396
  47.6 5.1 %homeward.1 = (f32[4,2,256,256]{3,2,1,0:T(8,128)S(1)}, f32[2,9,8,256]{3,2,1,0:T(8,128)S(1)}, f32[2,9,8,256]{3,2,1,0:T(8,128)S(1)}, f32[2,9,8,256]{3,2,1,0:T(8,128)S(1)}, f32[2,9,8,256]{3,2,1,0:T(8,128)S(1)}) custom-call(s32[5]{0:T(128)S(1)} %stack.28.where_ref, f32[4,2,256,256]{3,2,1,0:T(8,128)} %get-tuple-element.75.corrected_ref, ...), custom_call_target="tpu_custom_call" | custom-call | tf_op jit(solution)/shard_map/homeward/pallas_call | solution.py:229
  52.8 1.1 slice_add_fusion
  53.9 8.0 %collective-permute-start.10 = (f32[512,256]{1,0:T(8,128)}, f32[512,256]{1,0:T(8,128)}, u32[]{:S(2)}, u32[]{:S(2)}) collective-permute-start(f32[512,256]{1,0:T(8,128)} %bitcast.10), channel_id=1, source_target_pairs={{0,8},{1,9},{2,10},{3,11},{4,68},{5,69},{6,70},{7,71},{8,0},{9,1},... | collective-permute-start | bytes 1572872 | tf_op jit(solution)/shard_map/ppermute | solution.py:404
  61.9 2.9 %collective-permute-start.11 = (f32[512,256]{1,0:T(8,128)S(1)}, f32[512,256]{1,0:T(8,128)}, u32[]{:S(2)}, u32[]{:S(2)}) collective-permute-start(f32[512,256]{1,0:T(8,128)S(1)} %bitcast.67), channel_id=1, source_target_pairs={{0,16},{1,17},{2,18},{3,19},{4,132},{5,133},{6,134},{7,135},{8,24}... | collective-permute-start | bytes 1572872 | tf_op jit(solution)/shard_map/ppermute | solution.py:404
  64.8 1.9 %collective-permute-start.13 = (f32[2,9,8,256]{3,2,1,0:T(8,128)S(1)}, f32[2,9,8,256]{3,2,1,0:T(8,128)S(1)}, u32[]{:S(2)}, u32[]{:S(2)}) collective-permute-start(f32[2,9,8,256]{3,2,1,0:T(8,128)S(1)} %get-tuple-element.89), channel_id=1, source_target_pairs={{0,1},{1,0},{2,3},{3,2},{4,5},{5,4},{6,7},{7,6},{8,9},{9,8},{10,11... | collective-permute-start | bytes 442376 | tf_op jit(solution)/shard_map/ppermute | solution.py:396
  67.3 1.9 %collective-permute-done.13.rows1 = f32[2,9,8,256]{3,2,1,0:T(8,128)S(1)} collective-permute-done((f32[2,9,8,256]{3,2,1,0:T(8,128)S(1)}, f32[2,9,8,256]{3,2,1,0:T(8,128)S(1)}, u32[]{:S(2)}, u32[]{:S(2)}) %collective-permute-start.13) | collective-permute-done | bytes 147488 | tf_op jit(solution)/shard_map/ppermute | solution.py:396
  69.2 1.8 %collective-permute-start.15 = (f32[2,9,8,256]{3,2,1,0:T(8,128)S(1)}, f32[2,9,8,256]{3,2,1,0:T(8,128)S(1)}, u32[]{:S(2)}, u32[]{:S(2)}) collective-permute-start(f32[2,9,8,256]{3,2,1,0:T(8,128)S(1)} %get-tuple-element.91), channel_id=1, source_target_pairs={{0,3},{1,2},{2,1},{3,0},{4,7},{5,6},{6,5},{7,4},{8,11},{9,10},{10,... | collective-permute-start | bytes 442376 | tf_op jit(solution)/shard_map/ppermute | solution.py:396
  71.0 2.7 %collective-permute-done.14.rows2 = f32[2,9,8,256]{3,2,1,0:T(8,128)S(1)} collective-permute-done((f32[2,9,8,256]{3,2,1,0:T(8,128)S(1)}, f32[2,9,8,256]{3,2,1,0:T(8,128)S(1)}, u32[]{:S(2)}, u32[]{:S(2)}) %collective-permute-start.14) | collective-permute-done | bytes 147488 | tf_op jit(solution)/shard_map/ppermute | solution.py:396
  73.7 3.4 %collective-permute-done.15.rows3 = f32[2,9,8,256]{3,2,1,0:T(8,128)S(1)} collective-permute-done((f32[2,9,8,256]{3,2,1,0:T(8,128)S(1)}, f32[2,9,8,256]{3,2,1,0:T(8,128)S(1)}, u32[]{:S(2)}, u32[]{:S(2)}) %collective-permute-start.15) | collective-permute-done | bytes 147488 | tf_op jit(solution)/shard_map/ppermute | solution.py:396
  78.0 2.0 %collective-permute-done.12 = f32[512,256]{1,0:T(8,128)} collective-permute-done((f32[512,256]{1,0:T(8,128)S(1)}, f32[512,256]{1,0:T(8,128)}, u32[]{:S(2)}, u32[]{:S(2)}) %collective-permute-start.12) | collective-permute-done | bytes 524320 | tf_op jit(solution)/shard_map/ppermute | solution.py:404
  80.1 1.5 add_add_fusion
  82.6 3.8 %collective-permute-start.17 = (f32[128,256]{1,0:T(8,128)S(1)}, f32[128,256]{1,0:T(8,128)S(1)}, u32[]{:S(2)}, u32[]{:S(2)}) collective-permute-start(f32[128,256]{1,0:T(8,128)S(1)} %get-tuple-element.95), channel_id=1, source_target_pairs={{0,128},{1,129},{2,130},{3,131},{4,20},{5,21},{6,22},{7,23},{8,136... | collective-permute-start | bytes 393224 | tf_op jit(solution)/shard_map/ppermute | solution.py:404
  86.4 4.5 %collective-permute-start.19 = (f32[2,160,256]{2,1,0:T(8,128)S(1)}, f32[2,160,256]{2,1,0:T(8,128)S(1)}, u32[]{:S(2)}, u32[]{:S(2)}) collective-permute-start(f32[2,160,256]{2,1,0:T(8,128)S(1)} %get-tuple-element.98), channel_id=1, source_target_pairs={{0,4},{4,8},{8,12},{16,20},{20,24},{24,28},{32,36},{36,40},{40,44}... | collective-permute-start | bytes 983048 | tf_op jit(solution)/shard_map/ppermute | solution.py:381
  92.5 2.3 %collective-permute-done.19 = f32[2,160,256]{2,1,0:T(8,128)S(1)} collective-permute-done((f32[2,160,256]{2,1,0:T(8,128)S(1)}, f32[2,160,256]{2,1,0:T(8,128)S(1)}, u32[]{:S(2)}, u32[]{:S(2)}) %collective-permute-start.19) | collective-permute-done | bytes 327712 | tf_op jit(solution)/shard_map/ppermute | solution.py:381
  95.0 4.5 %all-to-all-start = ((f32[4,32,256]{2,1,0:T(8,128)}), f32[4,32,256]{2,1,0:T(8,128)S(1)}, u32[]{:S(2)}, u32[]{:S(2)}) async-start(f32[4,32,256]{2,1,0:T(8,128)} %bitcast.18), calls=%async_computation | async-start | bytes 262144 | tf_op jit(solution)/shard_map/all_to_all | solution.py:422
  99.4 6.2 %collective-permute-start.21 = (f32[2,64,384]{2,1,0:T(8,128)S(1)}, f32[2,64,384]{2,1,0:T(8,128)S(1)}, u32[]{:S(2)}, u32[]{:S(2)}) collective-permute-start(f32[2,64,384]{2,1,0:T(8,128)S(1)} %slice.126), channel_id=1, source_target_pairs={{0,16},{1,17},{2,18},{3,19},{4,20},{5,21},{6,22},{7,23},{8,24},{9,... | collective-permute-start | bytes 589832 | tf_op jit(solution)/shard_map/ppermute | solution.py:391
  105.7 3.1 %collective-permute-start.20 = (f32[32,256]{1,0:T(8,128)S(1)}, f32[32,256]{1,0:T(8,128)S(1)}, u32[]{:S(2)}, u32[]{:S(2)}) collective-permute-start(f32[32,256]{1,0:T(8,128)S(1)} %reduce_sum.9), channel_id=1, source_target_pairs={{0,35},{1,34},{2,33},{3,32},{4,39},{5,38},{6,37},{7,36},{8,43},{9,... | collective-permute-start | bytes 98312 | tf_op jit(solution)/shard_map/ppermute | solution.py:412
  110.2 3.3 %collective-permute-start.24 = (f32[32,256]{1,0:T(8,128)S(1)}, f32[32,256]{1,0:T(8,128)S(1)}, u32[]{:S(2)}, u32[]{:S(2)}) collective-permute-start(f32[32,256]{1,0:T(8,128)S(1)} %add_multiply_fusion), channel_id=1, source_target_pairs={{0,1},{1,0},{2,3},{3,2},{4,5},{5,4},{6,7},{7,6},{8,9},{9,8},{10,11... | collective-permute-start | bytes 98312 | tf_op jit(solution)/shard_map/ppermute | solution.py:396
  114.4 1.2 collective-permute-start.22
  117.3 1.8 %collective-permute-done.22 = f32[32,256]{1,0:T(8,128)S(1)} collective-permute-done((f32[32,256]{1,0:T(8,128)S(1)}, f32[32,256]{1,0:T(8,128)S(1)}, u32[]{:S(2)}, u32[]{:S(2)}) %collective-permute-start.22) | collective-permute-done | bytes 32800 | tf_op jit(solution)/shard_map/ppermute | solution.py:396
  119.1 1.9 %collective-permute-start.27 = (f32[128,256]{1,0:T(8,128)S(1)}, f32[128,256]{1,0:T(8,128)S(1)}, u32[]{:S(2)}, u32[]{:S(2)}) collective-permute-start(f32[128,256]{1,0:T(8,128)S(1)} %pad_maximum_fusion.2), channel_id=1, source_target_pairs={{0,192},{1,193},{2,194},{3,195},{4,28},{5,29},{6,30},{7,31},{8,200... | collective-permute-start | bytes 393224 | tf_op jit(solution)/shard_map/ppermute | solution.py:404
  121.0 5.4 %collective-permute-start.26 = (f32[128,256]{1,0:T(8,128)S(1)}, f32[128,256]{1,0:T(8,128)S(1)}, u32[]{:S(2)}, u32[]{:S(2)}) collective-permute-start(f32[128,256]{1,0:T(8,128)S(1)} %pad_maximum_fusion.2), channel_id=1, source_target_pairs={{0,128},{1,129},{2,130},{3,131},{4,20},{5,21},{6,22},{7,23},{8,136... | collective-permute-start | bytes 393224 | tf_op jit(solution)/shard_map/ppermute | solution.py:404
  126.4 2.4 %collective-permute-done.26 = f32[128,256]{1,0:T(8,128)S(1)} collective-permute-done((f32[128,256]{1,0:T(8,128)S(1)}, f32[128,256]{1,0:T(8,128)S(1)}, u32[]{:S(2)}, u32[]{:S(2)}) %collective-permute-start.26) | collective-permute-done | bytes 131104 | tf_op jit(solution)/shard_map/ppermute | solution.py:404
  128.7 1.8 %collective-permute-done.25 = f32[128,256]{1,0:T(8,128)S(1)} collective-permute-done((f32[128,256]{1,0:T(8,128)S(1)}, f32[128,256]{1,0:T(8,128)S(1)}, u32[]{:S(2)}, u32[]{:S(2)}) %collective-permute-start.25) | collective-permute-done | bytes 131104 | tf_op jit(solution)/shard_map/ppermute | solution.py:404
  130.5 1.8 %collective-permute-done.28.rows2 = f32[2,96,384]{2,1,0:T(8,128)S(1)} collective-permute-done((f32[2,96,384]{2,1,0:T(8,128)S(1)}, f32[2,96,384]{2,1,0:T(8,128)S(1)}, u32[]{:S(2)}, u32[]{:S(2)}) %collective-permute-start.28) | collective-permute-done | bytes 294944 | tf_op jit(solution)/shard_map/ppermute | solution.py:396
  132.6 6.6 %collective-permute-start.35 = (f32[512,256]{1,0:T(8,128)S(1)}, f32[512,256]{1,0:T(8,128)S(1)}, u32[]{:S(2)}, u32[]{:S(2)}) collective-permute-start(f32[512,256]{1,0:T(8,128)S(1)} %pad_maximum_fusion.1), channel_id=1, source_target_pairs={{0,8},{1,9},{2,10},{3,11},{4,68},{5,69},{6,70},{7,71},{8,0},{9,1},... | collective-permute-start | bytes 1572872 | tf_op jit(solution)/shard_map/ppermute | solution.py:404
  140.2 1.1 collective-permute-start.29
  141.3 4.0 %collective-permute-start.34 = (f32[512,256]{1,0:T(8,128)S(1)}, f32[512,256]{1,0:T(8,128)S(1)}, u32[]{:S(2)}, u32[]{:S(2)}) collective-permute-start(f32[512,256]{1,0:T(8,128)S(1)} %pad_maximum_fusion.1), channel_id=1, source_target_pairs={{0,4},{4,0},{1,5},{5,1},{2,6},{6,2},{3,7},{7,3},{8,12},{12,8},{9,1... | collective-permute-start | bytes 1572872 | tf_op jit(solution)/shard_map/ppermute | solution.py:396
  146.1 4.3 %collective-permute-start.36 = (f32[512,256]{1,0:T(8,128)S(1)}, f32[512,256]{1,0:T(8,128)S(1)}, u32[]{:S(2)}, u32[]{:S(2)}) collective-permute-start(f32[512,256]{1,0:T(8,128)S(1)} %collective-permute-done.35), channel_id=1, source_target_pairs={{0,4},{4,0},{1,5},{5,1},{2,6},{6,2},{3,7},{7,3},{8,12},{12,8},{9,1... | collective-permute-start | bytes 1572872 | tf_op jit(solution)/shard_map/ppermute | solution.py:396
  150.4 4.0 %collective-permute-done.30 = f32[512,256]{1,0:T(8,128)S(1)} collective-permute-done((f32[512,256]{1,0:T(8,128)S(1)}, f32[512,256]{1,0:T(8,128)S(1)}, u32[]{:S(2)}, u32[]{:S(2)}) %collective-permute-start.30) | collective-permute-done | bytes 524320 | tf_op jit(solution)/shard_map/ppermute | solution.py:404
  154.4 2.9 %collective-permute-start.32 = (f32[512,256]{1,0:T(8,128)S(1)}, f32[512,256]{1,0:T(8,128)S(1)}, u32[]{:S(2)}, u32[]{:S(2)}) collective-permute-start(f32[512,256]{1,0:T(8,128)S(1)} %collective-permute-done.29), channel_id=1, source_target_pairs={{0,4},{4,0},{1,5},{5,1},{2,6},{6,2},{3,7},{7,3},{8,12},{12,8},{9,1... | collective-permute-start | bytes 1572872 | tf_op jit(solution)/shard_map/ppermute | solution.py:396
  157.4 1.1 join.1
  158.5 2.3 %fill.2.refs_2_ = f32[8,2,256,256]{3,2,1,0:T(8,128)} custom-call(s32[5]{0:T(128)S(1)} %stack.28.where_ref, f32[2,256,256]{2,1,0:T(8,128)S(1)} %bitcast.46, f32[2,256,256]{2,1,0:T(8,128)S(1)} %bitcast.55, f32[2,256,256]{2,1,0:T(8,128)S(1)} %bitcast.53, f32[2,256,256]{2,1,0:T(8,128)S(1)} %bitcast.56, f32[2,256,256]{2,1,0:T(8,128)S(1)} %bitcast.54, ...), custom_call_target="tpu_custom_call" | custom-call | tf_op jit(solution)/shard_map/fill/pallas_call | solution.py:356
  160.8 1.5 fill.3
  (95 shorter events, 14.2 us)
Async XLA Ops:
  0.6 18.0 %copy-start.1 = (f32[1,2,384,384]{3,2,1,0:T(8,128)S(1)}, f32[1,2,384,384]{3,2,1,0:T(8,128)}, u32[]{:S(2)}) copy-start(f32[1,2,384,384]{3,2,1,0:T(8,128)} %param.15) | copy-start | bytes 3538948
  1.8 30.2 %copy-start.2 = (bf16[768,256]{1,0:T(8,128)(2,1)S(1)}, bf16[768,256]{1,0:T(8,128)(2,1)}, u32[]{:S(2)}) copy-start(bf16[768,256]{1,0:T(8,128)(2,1)} %constant.145.clone.down_t) | copy-start | bytes 1179652
  1.8 30.2 %copy-start.3 = (bf16[256,768]{1,0:T(8,128)(2,1)S(1)}, bf16[256,768]{1,0:T(8,128)(2,1)}, u32[]{:S(2)}) copy-start(bf16[256,768]{1,0:T(8,128)(2,1)} %constant.144.clone.across) | copy-start | bytes 1179652
  1.9 30.2 %copy-start.4 = (f32[2,128,128]{2,1,0:T(8,128)S(1)}, f32[2,128,128]{2,1,0:T(8,128)}, u32[]{:S(2)}) copy-start(f32[2,128,128]{2,1,0:T(8,128)} %constant.148.clone.rows_ref) | copy-start | bytes 393220
  1.9 30.2 %copy-start.5 = (bf16[256,768]{1,0:T(8,128)(2,1)S(1)}, bf16[256,768]{1,0:T(8,128)(2,1)}, u32[]{:S(2)}) copy-start(bf16[256,768]{1,0:T(8,128)(2,1)} %constant.146.clone.across_t) | copy-start | bytes 1179652
  1.9 30.2 %copy-start.6 = (bf16[768,256]{1,0:T(8,128)(2,1)S(1)}, bf16[768,256]{1,0:T(8,128)(2,1)}, u32[]{:S(2)}) copy-start(bf16[768,256]{1,0:T(8,128)(2,1)} %constant.143.clone.down) | copy-start | bytes 1179652
  1.9 16.7 %collective-permute-start.5 = (f32[2,64,256]{2,1,0:T(8,128)S(1)}, f32[2,64,256]{2,1,0:T(8,128)S(1)}, u32[]{:S(2)}, u32[]{:S(2)}) collective-permute-start(f32[2,64,256]{2,1,0:T(8,128)S(1)} %slice.121), channel_id=1, source_target_pairs={{20,0},{21,1},{22,2},{23,3},{24,4},{25,5},{26,6},{27,7},{28,8},{29... | collective-permute-start | bytes 393224 | tf_op jit(solution)/shard_map/ppermute | solution.py:391
  3.3 15.2 %collective-permute-start.3 = (f32[2,96,256]{2,1,0:T(8,128)S(1)}, f32[2,96,256]{2,1,0:T(8,128)S(1)}, u32[]{:S(2)}, u32[]{:S(2)}) collective-permute-start(f32[2,96,256]{2,1,0:T(8,128)S(1)} %slice.119), channel_id=1, source_target_pairs={{4,0},{8,4},{12,8},{20,16},{24,20},{28,24},{36,32},{40,36},{44,40}... | collective-permute-start | bytes 589832 | tf_op jit(solution)/shard_map/ppermute | solution.py:381
  8.5 10.1 %collective-permute-start.4 = (f32[2,64,384]{2,1,0:T(8,128)S(1)}, f32[2,64,384]{2,1,0:T(8,128)S(1)}, u32[]{:S(2)}, u32[]{:S(2)}) collective-permute-start(f32[2,64,384]{2,1,0:T(8,128)S(1)} %slice.120), channel_id=1, source_target_pairs={{16,0},{17,1},{18,2},{19,3},{20,4},{21,5},{22,6},{23,7},{24,8},{25... | collective-permute-start | bytes 589832 | tf_op jit(solution)/shard_map/ppermute | solution.py:391
  11.6 4.6 %collective-permute-start.2 = (s32[2]{0:T(128)S(1)}, s32[2]{0:T(128)S(1)}, u32[]{:S(2)}, u32[]{:S(2)}) collective-permute-start(s32[2]{0:T(128)S(1)} %bitcast.58), channel_id=1, source_target_pairs={{0,3},{1,2},{2,1},{3,0},{4,7},{5,6},{6,5},{7,4},{8,11},{9,10},{10,... | collective-permute-start | bytes 32 | tf_op jit(solution)/shard_map/ppermute | solution.py:396
  14.3 3.6 %collective-permute-start.1 = (s32[2]{0:T(128)S(1)}, s32[2]{0:T(128)S(1)}, u32[]{:S(2)}, u32[]{:S(2)}) collective-permute-start(s32[2]{0:T(128)S(1)} %bitcast.59), channel_id=1, source_target_pairs={{0,2},{1,3},{2,0},{3,1},{4,6},{5,7},{6,4},{7,5},{8,10},{9,11},{10,... | collective-permute-start | bytes 32 | tf_op jit(solution)/shard_map/ppermute | solution.py:396
  16.2 2.4 %collective-permute-start = (s32[2]{0:T(128)S(1)}, s32[2]{0:T(128)S(1)}, u32[]{:S(2)}, u32[]{:S(2)}) collective-permute-start(s32[2]{0:T(128)S(1)} %bitcast.60), channel_id=1, source_target_pairs={{0,1},{1,0},{2,3},{3,2},{4,5},{5,4},{6,7},{7,6},{8,9},{9,8},{10,11... | collective-permute-start | bytes 32 | tf_op jit(solution)/shard_map/ppermute | solution.py:396
  20.2 5.6 %collective-permute-start.6 = (f32[2,9,8,256]{3,2,1,0:T(8,128)}, f32[2,9,8,256]{3,2,1,0:T(8,128)S(1)}, u32[]{:S(2)}, u32[]{:S(2)}) collective-permute-start(f32[2,9,8,256]{3,2,1,0:T(8,128)} %get-tuple-element.71), channel_id=1, source_target_pairs={{0,1},{1,0},{2,3},{3,2},{4,5},{5,4},{6,7},{7,6},{8,9},{9,8},{10,11... | collective-permute-start | bytes 442376 | tf_op jit(solution)/shard_map/ppermute | solution.py:396
  20.3 5.9 %collective-permute-start.7 = (f32[2,9,8,256]{3,2,1,0:T(8,128)}, f32[2,9,8,256]{3,2,1,0:T(8,128)S(1)}, u32[]{:S(2)}, u32[]{:S(2)}) collective-permute-start(f32[2,9,8,256]{3,2,1,0:T(8,128)} %get-tuple-element.72), channel_id=1, source_target_pairs={{0,2},{1,3},{2,0},{3,1},{4,6},{5,7},{6,4},{7,5},{8,10},{9,11},{10,... | collective-permute-start | bytes 442376 | tf_op jit(solution)/shard_map/ppermute | solution.py:396
  23.1 8.9 %collective-permute-start.8 = (f32[2,9,8,256]{3,2,1,0:T(8,128)}, f32[2,9,8,256]{3,2,1,0:T(8,128)S(1)}, u32[]{:S(2)}, u32[]{:S(2)}) collective-permute-start(f32[2,9,8,256]{3,2,1,0:T(8,128)} %get-tuple-element.73), channel_id=1, source_target_pairs={{0,3},{1,2},{2,1},{3,0},{4,7},{5,6},{6,5},{7,4},{8,11},{9,10},{10,... | collective-permute-start | bytes 442376 | tf_op jit(solution)/shard_map/ppermute | solution.py:396
  43.5 9.2 %collective-permute-start.9 = (f32[4,2,256,256]{3,2,1,0:T(8,128)S(1)}, f32[4,2,256,256]{3,2,1,0:T(8,128)S(1)}, u32[]{:S(2)}, u32[]{:S(2)}) collective-permute-start(f32[4,2,256,256]{3,2,1,0:T(8,128)S(1)} %get-tuple-element.79), channel_id=1, source_target_pairs={{0,4},{4,0},{1,5},{5,1},{2,6},{6,2},{3,7},{7,3},{8,12},{12,8},{9,1... | collective-permute-start | bytes 6291464 | tf_op jit(solution)/shard_map/ppermute | solution.py:396
  52.7 24.4 %copy-start.9 = (s32[1,1,2]{2,1,0:T(1,128)S(1)}, s32[1,1,2]{2,1,0:T(1,128)}, u32[]{:S(2)}) copy-start(s32[1,1,2]{2,1,0:T(1,128)} %param.17) | copy-start | bytes 28
  52.7 24.4 %copy-start.12 = (s32[2]{0:T(128)S(1)}, s32[2]{0:T(128)}, u32[]{:S(2)}) copy-start(s32[2]{0:T(128)} %copy-done.11) | copy-start | bytes 28
  52.8 24.4 %copy-start.14 = (s32[2]{0:T(128)S(1)}, s32[2]{0:T(128)}, u32[]{:S(2)}) copy-start(s32[2]{0:T(128)} %copy-done.13) | copy-start | bytes 28
  52.8 24.4 %copy-start.16 = (s32[2]{0:T(128)S(1)}, s32[2]{0:T(128)}, u32[]{:S(2)}) copy-start(s32[2]{0:T(128)} %copy-done.15) | copy-start | bytes 28
  53.9 24.1 %collective-permute-start.10 = (f32[512,256]{1,0:T(8,128)}, f32[512,256]{1,0:T(8,128)}, u32[]{:S(2)}, u32[]{:S(2)}) collective-permute-start(f32[512,256]{1,0:T(8,128)} %bitcast.10), channel_id=1, source_target_pairs={{0,8},{1,9},{2,10},{3,11},{4,68},{5,69},{6,70},{7,71},{8,0},{9,1},... | collective-permute-start | bytes 1572872 | tf_op jit(solution)/shard_map/ppermute | solution.py:404
  61.9 16.1 %collective-permute-start.11 = (f32[512,256]{1,0:T(8,128)S(1)}, f32[512,256]{1,0:T(8,128)}, u32[]{:S(2)}, u32[]{:S(2)}) collective-permute-start(f32[512,256]{1,0:T(8,128)S(1)} %bitcast.67), channel_id=1, source_target_pairs={{0,16},{1,17},{2,18},{3,19},{4,132},{5,133},{6,134},{7,135},{8,24}... | collective-permute-start | bytes 1572872 | tf_op jit(solution)/shard_map/ppermute | solution.py:404
  64.8 15.3 %collective-permute-start.12 = (f32[512,256]{1,0:T(8,128)S(1)}, f32[512,256]{1,0:T(8,128)}, u32[]{:S(2)}, u32[]{:S(2)}) collective-permute-start(f32[512,256]{1,0:T(8,128)S(1)} %bitcast.66), channel_id=1, source_target_pairs={{0,24},{1,25},{2,26},{3,27},{4,196},{5,197},{6,198},{7,199},{8,16}... | collective-permute-start | bytes 1572872 | tf_op jit(solution)/shard_map/ppermute | solution.py:404
  64.8 4.4 %collective-permute-start.13 = (f32[2,9,8,256]{3,2,1,0:T(8,128)S(1)}, f32[2,9,8,256]{3,2,1,0:T(8,128)S(1)}, u32[]{:S(2)}, u32[]{:S(2)}) collective-permute-start(f32[2,9,8,256]{3,2,1,0:T(8,128)S(1)} %get-tuple-element.89), channel_id=1, source_target_pairs={{0,1},{1,0},{2,3},{3,2},{4,5},{5,4},{6,7},{7,6},{8,9},{9,8},{10,11... | collective-permute-start | bytes 442376 | tf_op jit(solution)/shard_map/ppermute | solution.py:396
  66.7 7.1 %collective-permute-start.14 = (f32[2,9,8,256]{3,2,1,0:T(8,128)S(1)}, f32[2,9,8,256]{3,2,1,0:T(8,128)S(1)}, u32[]{:S(2)}, u32[]{:S(2)}) collective-permute-start(f32[2,9,8,256]{3,2,1,0:T(8,128)S(1)} %get-tuple-element.90), channel_id=1, source_target_pairs={{0,2},{1,3},{2,0},{3,1},{4,6},{5,7},{6,4},{7,5},{8,10},{9,11},{10,... | collective-permute-start | bytes 442376 | tf_op jit(solution)/shard_map/ppermute | solution.py:396
  69.2 7.9 %collective-permute-start.15 = (f32[2,9,8,256]{3,2,1,0:T(8,128)S(1)}, f32[2,9,8,256]{3,2,1,0:T(8,128)S(1)}, u32[]{:S(2)}, u32[]{:S(2)}) collective-permute-start(f32[2,9,8,256]{3,2,1,0:T(8,128)S(1)} %get-tuple-element.91), channel_id=1, source_target_pairs={{0,3},{1,2},{2,1},{3,0},{4,7},{5,6},{6,5},{7,4},{8,11},{9,10},{10,... | collective-permute-start | bytes 442376 | tf_op jit(solution)/shard_map/ppermute | solution.py:396
  81.6 9.2 %collective-permute-start.16 = (f32[128,256]{1,0:T(8,128)S(1)}, f32[128,256]{1,0:T(8,128)S(1)}, u32[]{:S(2)}, u32[]{:S(2)}) collective-permute-start(f32[128,256]{1,0:T(8,128)S(1)} %get-tuple-element.94), channel_id=1, source_target_pairs={{0,64},{1,65},{2,66},{3,67},{4,12},{5,13},{6,14},{7,15},{8,72},{9,... | collective-permute-start | bytes 393224 | tf_op jit(solution)/shard_map/ppermute | solution.py:404
  82.6 8.3 %collective-permute-start.17 = (f32[128,256]{1,0:T(8,128)S(1)}, f32[128,256]{1,0:T(8,128)S(1)}, u32[]{:S(2)}, u32[]{:S(2)}) collective-permute-start(f32[128,256]{1,0:T(8,128)S(1)} %get-tuple-element.95), channel_id=1, source_target_pairs={{0,128},{1,129},{2,130},{3,131},{4,20},{5,21},{6,22},{7,23},{8,136... | collective-permute-start | bytes 393224 | tf_op jit(solution)/shard_map/ppermute | solution.py:404
  86.4 5.5 %collective-permute-start.18 = (f32[128,256]{1,0:T(8,128)S(1)}, f32[128,256]{1,0:T(8,128)S(1)}, u32[]{:S(2)}, u32[]{:S(2)}) collective-permute-start(f32[128,256]{1,0:T(8,128)S(1)} %get-tuple-element.96), channel_id=1, source_target_pairs={{0,192},{1,193},{2,194},{3,195},{4,28},{5,29},{6,30},{7,31},{8,200... | collective-permute-start | bytes 393224 | tf_op jit(solution)/shard_map/ppermute | solution.py:404
  86.4 8.5 %collective-permute-start.19 = (f32[2,160,256]{2,1,0:T(8,128)S(1)}, f32[2,160,256]{2,1,0:T(8,128)S(1)}, u32[]{:S(2)}, u32[]{:S(2)}) collective-permute-start(f32[2,160,256]{2,1,0:T(8,128)S(1)} %get-tuple-element.98), channel_id=1, source_target_pairs={{0,4},{4,8},{8,12},{16,20},{20,24},{24,28},{32,36},{36,40},{40,44}... | collective-permute-start | bytes 983048 | tf_op jit(solution)/shard_map/ppermute | solution.py:381
  95.0 10.7 %all-to-all-start = ((f32[4,32,256]{2,1,0:T(8,128)}), f32[4,32,256]{2,1,0:T(8,128)S(1)}, u32[]{:S(2)}, u32[]{:S(2)}) async-start(f32[4,32,256]{2,1,0:T(8,128)} %bitcast.18), calls=%async_computation | async-start | bytes 262144 | tf_op jit(solution)/shard_map/all_to_all | solution.py:422
  99.4 10.0 %collective-permute-start.21 = (f32[2,64,384]{2,1,0:T(8,128)S(1)}, f32[2,64,384]{2,1,0:T(8,128)S(1)}, u32[]{:S(2)}, u32[]{:S(2)}) collective-permute-start(f32[2,64,384]{2,1,0:T(8,128)S(1)} %slice.126), channel_id=1, source_target_pairs={{0,16},{1,17},{2,18},{3,19},{4,20},{5,21},{6,22},{7,23},{8,24},{9,... | collective-permute-start | bytes 589832 | tf_op jit(solution)/shard_map/ppermute | solution.py:391
  105.7 4.4 %collective-permute-start.20 = (f32[32,256]{1,0:T(8,128)S(1)}, f32[32,256]{1,0:T(8,128)S(1)}, u32[]{:S(2)}, u32[]{:S(2)}) collective-permute-start(f32[32,256]{1,0:T(8,128)S(1)} %reduce_sum.9), channel_id=1, source_target_pairs={{0,35},{1,34},{2,33},{3,32},{4,39},{5,38},{6,37},{7,36},{8,43},{9,... | collective-permute-start | bytes 98312 | tf_op jit(solution)/shard_map/ppermute | solution.py:412
  110.2 6.5 %collective-permute-start.24 = (f32[32,256]{1,0:T(8,128)S(1)}, f32[32,256]{1,0:T(8,128)S(1)}, u32[]{:S(2)}, u32[]{:S(2)}) collective-permute-start(f32[32,256]{1,0:T(8,128)S(1)} %add_multiply_fusion), channel_id=1, source_target_pairs={{0,1},{1,0},{2,3},{3,2},{4,5},{5,4},{6,7},{7,6},{8,9},{9,8},{10,11... | collective-permute-start | bytes 98312 | tf_op jit(solution)/shard_map/ppermute | solution.py:396
  113.5 3.8 %collective-permute-start.23 = (f32[32,256]{1,0:T(8,128)S(1)}, f32[32,256]{1,0:T(8,128)S(1)}, u32[]{:S(2)}, u32[]{:S(2)}) collective-permute-start(f32[32,256]{1,0:T(8,128)S(1)} %add_multiply_fusion), channel_id=1, source_target_pairs={{0,2},{1,3},{2,0},{3,1},{4,6},{5,7},{6,4},{7,5},{8,10},{9,11},{10,... | collective-permute-start | bytes 98312 | tf_op jit(solution)/shard_map/ppermute | solution.py:396
  114.4 4.6 %collective-permute-start.22 = (f32[32,256]{1,0:T(8,128)S(1)}, f32[32,256]{1,0:T(8,128)S(1)}, u32[]{:S(2)}, u32[]{:S(2)}) collective-permute-start(f32[32,256]{1,0:T(8,128)S(1)} %add_multiply_fusion), channel_id=1, source_target_pairs={{0,3},{1,2},{2,1},{3,0},{4,7},{5,6},{6,5},{7,4},{8,11},{9,10},{10,... | collective-permute-start | bytes 98312 | tf_op jit(solution)/shard_map/ppermute | solution.py:396
  115.6 16.7 %collective-permute-start.28 = (f32[2,96,384]{2,1,0:T(8,128)S(1)}, f32[2,96,384]{2,1,0:T(8,128)S(1)}, u32[]{:S(2)}, u32[]{:S(2)}) collective-permute-start(f32[2,96,384]{2,1,0:T(8,128)S(1)} %fusion.2.rows0), channel_id=1, source_target_pairs={{0,2},{1,3},{2,0},{3,1},{4,6},{5,7},{6,4},{7,5},{8,10},{9,11},{10,... | collective-permute-start | bytes 884744 | tf_op jit(solution)/shard_map/ppermute | solution.py:396
  119.1 7.3 %collective-permute-start.27 = (f32[128,256]{1,0:T(8,128)S(1)}, f32[128,256]{1,0:T(8,128)S(1)}, u32[]{:S(2)}, u32[]{:S(2)}) collective-permute-start(f32[128,256]{1,0:T(8,128)S(1)} %pad_maximum_fusion.2), channel_id=1, source_target_pairs={{0,192},{1,193},{2,194},{3,195},{4,28},{5,29},{6,30},{7,31},{8,200... | collective-permute-start | bytes 393224 | tf_op jit(solution)/shard_map/ppermute | solution.py:404
  121.0 7.7 %collective-permute-start.26 = (f32[128,256]{1,0:T(8,128)S(1)}, f32[128,256]{1,0:T(8,128)S(1)}, u32[]{:S(2)}, u32[]{:S(2)}) collective-permute-start(f32[128,256]{1,0:T(8,128)S(1)} %pad_maximum_fusion.2), channel_id=1, source_target_pairs={{0,128},{1,129},{2,130},{3,131},{4,20},{5,21},{6,22},{7,23},{8,136... | collective-permute-start | bytes 393224 | tf_op jit(solution)/shard_map/ppermute | solution.py:404
  126.4 4.1 %collective-permute-start.25 = (f32[128,256]{1,0:T(8,128)S(1)}, f32[128,256]{1,0:T(8,128)S(1)}, u32[]{:S(2)}, u32[]{:S(2)}) collective-permute-start(f32[128,256]{1,0:T(8,128)S(1)} %pad_maximum_fusion.2), channel_id=1, source_target_pairs={{0,64},{1,65},{2,66},{3,67},{4,12},{5,13},{6,14},{7,15},{8,72},{9,... | collective-permute-start | bytes 393224 | tf_op jit(solution)/shard_map/ppermute | solution.py:404
  132.5 21.9 %collective-permute-start.31 = (f32[2,2,96,384]{3,2,1,0:T(8,128)S(1)}, f32[2,2,96,384]{3,2,1,0:T(8,128)S(1)}, u32[]{:S(2)}, u32[]{:S(2)}) collective-permute-start(f32[2,2,96,384]{3,2,1,0:T(8,128)S(1)} %pad_maximum_fusion), channel_id=1, source_target_pairs={{0,1},{1,0},{2,3},{3,2},{4,5},{5,4},{6,7},{7,6},{8,9},{9,8},{10,11... | collective-permute-start | bytes 1769480 | tf_op jit(solution)/shard_map/ppermute | solution.py:396
  132.6 13.5 %collective-permute-start.35 = (f32[512,256]{1,0:T(8,128)S(1)}, f32[512,256]{1,0:T(8,128)S(1)}, u32[]{:S(2)}, u32[]{:S(2)}) collective-permute-start(f32[512,256]{1,0:T(8,128)S(1)} %pad_maximum_fusion.1), channel_id=1, source_target_pairs={{0,8},{1,9},{2,10},{3,11},{4,68},{5,69},{6,70},{7,71},{8,0},{9,1},... | collective-permute-start | bytes 1572872 | tf_op jit(solution)/shard_map/ppermute | solution.py:404
  139.2 15.2 %collective-permute-start.30 = (f32[512,256]{1,0:T(8,128)S(1)}, f32[512,256]{1,0:T(8,128)S(1)}, u32[]{:S(2)}, u32[]{:S(2)}) collective-permute-start(f32[512,256]{1,0:T(8,128)S(1)} %pad_maximum_fusion.1), channel_id=1, source_target_pairs={{0,24},{1,25},{2,26},{3,27},{4,196},{5,197},{6,198},{7,199},{8,16}... | collective-permute-start | bytes 1572872 | tf_op jit(solution)/shard_map/ppermute | solution.py:404
  140.2 14.2 %collective-permute-start.29 = (f32[512,256]{1,0:T(8,128)S(1)}, f32[512,256]{1,0:T(8,128)S(1)}, u32[]{:S(2)}, u32[]{:S(2)}) collective-permute-start(f32[512,256]{1,0:T(8,128)S(1)} %pad_maximum_fusion.1), channel_id=1, source_target_pairs={{0,16},{1,17},{2,18},{3,19},{4,132},{5,133},{6,134},{7,135},{8,24}... | collective-permute-start | bytes 1572872 | tf_op jit(solution)/shard_map/ppermute | solution.py:404
  141.3 17.2 %collective-permute-start.34 = (f32[512,256]{1,0:T(8,128)S(1)}, f32[512,256]{1,0:T(8,128)S(1)}, u32[]{:S(2)}, u32[]{:S(2)}) collective-permute-start(f32[512,256]{1,0:T(8,128)S(1)} %pad_maximum_fusion.1), channel_id=1, source_target_pairs={{0,4},{4,0},{1,5},{5,1},{2,6},{6,2},{3,7},{7,3},{8,12},{12,8},{9,1... | collective-permute-start | bytes 1572872 | tf_op jit(solution)/shard_map/ppermute | solution.py:396
  146.1 12.4 %collective-permute-start.36 = (f32[512,256]{1,0:T(8,128)S(1)}, f32[512,256]{1,0:T(8,128)S(1)}, u32[]{:S(2)}, u32[]{:S(2)}) collective-permute-start(f32[512,256]{1,0:T(8,128)S(1)} %collective-permute-done.35), channel_id=1, source_target_pairs={{0,4},{4,0},{1,5},{5,1},{2,6},{6,2},{3,7},{7,3},{8,12},{12,8},{9,1... | collective-permute-start | bytes 1572872 | tf_op jit(solution)/shard_map/ppermute | solution.py:396
  154.4 6.4 %collective-permute-start.32 = (f32[512,256]{1,0:T(8,128)S(1)}, f32[512,256]{1,0:T(8,128)S(1)}, u32[]{:S(2)}, u32[]{:S(2)}) collective-permute-start(f32[512,256]{1,0:T(8,128)S(1)} %collective-permute-done.29), channel_id=1, source_target_pairs={{0,4},{4,0},{1,5},{5,1},{2,6},{6,2},{3,7},{7,3},{8,12},{12,8},{9,1... | collective-permute-start | bytes 1572872 | tf_op jit(solution)/shard_map/ppermute | solution.py:396
  157.2 3.6 %collective-permute-start.33 = (f32[512,256]{1,0:T(8,128)S(1)}, f32[512,256]{1,0:T(8,128)S(1)}, u32[]{:S(2)}, u32[]{:S(2)}) collective-permute-start(f32[512,256]{1,0:T(8,128)S(1)} %collective-permute-done.30), channel_id=1, source_target_pairs={{0,4},{4,0},{1,5},{5,1},{2,6},{6,2},{3,7},{7,3},{8,12},{12,8},{9,1... | collective-permute-start | bytes 1572872 | tf_op jit(solution)/shard_map/ppermute | solution.py:396
  (8 other events, 65.9 us)
